TPU v7x, 32 devices: a whole 2x2x4 slice. The times are simulated.
32 devices in a mesh: section: 2 (over core), dp: 16 (over z, y, x).
Axes of the slice: x: 2, y: 2, z: 4, core: 2. Of those that a mesh axis runs over, the one named last changes fastest.
Arguments:
- inputs_down: bfloat16 [2, 512, 4096], P(None, 'dp', 'section'), may hold values from -6 to 6
- inputs_up: bfloat16 [2, 512, 4096], P(None, 'dp', 'section'), may hold values from -6 to 6
- cotan_down: bfloat16 [2, 512, 4096], P(None, 'dp', 'section'), may hold values from -0.119628906 to 0.119628906
- cotan_up: bfloat16 [2, 512, 4096], P(None, 'dp', 'section'), may hold values from -0.119628906 to 0.119628906
- norm_gains: bfloat16 [2, 4096], P('section'), may hold values from 0.099609375 to 1.8984375
- adapt_down: bfloat16 [2, 64, 4096], P('section'), may hold values from -0.09375 to 0.09375
- adapt_up: bfloat16 [2, 64, 4096], P('section'), may hold values from -0.75 to 0.75
Outputs:
- grad_adapt_down: float32 [2, 64, 4096], P('section', None, 'dp')
- grad_adapt_up: float32 [2, 64, 4096], P('section', None, 'dp')
All inputs are finite; a program needn't handle non-finite values.
Results may differ from a plain program's by a relative error of at most 0.006.
Values may be sent and summed in bfloat16 or wider, within the bound.
No kernel may reach another device: no remote copies, remote signals or barrier semaphores. Data moves between devices by JAX's collectives and lax.ppermute only.
A program may use at most 64 MiB of HBM per device.

v0:
```python
import jax
import jax.numpy as jnp
from jax import lax
from jax.sharding import PartitionSpec as P

epsilon = 1e-05


def from_partner(value, axis, stride):
    return lax.ppermute(value, axis, [(i, i ^ 1 << stride) for i in range(lax.axis_size(axis))])


def shifted(block, axis, distance):
    devices = range(lax.axis_size(axis))
    route = [(i - distance, i) for i in devices if i - distance in devices]
    return lax.ppermute(block, axis, route)


def norm_branch(hidden, norm_gain, down_proj):
    hidden_f = hidden.astype(jnp.float32)
    inverse = lax.rsqrt(jnp.mean(hidden_f * hidden_f, axis=-1, keepdims=True) + epsilon)
    normed = (hidden_f * inverse * norm_gain.astype(jnp.float32)).astype(jnp.bfloat16)
    bottle = lax.dot_general(
        normed, down_proj, (((1,), (1,)), ((), ())), preferred_element_type=jnp.float32
    )
    active = jax.nn.silu(bottle).astype(jnp.bfloat16)
    return (hidden_f, inverse, normed, bottle, active)


def block_forward(hidden, norm_gain, down_proj, up_proj):
    hidden_f, inverse, normed, bottle, active = norm_branch(hidden, norm_gain, down_proj)
    return (hidden_f + jnp.dot(active, up_proj, preferred_element_type=jnp.float32)).astype(
        jnp.bfloat16
    )


def block_backward(hidden, upstream, norm_gain, down_proj, up_proj):
    hidden_f, inverse, normed, bottle, active = norm_branch(hidden, norm_gain, down_proj)
    upstream_f = upstream.astype(jnp.float32)
    grad_up = lax.dot_general(
        active, upstream, (((0,), (0,)), ((), ())), preferred_element_type=jnp.float32
    )
    grad_active = lax.dot_general(
        upstream, up_proj, (((1,), (1,)), ((), ())), preferred_element_type=jnp.float32
    )
    sigma = jax.nn.sigmoid(bottle)
    grad_bottle = (grad_active * sigma * (1.0 + bottle * (1.0 - sigma))).astype(jnp.bfloat16)
    grad_down = lax.dot_general(
        grad_bottle, normed, (((0,), (0,)), ((), ())), preferred_element_type=jnp.float32
    )
    grad_normed = jnp.dot(grad_bottle, down_proj, preferred_element_type=jnp.float32)
    scaled = norm_gain.astype(jnp.float32) * grad_normed
    project = jnp.mean(scaled * hidden_f, axis=-1, keepdims=True)
    downstream = (upstream_f + inverse * scaled - hidden_f * inverse**3 * project).astype(
        jnp.bfloat16
    )
    return (downstream, grad_down, grad_up)


def pick_slot(stacked, offset, count):
    slot_idx = jnp.clip(offset, 0, count - 1)
    is_live = (offset >= 0) & (offset < count)
    return (slot_idx, is_live, lax.dynamic_index_in_dim(stacked, slot_idx, 0, keepdims=False))


def per_device(inputs_down, inputs_up, cotan_down, cotan_up, norm_gains, adapt_down, adapt_up):
    sections = lax.axis_size("section")
    section_idx = lax.axis_index("section")
    enter_down, enter_up, final_down, final_up = (
        lax.all_gather(inputs_down, "section", axis=2, tiled=True),
        lax.all_gather(inputs_up, "section", axis=2, tiled=True),
        lax.all_gather(cotan_down, "section", axis=2, tiled=True),
        lax.all_gather(cotan_up, "section", axis=2, tiled=True),
    )
    micro_count = inputs_down.shape[0]
    own_gain, own_down, own_up = (norm_gains[0], adapt_down[0], adapt_up[0])
    mirrored = (norm_gains, adapt_down, adapt_up)
    bit_count = sections.bit_length() - 1
    for bit_idx in range(bit_count):
        mirrored = from_partner((mirrored[0], mirrored[1], mirrored[2]), "section", bit_idx)
    mirror_gain, mirror_down, mirror_up = (mirrored[0][0], mirrored[1][0], mirrored[2][0])
    is_first = section_idx == 0
    is_last = section_idx == sections - 1
    zero_rows = jnp.zeros_like(enter_down[0])
    stash_empty = jnp.zeros_like(enter_down)
    ticks = sections + micro_count - 1

    def forward_step(step_idx, carry):
        recv_down, recv_up, stash_down, stash_up = carry
        slot_down, live_down, fresh_down = pick_slot(
            enter_down, step_idx - section_idx, micro_count
        )
        slot_up, live_up, fresh_up = pick_slot(
            enter_up, step_idx - (sections - 1 - section_idx), micro_count
        )
        hidden_down = jnp.where(is_first, fresh_down, recv_down)
        hidden_up = jnp.where(is_last, fresh_up, recv_up)
        kept_down = lax.dynamic_index_in_dim(stash_down, slot_down, 0, keepdims=False)
        kept_up = lax.dynamic_index_in_dim(stash_up, slot_up, 0, keepdims=False)
        stash_down = lax.dynamic_update_index_in_dim(
            stash_down, jnp.where(live_down, hidden_down, kept_down), slot_down, 0
        )
        stash_up = lax.dynamic_update_index_in_dim(
            stash_up, jnp.where(live_up, hidden_up, kept_up), slot_up, 0
        )
        out_down = block_forward(hidden_down, own_gain, own_down, own_up)
        out_up = block_forward(hidden_up, mirror_gain, mirror_down, mirror_up)
        recv_down = shifted(out_down, "section", 1)
        recv_up = shifted(out_up, "section", -1)
        return (recv_down, recv_up, stash_down, stash_up)

    forward_state = lax.fori_loop(
        0, ticks, forward_step, (zero_rows, zero_rows, stash_empty, stash_empty)
    )
    stash_down, stash_up = (forward_state[2], forward_state[3])
    zero_grad = jnp.zeros(own_down.shape, jnp.float32)

    def backward_step(step_idx, carry):
        recv_down, recv_up, own_gd, own_gu, mirror_gd, mirror_gu = carry
        slot_down, live_down, closing_down = pick_slot(
            final_down, step_idx - (sections - 1 - section_idx), micro_count
        )
        slot_up, live_up, closing_up = pick_slot(final_up, step_idx - section_idx, micro_count)
        upstream_down = jnp.where(live_down, jnp.where(is_last, closing_down, recv_down), zero_rows)
        upstream_up = jnp.where(live_up, jnp.where(is_first, closing_up, recv_up), zero_rows)
        hidden_down = lax.dynamic_index_in_dim(stash_down, slot_down, 0, keepdims=False)
        hidden_up = lax.dynamic_index_in_dim(stash_up, slot_up, 0, keepdims=False)
        back_down, grad_down, grad_up = block_backward(
            hidden_down, upstream_down, own_gain, own_down, own_up
        )
        back_up, mgrad_down, mgrad_up = block_backward(
            hidden_up, upstream_up, mirror_gain, mirror_down, mirror_up
        )
        recv_down = shifted(back_down, "section", -1)
        recv_up = shifted(back_up, "section", 1)
        return (
            recv_down,
            recv_up,
            own_gd + grad_down,
            own_gu + grad_up,
            mirror_gd + mgrad_down,
            mirror_gu + mgrad_up,
        )

    backward_state = lax.fori_loop(
        0, ticks, backward_step, (zero_rows, zero_rows, zero_grad, zero_grad, zero_grad, zero_grad)
    )
    own_gd, own_gu, mirror_gd, mirror_gu = (
        backward_state[2],
        backward_state[3],
        backward_state[4],
        backward_state[5],
    )
    share_gd, share_gu, share_mgd, share_mgu = (
        lax.psum_scatter(own_gd, "dp", scatter_dimension=1, tiled=True),
        lax.psum_scatter(own_gu, "dp", scatter_dimension=1, tiled=True),
        lax.psum_scatter(mirror_gd, "dp", scatter_dimension=1, tiled=True),
        lax.psum_scatter(mirror_gu, "dp", scatter_dimension=1, tiled=True),
    )
    homeward = (share_mgd, share_mgu)
    for bit_idx in range(bit_count):
        homeward = from_partner((homeward[0], homeward[1]), "section", bit_idx)
    total_down = share_gd + homeward[0]
    total_up = share_gu + homeward[1]
    return (total_down[None], total_up[None])


def solution(mesh):
    placed = (
        P(None, "dp", "section"),
        P(None, "dp", "section"),
        P(None, "dp", "section"),
        P(None, "dp", "section"),
        P("section", None),
        P("section", None, None),
        P("section", None, None),
    )
    return jax.shard_map(
        per_device,
        mesh=mesh,
        in_specs=placed,
        out_specs=(P("section", None, "dp"), P("section", None, "dp")),
        check_vma=False,
    )
```

profile of v0, /device:TPU:0, one launch (start us, length us, event | category | flops | bytes accessed | tf_op | source)
XLA Modules:
  0.0 444.2 jit_solution(18768587379941596)
XLA Ops:
  8.2 3.8 all_gather.13
  12.1 2.4 all_gather.14
  14.5 2.4 all_gather.12
  16.9 2.3 all_gather.15
  22.7 43.2 %while.45 = (s32[]{:T(128)}, bf16[32,4096]{1,0:T(8,128)(2,1)}, bf16[32,4096]{1,0:T(8,128)(2,1)}, bf16[2,32,4096]{2,1,0:T(8,128)(2,1)S(1)}, bf16[2,32,4096]{2,1,0...) while((s32[]{:T(128)}, bf16[32,4096]{1,0:T(8,128)(2,1)}, ...), condition=%wide.region_3.4_spmd, body=%wide.region_0.3_spmd.sunk | while | flops 70283336 | bytes 13714911 | solution.py:112
  25.4 3.9 collective-permute-start
  34.2 2.3 collective-permute-done.1
  40.0 3.7 collective-permute-start
  45.9 1.4 fusion.129
  48.6 2.3 collective-permute-done.1
  54.3 3.7 collective-permute-start
  62.9 2.3 collective-permute-done.1
  67.3 59.2 %while.46 = (s32[]{:T(128)}, bf16[32,4096]{1,0:T(8,128)(2,1)}, bf16[32,4096]{1,0:T(8,128)(2,1)}, f32[64,4096]{1,0:T(8,128)}, f32[64,4096]{1,0:T(8,128)}, /*index...) while((s32[]{:T(128)}, bf16[32,4096]{1,0:T(8,128)(2,1)}, ...), condition=%wide.region_9.10_spmd.clone, body=%wide.region_4.9_spmd.clone.sunk | while | flops 176488640 | bytes 53712088 | solution.py:145
  76.5 4.5 %collective-permute-start.3 = (bf16[32,4096]{1,0:T(8,128)(2,1)}, bf16[32,4096]{1,0:T(8,128)(2,1)}, u32[]{:S(2)}, u32[]{:S(2)}) collective-permute-start(bf16[32,4096]{1,0:T(8,128)(2,1)} %fusion.159), channel_id=1, source_target_pairs={{0,16},{1,17},{2,18},{3,19},{4,20},{5,21},{6,22},{7,23},{8,24},{9,... | collective-permute-start | bytes 786440 | tf_op jit(solution)/shard_map/while/body/eval_jaxpr/ppermute | solution.py:16
  95.3 4.5 %collective-permute-start.3 = (bf16[32,4096]{1,0:T(8,128)(2,1)}, bf16[32,4096]{1,0:T(8,128)(2,1)}, u32[]{:S(2)}, u32[]{:S(2)}) collective-permute-start(bf16[32,4096]{1,0:T(8,128)(2,1)} %fusion.159), channel_id=1, source_target_pairs={{0,16},{1,17},{2,18},{3,19},{4,20},{5,21},{6,22},{7,23},{8,24},{9,... | collective-permute-start | bytes 786440 | tf_op jit(solution)/shard_map/while/body/eval_jaxpr/ppermute | solution.py:16
  99.8 2.7 convolution_add_fusion.13
  115.5 4.5 %collective-permute-start.3 = (bf16[32,4096]{1,0:T(8,128)(2,1)}, bf16[32,4096]{1,0:T(8,128)(2,1)}, u32[]{:S(2)}, u32[]{:S(2)}) collective-permute-start(bf16[32,4096]{1,0:T(8,128)(2,1)} %fusion.159), channel_id=1, source_target_pairs={{0,16},{1,17},{2,18},{3,19},{4,20},{5,21},{6,22},{7,23},{8,24},{9,... | collective-permute-start | bytes 786440 | tf_op jit(solution)/shard_map/while/body/eval_jaxpr/ppermute | solution.py:16
  120.0 2.7 convolution_add_fusion.13
  128.6 78.3 %reduce-scatter.11.cloned.1.call-done = f32[64,256]{1,0:T(8,128)} async-done(((f32[64,4096]{1,0:T(8,128)}), f32[64,256]{1,0:T(8,128)}) %reduce-scatter.11.cloned.1.call-update) | async-done | bytes 65552 | tf_op jit(solution)/shard_map/reduce_scatter | solution.py:158
  206.9 76.4 %reduce-scatter.7.cloned.1.call-done = f32[64,256]{1,0:T(8,128)} async-done(((f32[64,4096]{1,0:T(8,128)}), f32[64,256]{1,0:T(8,128)}) %reduce-scatter.7.cloned.1.call-update) | async-done | bytes 65552 | tf_op jit(solution)/shard_map/reduce_scatter | solution.py:157
  283.4 76.6 %reduce-scatter.9.cloned.1.call-done = f32[64,256]{1,0:T(8,128)} async-done(((f32[64,4096]{1,0:T(8,128)}), f32[64,256]{1,0:T(8,128)}) %reduce-scatter.9.cloned.1.call-update) | async-done | bytes 65552 | tf_op jit(solution)/shard_map/reduce_scatter | solution.py:156
  360.0 1.5 add_bitcast_fusion
  361.5 74.8 %reduce-scatter.5.cloned.1.call-done = f32[64,256]{1,0:T(8,128)} async-done(((f32[64,4096]{1,0:T(8,128)}), f32[64,256]{1,0:T(8,128)}) %reduce-scatter.5.cloned.1.call-update) | async-done | bytes 65552 | tf_op jit(solution)/shard_map/reduce_scatter | solution.py:155
  436.2 1.5 add_bitcast_fusion.1
  (228 shorter events, 71.4 us)
Async XLA Ops:
  7.2 4.9 %copy-start.14 = (bf16[2,32,2048]{2,1,0:T(8,128)(2,1)S(1)}, bf16[2,32,2048]{2,1,0:T(8,128)(2,1)}, u32[]{:S(2)}) copy-start(bf16[2,32,2048]{2,1,0:T(8,128)(2,1)} %param.12) | copy-start | bytes 786436
  7.2 199.7 %reduce-scatter.11.cloned.1.call-start = ((), (), s32[]{:S(2)}) async-start(), calls=%async_computation.7 | async-start | bytes 1114112 | tf_op jit(solution)/shard_map/reduce_scatter | solution.py:158
  7.2 12.8 %collective-permute-start.4 = (bf16[1,4096]{1,0:T(2,128)(2,1)}, bf16[1,4096]{1,0:T(2,128)(2,1)S(1)}, u32[]{:S(2)}, u32[]{:S(2)}) collective-permute-start(bf16[1,4096]{1,0:T(2,128)(2,1)} %param.15), channel_id=1, source_target_pairs={{0,16},{16,0},{1,17},{17,1},{2,18},{18,2},{3,19},{19,3},{4,20},{20... | collective-permute-start | bytes 24584 | tf_op jit(solution)/shard_map/ppermute | solution.py:10
  7.7 12.3 %collective-permute-start.5 = (bf16[1,64,4096]{2,1,0:T(8,128)(2,1)}, bf16[1,64,4096]{2,1,0:T(8,128)(2,1)S(1)}, u32[]{:S(2)}, u32[]{:S(2)}) collective-permute-start(bf16[1,64,4096]{2,1,0:T(8,128)(2,1)} %param.16), channel_id=1, source_target_pairs={{0,16},{16,0},{1,17},{17,1},{2,18},{18,2},{3,19},{19,3},{4,20},{20... | collective-permute-start | bytes 1572872 | tf_op jit(solution)/shard_map/ppermute | solution.py:10
  7.8 12.3 %collective-permute-start.6 = (bf16[1,64,4096]{2,1,0:T(8,128)(2,1)}, bf16[1,64,4096]{2,1,0:T(8,128)(2,1)S(1)}, u32[]{:S(2)}, u32[]{:S(2)}) collective-permute-start(bf16[1,64,4096]{2,1,0:T(8,128)(2,1)} %param.17), channel_id=1, source_target_pairs={{0,16},{16,0},{1,17},{17,1},{2,18},{18,2},{3,19},{19,3},{4,20},{20... | collective-permute-start | bytes 1572872 | tf_op jit(solution)/shard_map/ppermute | solution.py:10
  25.4 8.8 %collective-permute-start = (bf16[32,4096]{1,0:T(8,128)(2,1)}, bf16[32,4096]{1,0:T(8,128)(2,1)}, u32[]{:S(2)}, u32[]{:S(2)}) collective-permute-start(bf16[32,4096]{1,0:T(8,128)(2,1)} %fusion.127), channel_id=1, source_target_pairs={{0,16},{1,17},{2,18},{3,19},{4,20},{5,21},{6,22},{7,23},{8,24},{9,... | collective-permute-start | bytes 786440 | tf_op jit(solution)/shard_map/while/body/eval_jaxpr/ppermute | solution.py:16
  32.9 3.6 collective-permute-start.1
  40.0 8.6 %collective-permute-start = (bf16[32,4096]{1,0:T(8,128)(2,1)}, bf16[32,4096]{1,0:T(8,128)(2,1)}, u32[]{:S(2)}, u32[]{:S(2)}) collective-permute-start(bf16[32,4096]{1,0:T(8,128)(2,1)} %fusion.127), channel_id=1, source_target_pairs={{0,16},{1,17},{2,18},{3,19},{4,20},{5,21},{6,22},{7,23},{8,24},{9,... | collective-permute-start | bytes 786440 | tf_op jit(solution)/shard_map/while/body/eval_jaxpr/ppermute | solution.py:16
  47.3 3.6 collective-permute-start.1
  54.3 8.6 %collective-permute-start = (bf16[32,4096]{1,0:T(8,128)(2,1)}, bf16[32,4096]{1,0:T(8,128)(2,1)}, u32[]{:S(2)}, u32[]{:S(2)}) collective-permute-start(bf16[32,4096]{1,0:T(8,128)(2,1)} %fusion.127), channel_id=1, source_target_pairs={{0,16},{1,17},{2,18},{3,19},{4,20},{5,21},{6,22},{7,23},{8,24},{9,... | collective-permute-start | bytes 786440 | tf_op jit(solution)/shard_map/while/body/eval_jaxpr/ppermute | solution.py:16
  61.6 3.6 collective-permute-start.1
  71.1 14.1 %collective-permute-start.2 = (bf16[32,4096]{1,0:T(8,128)(2,1)}, bf16[32,4096]{1,0:T(8,128)(2,1)}, u32[]{:S(2)}, u32[]{:S(2)}) collective-permute-start(bf16[32,4096]{1,0:T(8,128)(2,1)} %fusion.153), channel_id=1, source_target_pairs={{16,0},{17,1},{18,2},{19,3},{20,4},{21,5},{22,6},{23,7},{24,8},{25... | collective-permute-start | bytes 786440 | tf_op jit(solution)/shard_map/while/body/eval_jaxpr/ppermute | solution.py:16
  76.5 8.8 %collective-permute-start.3 = (bf16[32,4096]{1,0:T(8,128)(2,1)}, bf16[32,4096]{1,0:T(8,128)(2,1)}, u32[]{:S(2)}, u32[]{:S(2)}) collective-permute-start(bf16[32,4096]{1,0:T(8,128)(2,1)} %fusion.159), channel_id=1, source_target_pairs={{0,16},{1,17},{2,18},{3,19},{4,20},{5,21},{6,22},{7,23},{8,24},{9,... | collective-permute-start | bytes 786440 | tf_op jit(solution)/shard_map/while/body/eval_jaxpr/ppermute | solution.py:16
  86.2 2.8 copy-start.2
  89.9 15.5 %collective-permute-start.2 = (bf16[32,4096]{1,0:T(8,128)(2,1)}, bf16[32,4096]{1,0:T(8,128)(2,1)}, u32[]{:S(2)}, u32[]{:S(2)}) collective-permute-start(bf16[32,4096]{1,0:T(8,128)(2,1)} %fusion.153), channel_id=1, source_target_pairs={{16,0},{17,1},{18,2},{19,3},{20,4},{21,5},{22,6},{23,7},{24,8},{25... | collective-permute-start | bytes 786440 | tf_op jit(solution)/shard_map/while/body/eval_jaxpr/ppermute | solution.py:16
  95.3 10.1 %collective-permute-start.3 = (bf16[32,4096]{1,0:T(8,128)(2,1)}, bf16[32,4096]{1,0:T(8,128)(2,1)}, u32[]{:S(2)}, u32[]{:S(2)}) collective-permute-start(bf16[32,4096]{1,0:T(8,128)(2,1)} %fusion.159), channel_id=1, source_target_pairs={{0,16},{1,17},{2,18},{3,19},{4,20},{5,21},{6,22},{7,23},{8,24},{9,... | collective-permute-start | bytes 786440 | tf_op jit(solution)/shard_map/while/body/eval_jaxpr/ppermute | solution.py:16
  106.3 2.8 copy-start.2
  110.1 15.5 %collective-permute-start.2 = (bf16[32,4096]{1,0:T(8,128)(2,1)}, bf16[32,4096]{1,0:T(8,128)(2,1)}, u32[]{:S(2)}, u32[]{:S(2)}) collective-permute-start(bf16[32,4096]{1,0:T(8,128)(2,1)} %fusion.153), channel_id=1, source_target_pairs={{16,0},{17,1},{18,2},{19,3},{20,4},{21,5},{22,6},{23,7},{24,8},{25... | collective-permute-start | bytes 786440 | tf_op jit(solution)/shard_map/while/body/eval_jaxpr/ppermute | solution.py:16
  115.5 10.1 %collective-permute-start.3 = (bf16[32,4096]{1,0:T(8,128)(2,1)}, bf16[32,4096]{1,0:T(8,128)(2,1)}, u32[]{:S(2)}, u32[]{:S(2)}) collective-permute-start(bf16[32,4096]{1,0:T(8,128)(2,1)} %fusion.159), channel_id=1, source_target_pairs={{0,16},{1,17},{2,18},{3,19},{4,20},{5,21},{6,22},{7,23},{8,24},{9,... | collective-permute-start | bytes 786440 | tf_op jit(solution)/shard_map/while/body/eval_jaxpr/ppermute | solution.py:16
  126.5 156.8 %reduce-scatter.7.cloned.1.call-start = ((), (), s32[]{:S(2)}) async-start(), calls=%async_computation.5 | async-start | bytes 1114112 | tf_op jit(solution)/shard_map/reduce_scatter | solution.py:157
  127.3 232.7 %reduce-scatter.9.cloned.1.call-start = ((), (), s32[]{:S(2)}) async-start(), calls=%async_computation.6 | async-start | bytes 1114112 | tf_op jit(solution)/shard_map/reduce_scatter | solution.py:156
  128.0 308.2 %reduce-scatter.5.cloned.1.call-start = ((), (), s32[]{:S(2)}) async-start(), calls=%async_computation.4 | async-start | bytes 1114112 | tf_op jit(solution)/shard_map/reduce_scatter | solution.py:155
  206.9 153.1 %collective-permute-start.8 = (f32[64,256]{1,0:T(8,128)}, f32[64,256]{1,0:T(8,128)S(1)}, u32[]{:S(2)}, u32[]{:S(2)}) collective-permute-start(f32[64,256]{1,0:T(8,128)} %reduce-scatter.11.cloned.1.call-done), channel_id=1, source_target_pairs={{0,16},{16,0},{1,17},{17,1},{2,18},{18,2},{3,19},{19,3},{4,20},{20... | collective-permute-start | bytes 196616 | tf_op jit(solution)/shard_map/ppermute | solution.py:10
  283.4 152.9 %collective-permute-start.7 = (f32[64,256]{1,0:T(8,128)}, f32[64,256]{1,0:T(8,128)S(1)}, u32[]{:S(2)}, u32[]{:S(2)}) collective-permute-start(f32[64,256]{1,0:T(8,128)} %reduce-scatter.7.cloned.1.call-done), channel_id=1, source_target_pairs={{0,16},{16,0},{1,17},{17,1},{2,18},{18,2},{3,19},{19,3},{4,20},{20... | collective-permute-start | bytes 196616 | tf_op jit(solution)/shard_map/ppermute | solution.py:10
  (39 other events, 50.7 us)
Sparse Core Ops, SparseCore 0:
  126.7 80.2 reduce-scatter.10
  209.3 74.0 reduce-scatter.6
  285.6 74.3 reduce-scatter.8
  362.2 73.9 reduce-scatter.4
where the time goes:
time: 446 us; the launch traced here: 444 us
  waiting for transfers between devices  315 us (71%)
  starting transfers between devices  33.6 us (8%)
  matrix products  27.6 us (6%)
  local copies, waits for them, and re-layouts  22.4 us (5%)
  other arithmetic  20.2 us (5%)
  between operations  13.8 us (3%)
  blocking collectives  11 us (2%)
    reduce_scatter x1, waiting for transfers between devices, per_device(): lax.psum_scatter(mirror_gu, 'dp', scatter_dimension=1, tiled=True)  78.3 us
    reduce_scatter x1, waiting for transfers between devices, per_device(): lax.psum_scatter(own_gu, 'dp', scatter_dimension=1, tiled=True)  76.6 us
    reduce_scatter x1, waiting for transfers between devices, per_device(): lax.psum_scatter(mirror_gd, 'dp', scatter_dimension=1, tiled=True)  76.4 us
    reduce_scatter x1, waiting for transfers between devices, per_device(): lax.psum_scatter(own_gd, 'dp', scatter_dimension=1, tiled=True)  74.8 us
    ppermute x12, starting transfers between devices, shifted(): return lax.ppermute(block, axis, route)  32.4 us
    while x72, local copies, waits for them, and re-layouts  17.5 us
  transfers between devices with their start and end apart: 21, of which 7 were waited for; matrix products, arithmetic and copies ran while one was open for 7% of the time, Pallas kernels for 0%

commit v1 on v0

v1 whole, which is shorter than its diff:
```python
import functools

import jax
import jax.numpy as jnp
from jax import lax
from jax.experimental import pallas as pl
from jax.experimental.pallas import tpu as pltpu
from jax.sharding import PartitionSpec as P

epsilon = 1e-05
BOTH = ("section", "dp")
VMEM_BYTES = 32 * 1024 * 1024
f32 = jnp.float32
bf16 = jnp.bfloat16


def from_partner(value, axis, flip):
    return lax.ppermute(value, axis, [(i, i ^ flip) for i in range(lax.axis_size(axis))])


def dot_nn(left, right):
    return lax.dot_general(left, right, (((1,), (0,)), ((), ())), preferred_element_type=f32)


def dot_nt(left, right):
    return lax.dot_general(left, right, (((1,), (1,)), ((), ())), preferred_element_type=f32)


def split(value):
    high = value.astype(bf16)
    return high, (value - high.astype(f32)).astype(bf16)


def dot_split(left, right):
    high, low = split(left)
    return dot_nn(high, right) + dot_nn(low, right)


def rows_of(ref):
    value = ref[...]
    return value.reshape(-1, value.shape[-1])


def pack_kernel(width, group, members, place, *refs):
    acts = refs[:4]
    outs = refs[4:-1]
    sems = refs[-1]
    copies = []
    for k, out in enumerate(outs):
        index = place[1] ^ (k + 1)
        for a, act in enumerate(acts):
            for part in range(group):
                span = pl.ds(pl.multiple_of((part * members + index) * width, width), width)
                copies.append(
                    pltpu.make_async_copy(
                        act.at[:, :, span],
                        out.at[a, :, :, pl.ds(part * width, width)],
                        sems.at[len(copies)],
                    )
                )
                copies[-1].start()
    for copy in copies:
        copy.wait()


def products_kernel(layers, width, group, members, place, *refs):
    enter_down, enter_up, close_down, close_up = refs[:4]
    weights = [refs[4 + 3 * k : 7 + 3 * k] for k in range(layers)]
    piece_out, gain_out, low_out, high_out, prod_out, gram_out = refs[
        4 + 3 * layers : 10 + 3 * layers
    ]
    low_scr, fine_scr, high_scr, hidden_scr, close_scr = refs[10 + 3 * layers :]
    bottle = weights[0][1].shape[1]
    section = place[0]
    member = place[1]
    for k in range(layers):
        gain, down, up = weights[k]
        layer = section ^ k
        exact = gain[0].astype(f32) * down[0].astype(f32)
        low = exact.astype(bf16)
        low_scr[layer] = low
        fine_scr[layer] = (exact - low.astype(f32)).astype(bf16)
        high_scr[layer] = up[0]
        if group:
            for part in range(group):
                span = pl.ds(pl.multiple_of((part * members + member) * width, width), width)
                here = slice(part * width, (part + 1) * width)
                gain_out[layer, :, here] = gain[0, :, span].astype(f32)
    half = hidden_scr.shape[0] // 2
    hidden_scr[:half] = rows_of(enter_down)
    hidden_scr[half:] = rows_of(enter_up)
    close_scr[:half] = rows_of(close_down)
    close_scr[half:] = rows_of(close_up)
    if group:
        for part in range(group):
            span = pl.ds(pl.multiple_of((part * members + member) * width, width), width)
            here = slice(part * width, (part + 1) * width)
            low_out[:, :, here] = low_scr[:, :, span]
            high_out[:, :, here] = high_scr[:, :, span]
            piece_out[0, :, here] = hidden_scr[:, span]
            piece_out[1, :, here] = close_scr[:, span]
    hidden = hidden_scr[...]
    features = hidden.shape[-1]
    low_all = low_scr[...].reshape(layers * bottle, features)
    fine_all = fine_scr[...].reshape(layers * bottle, features)
    high_all = high_scr[...].reshape(layers * bottle, features)
    at = 0
    prod_out[: layers * bottle] = dot_nt(low_all, hidden) + dot_nt(fine_all, hidden)
    at += layers * bottle
    if layers > 1:
        prod_out[at : at + (layers - 1) * bottle] = dot_nt(
            high_all[: (layers - 1) * bottle], hidden
        )
        at += (layers - 1) * bottle
    prod_out[at : at + layers * bottle] = dot_nt(high_all, close_scr[...])
    at += layers * bottle
    square = dot_nt(hidden, hidden)
    eye = lax.broadcasted_iota(jnp.int32, square.shape, 0) == lax.broadcasted_iota(
        jnp.int32, square.shape, 1
    )
    norms = jnp.sum(jnp.where(eye, square, 0.0), axis=0, keepdims=True)
    prod_out[at : at + 8] = jnp.broadcast_to(norms, (8, norms.shape[1]))
    if layers > 1:
        high_part = high_all[: (layers - 1) * bottle]
        low_part = low_all[bottle:]
        fine_part = fine_all[bottle:]
        size = (layers - 1) * bottle
        gram_out[:size, :size] = jnp.zeros((size, size), f32)
        gram_out[:size, size:] = dot_nt(low_part, high_part) + dot_nt(fine_part, high_part)
        gram_out[size:, :size] = dot_nt(high_part, low_part) + dot_nt(high_part, fine_part)
        gram_out[size:, size:] = dot_nt(high_part, high_part)
    else:
        gram_out[...] = jnp.zeros_like(gram_out)


def relay_kernel(layers, bottle, features, sections, *refs):
    prods = refs[:sections]
    grams = refs[sections : 2 * sections]
    coef_out = refs[2 * sections]
    prod = sum((ref[...] for ref in prods[1:]), prods[0][...])
    gram = sum((ref[...] for ref in grams[1:]), grams[0][...])
    K = bottle
    inner = layers - 1
    h_low = [prod[l * K : (l + 1) * K] for l in range(layers)]
    at = layers * K
    h_high = [prod[at + l * K : at + (l + 1) * K] for l in range(inner)]
    at += inner * K
    u_high = [prod[at + l * K : at + (l + 1) * K] for l in range(layers)]
    at += layers * K
    norm = prod[at : at + 1]

    def low_high(l, m):
        return gram[(l - 1) * K : l * K, (inner + m) * K : (inner + m + 1) * K]

    def high_low(m, l):
        return gram[(inner + m) * K : (inner + m + 1) * K, (l - 1) * K : l * K]

    def high_high(m, n):
        return gram[
            (inner + m) * K : (inner + m + 1) * K, (inner + n) * K : (inner + n + 1) * K
        ]

    inverses, bottles, actives, hidden_high = [], [], [], []
    for l in range(layers):
        inverse = lax.rsqrt(jnp.maximum(norm, 0.0) * (1.0 / features) + epsilon)
        value = h_low[l] * inverse
        active = (value * jax.nn.sigmoid(value)).astype(bf16)
        inverses.append(inverse)
        bottles.append(value)
        actives.append(active)
        hidden_high.append(list(h_high))
        if l < inner:
            before = h_high[l]
            h_high = [h_high[n] + dot_split(high_high(n, l), active) for n in range(inner)]
            for n in range(l + 1, layers):
                h_low[n] = h_low[n] + dot_split(low_high(n, l), active)
            norm = norm + jnp.sum(
                active.astype(f32) * (before + h_high[l]), axis=0, keepdims=True
            )
    grads, pulls = [None] * layers, [None] * layers
    for l in range(layers - 1, -1, -1):
        sigma = jax.nn.sigmoid(bottles[l])
        grad = (u_high[l] * sigma * (1.0 + bottles[l] * (1.0 - sigma))).astype(bf16).astype(f32)
        scaled, fine = split(grad * inverses[l])
        pull = (
            inverses[l]
            * inverses[l]
            * jnp.sum(grad * bottles[l], axis=0, keepdims=True)
            * (1.0 / features)
        )
        grads[l], pulls[l] = grad.astype(bf16), pull
        for n in range(l):
            u_high[n] = (
                u_high[n]
                + dot_split(high_low(n, l), scaled)
                + dot_nn(high_low(n, l).astype(bf16), fine)
                - pull * hidden_high[l][n]
            )
    for l in range(layers):
        coef_out[l * K : (l + 1) * K] = actives[l]
        coef_out[(layers + l) * K : (layers + l + 1) * K] = grads[l]
    tail = coef_out.shape[0] - 2 * layers * K
    lines = [line.astype(bf16) for line in pulls[1:]]
    for l in range(layers):
        lines.extend(split(inverses[l]))
    lines = [line.astype(f32) for line in lines]
    lines += [jnp.zeros_like(pulls[0])] * (tail - len(lines))
    coef_out[2 * layers * K :] = jnp.concatenate(lines, axis=0).astype(bf16)


def grads_kernel(layers, bottle, width, group, members, place, *refs):
    K = bottle
    inner = layers - 1
    coefs = refs[:members]
    pieces = refs[members : 2 * members]
    gain, low, high = refs[2 * members : 2 * members + 3]
    outs = refs[2 * members + 3 : -1]
    parcel = refs[-1]
    by_hidden, by_close = 0.0, 0.0
    grad_active = [[0.0] * layers for _ in range(layers)]
    active_grad = [[0.0] * layers for _ in range(layers)]
    active_active = [[0.0] * layers for _ in range(layers)]
    for k in range(members):
        coef = coefs[k][...]
        actives = [coef[l * K : (l + 1) * K] for l in range(layers)]
        lines = coef[2 * layers * K :].astype(f32)
        scaled, fine = [], []
        for l in range(layers):
            at = inner + 2 * l
            inverse = lines[at : at + 1] + lines[at + 1 : at + 2]
            grad = coef[(layers + l) * K : (layers + l + 1) * K].astype(f32)
            coarse, rest = split(grad * inverse)
            scaled.append(coarse)
            fine.append(rest)
        pulled = [None] * layers
        total = None
        for l in range(inner - 1, -1, -1):
            line = lines[l : l + 1]
            total = line if total is None else total + line
            pulled[l] = (-total * actives[l].astype(f32)).astype(bf16)
        hidden = pieces[k][0]
        close = pieces[k][1]
        left = jnp.concatenate(scaled + fine + pulled[:inner], axis=0)
        by_hidden = by_hidden + dot_nn(left, hidden)
        by_close = by_close + dot_nn(coef[: layers * K], close)
        for l in range(layers):
            for n in range(l):
                grad_active[l][n] = grad_active[l][n] + dot_nt(scaled[l], actives[n])
                active_grad[n][l] = active_grad[n][l] + dot_nt(actives[n], scaled[l])
        for l in range(inner):
            for n in range(inner):
                if n <= l:
                    term = dot_nt(pulled[l], actives[n])
                else:
                    term = dot_nt(actives[l], pulled[n])
                active_active[l][n] = active_active[l][n] + term
    for l in range(layers):
        grad_down = (
            by_hidden[l * K : (l + 1) * K]
            + by_hidden[(layers + l) * K : (layers + l + 1) * K]
        )
        for n in range(l):
            grad_down = grad_down + dot_nn(grad_active[l][n].astype(bf16), high[n])
        grad_down = grad_down * gain[l]
        grad_up = by_close[l * K : (l + 1) * K]
        for n in range(l + 1, layers):
            grad_up = grad_up + dot_nn(active_grad[l][n].astype(bf16), low[n])
        if l < inner:
            grad_up = grad_up + by_hidden[
                (2 * layers + l) * K : (2 * layers + l + 1) * K
            ]
            for n in range(inner):
                grad_up = grad_up + dot_nn(active_active[l][n].astype(bf16), high[n])
        for part in range(group):
            here = slice(part * width, (part + 1) * width)
            parcel[l * group + part, 0] = grad_down[:, here].astype(bf16)
            parcel[l * group + part, 1] = grad_up[:, here].astype(bf16)
    if len(outs) == 1:
        outs[0][...] = parcel[...]
    else:
        for r, out in enumerate(outs):
            out[...] = parcel[place[2] ^ r]


def whole_spec(shape):
    return pl.BlockSpec(shape, lambda i, place: (0,) * len(shape))


def per_device(inputs_down, inputs_up, cotan_down, cotan_up, norm_gains, adapt_down, adapt_up):
    sections = lax.axis_size("section")
    replicas = lax.axis_size("dp")
    section = lax.axis_index("section")
    replica = lax.axis_index("dp")
    layers = sections
    members = min(4, replicas // sections)
    lines = replicas // members
    group = lines // sections
    bottle = adapt_down.shape[1]
    features = adapt_down.shape[2]
    share = features // sections
    width = features // replicas
    columns = group * width
    member = replica % members
    line = replica // members
    micro, tokens = inputs_down.shape[0], inputs_down.shape[1]
    half = micro * tokens
    rows = 2 * half
    aligned = width % 128 == 0
    place = jnp.stack([section, member, line]).astype(jnp.int32)

    own = (norm_gains[:, None, :], adapt_down, adapt_up)
    weights = [own]
    for k in range(1, sections):
        weights.append(tuple(from_partner(w, "section", k) for w in own))

    def piece(k):
        index = member ^ k
        parts = [
            lax.dynamic_index_in_dim(
                v.reshape(half, group, members, width), index, 2, keepdims=False
            ).reshape(half, columns)
            for v in (inputs_down, inputs_up, cotan_down, cotan_up)
        ]
        return jnp.concatenate(parts, axis=0).reshape(2, rows, columns)

    params = pltpu.CompilerParams(vmem_limit_bytes=VMEM_BYTES)
    acts = (inputs_down, inputs_up, cotan_down, cotan_up)
    if aligned:
        cut = (4, micro, tokens, columns)
        packed = pl.pallas_call(
            functools.partial(pack_kernel, width, group, members),
            out_shape=[jax.ShapeDtypeStruct(cut, bf16)] * (members - 1),
            in_specs=[pl.BlockSpec(memory_space=pltpu.SMEM)]
            + [pl.BlockSpec(memory_space=pl.ANY)] * 4,
            out_specs=[pl.BlockSpec(memory_space=pl.ANY)] * (members - 1),
            scratch_shapes=[pltpu.SemaphoreType.DMA((4 * group * (members - 1),))],
            compiler_params=params,
            name="pack",
        )(place, *acts)
        packed = [v.reshape(2, rows, columns) for v in packed]
    else:
        packed = [piece(k) for k in range(1, members)]
    pieces = [from_partner(v, "dp", k + 1) for k, v in enumerate(packed)]

    inner = max(layers - 1, 1)
    prod_rows = (3 * layers - 1) * bottle + 8
    block = pl.BlockSpec((1, 1, share), lambda i, place: (0, 0, place[0]))
    wide = pl.BlockSpec((1, bottle, share), lambda i, place: (0, 0, place[0]))
    own_shape = (layers, bottle, columns)
    out_shapes = [
        ((2, rows, columns), bf16),
        ((layers, 1, columns), f32),
        (own_shape, bf16),
        (own_shape, bf16),
        ((prod_rows, rows), f32),
        ((2 * inner * bottle, 2 * inner * bottle), f32),
    ]
    piece_own, gain_own, low_own, high_own, prod, gram = pl.pallas_call(
        functools.partial(
            products_kernel, layers, width, group if aligned else 0, members
        ),
        out_shape=[jax.ShapeDtypeStruct(s, d) for s, d in out_shapes],
        grid_spec=pltpu.PrefetchScalarGridSpec(
            num_scalar_prefetch=1,
            grid=(1,),
            in_specs=[whole_spec(v.shape) for v in acts] + [block, wide, wide] * sections,
            out_specs=[whole_spec(s) for s, _ in out_shapes],
            scratch_shapes=[
                pltpu.VMEM((layers, bottle, share), bf16),
                pltpu.VMEM((layers, bottle, share), bf16),
                pltpu.VMEM((layers, bottle, share), bf16),
                pltpu.VMEM((rows, share), bf16),
                pltpu.VMEM((rows, share), bf16),
            ],
        ),
        compiler_params=params,
        name="products",
    )(place, *acts, *[w for ws in weights for w in ws])
    if not aligned:
        piece_own = piece(0)
        layer_of = [section ^ k for k in range(sections)]

        def own_columns(which):
            shape = weights[0][which].shape[1]
            held = jnp.zeros((layers, shape, columns), bf16)
            for k in range(sections):
                cut = weights[k][which][0].reshape(shape, sections, group, members, width)
                cut = lax.dynamic_index_in_dim(cut, section, 1, keepdims=False)
                cut = lax.dynamic_index_in_dim(cut, member, 2, keepdims=False)
                held = lax.dynamic_update_index_in_dim(
                    held, cut.reshape(shape, columns), layer_of[k], 0
                )
            return held

        gain_own = own_columns(0).astype(f32)
        low_own = (own_columns(1).astype(f32) * gain_own).astype(bf16)
        high_own = own_columns(2)

    prods, grams = [prod], [gram]
    for k in range(1, sections):
        prods.append(from_partner(prod, "section", k))
        grams.append(from_partner(gram, "section", k))

    tail = layers - 1 + 2 * layers
    coef_rows = 2 * layers * bottle + -(-tail // 16) * 16
    coef = pl.pallas_call(
        functools.partial(relay_kernel, layers, bottle, features, sections),
        out_shape=jax.ShapeDtypeStruct((coef_rows, rows), bf16),
        compiler_params=params,
        name="relay",
    )(*prods, *grams)
    coefs = [coef]
    for k in range(1, members):
        coefs.append(from_partner(coef, "dp", k))

    message = (2, bottle, width)
    if aligned:
        sends = [(message, bf16)] * lines
    else:
        sends = [((lines,) + message, bf16)]
    operands = (*coefs, piece_own, *pieces, gain_own, low_own, high_own)
    parcels = pl.pallas_call(
        functools.partial(grads_kernel, layers, bottle, width, group, members),
        out_shape=[jax.ShapeDtypeStruct(s, d) for s, d in sends],
        grid_spec=pltpu.PrefetchScalarGridSpec(
            num_scalar_prefetch=1,
            grid=(1,),
            in_specs=[whole_spec(v.shape) for v in operands],
            out_specs=[whole_spec(s) for s, _ in sends],
            scratch_shapes=[pltpu.VMEM((lines,) + message, bf16)],
        ),
        compiler_params=params,
        name="grads",
    )(place, *operands)
    if not aligned:
        parcels = [
            lax.dynamic_index_in_dim(parcels[0], line ^ r, 0, keepdims=False)
            for r in range(lines)
        ]

    total = jnp.zeros(message, f32)
    for r in range(lines):
        route = []
        for c in range(sections):
            for g in range(lines):
                layer, part = divmod(g ^ r, group)
                for m in range(members):
                    target = (c * group + part) * members + m
                    route.append(
                        (c * replicas + g * members + m, layer * replicas + target)
                    )
        total = total + lax.ppermute(parcels[r], BOTH, route).astype(f32)
    return (total[0][None], total[1][None])


def solution(mesh):
    placed = (
        P(None, "dp", "section"),
        P(None, "dp", "section"),
        P(None, "dp", "section"),
        P(None, "dp", "section"),
        P("section", None),
        P("section", None, None),
        P("section", None, None),
    )
    return jax.shard_map(
        per_device,
        mesh=mesh,
        in_specs=placed,
        out_specs=(P("section", None, "dp"), P("section", None, "dp")),
        check_vma=False,
    )
```

time: 446 us -> 41.4 us (0.09)
  waiting for transfers between devices: 315 us -> 14.5 us
  matrix products: 27.6 us -> 0 us
  other arithmetic: 20.2 us -> 0.11 us
  local copies, waits for them, and re-layouts: 22.4 us -> 4.47 us
  starting transfers between devices: 33.6 us -> 16.3 us
  between operations: 13.8 us -> 0.7 us
  blocking collectives: 11 us -> 0 us
  Pallas kernels: 0 us -> 5.09 us
    reduce_scatter x4 -> x0, waiting for transfers between devices: 306 us -> none  [the longest x1 78.3 us: per_device(): lax.psum_scatter(mirror_gu, 'dp', scatter_dimension=1, tiled=True)]
    dot_general x36 -> x0, matrix products: 27.6 us -> none  [the longest x6 8.25 us: block_forward(): jnp.dot(active, up_proj, preferred_element_type=jnp.float32)]
    while x72 -> x0, local copies, waits for them, and re-layouts: 17.5 us -> none
    ppermute x17 -> x15, starting transfers between devices: 33.4 us -> 16.3 us  [the longest x11 10.3 us: from_partner(): lax.ppermute(value, axis, [(i, i ^ flip) for i in range(lax.axis_size(axi...]
    all_gather x4 -> x0, blocking collectives: 11 us -> none  [the longest x1 3.8 us: per_device(): lax.all_gather(inputs_down, 'section', axis=2, tiled=True)]
    ppermute x17 -> x15, waiting for transfers between devices: 7.01 us -> 14.5 us  [the longest x11 7.95 us: from_partner(): lax.ppermute(value, axis, [(i, i ^ flip) for i in range(lax.axis_size(axi...]
    select_n x6 -> x0, other arithmetic: 5.93 us -> none  [the longest x3 2.99 us: backward_step(): jnp.where(live_up, jnp.where(is_first, closing_up, recv_up), zero_rows)]
    convert_element_type x18 -> x0, other arithmetic: 5.48 us -> none  [the longest x6 5.44 us: block_backward(): (upstream_f + inverse * scaled - hidden_f * inverse ** 3 * project).astyp...]
  transfers between devices with their start and end apart: 21 -> 15, of which waited for: 7 -> 7; matrix products, arithmetic and copies ran while one was open for 7% -> 0% of each run, Pallas kernels for 0% -> 9%
where the time goes in v1:
time: 41.4 us; the launch traced here: 41.1 us
  starting transfers between devices  16.3 us (39%)
  waiting for transfers between devices  14.5 us (35%)
  Pallas kernels  5.09 us (12%)
  local copies, waits for them, and re-layouts  4.47 us (11%)
  between operations  0.7 us (2%)
    ppermute x11, starting transfers between devices, from_partner(): lax.ppermute(value, axis, [(i, i ^ flip) for i in range(lax.axis_size(axi...  10.3 us
    ppermute x11, waiting for transfers between devices, from_partner(): lax.ppermute(value, axis, [(i, i ^ flip) for i in range(lax.axis_size(axi...  7.95 us
    ppermute x4, waiting for transfers between devices, per_device(): total = total + lax.ppermute(parcels[r], BOTH, route).astype(f32)  6.5 us
    ppermute x4, starting transfers between devices, per_device(): total = total + lax.ppermute(parcels[r], BOTH, route).astype(f32)  6 us
    unnamed x14, local copies, waits for them, and re-layouts  3.81 us
    pallas_call x1, Pallas kernels, per_device(): pl.pallas_call(functools.partial(products_kernel, layers, width, group if...  2.27 us
    pallas_call x1, Pallas kernels, per_device(): pl.pallas_call(functools.partial(grads_kernel, layers, bottle, width, gro...  1.45 us
    pallas_call x1, Pallas kernels, per_device(): pl.pallas_call(functools.partial(pack_kernel, width, group, members), out...  0.97 us
  transfers between devices with their start and end apart: 15, of which 7 were waited for; matrix products, arithmetic and copies ran while one was open for 0% of the time, Pallas kernels for 9%

profile of v1, /device:TPU:0, one launch (start us, length us, event | category | flops | bytes accessed | tf_op | source)
XLA Modules:
  0.0 41.1 jit_solution(18381419474404012059)
XLA Ops:
  0.6 0.5 %collective-permute-start.1 = (bf16[1,64,4096]{2,1,0:T(8,128)(2,1)}, bf16[1,64,4096]{2,1,0:T(8,128)(2,1)S(1)}, u32[]{:S(2)}, u32[]{:S(2)}) collective-permute-start(bf16[1,64,4096]{2,1,0:T(8,128)(2,1)} %refs_5_.1), channel_id=1, source_target_pairs={{0,16},{16,0},{1,17},{17,1},{2,18},{18,2},{3,19},{19,3},{4,20},{20... | collective-permute-start | bytes 1572872 | tf_op jit(solution)/shard_map/ppermute | solution.py:18
  1.3 0.9 %copy-done = bf16[2,32,2048]{2,1,0:T(8,128)(2,1)S(1)} copy-done((bf16[2,32,2048]{2,1,0:T(8,128)(2,1)S(1)}, bf16[2,32,2048]{2,1,0:T(8,128)(2,1)}, u32[]{:S(2)}) %copy-start) | copy-done | bytes 262168
  2.3 0.9 %copy-done.1 = bf16[2,32,2048]{2,1,0:T(8,128)(2,1)S(1)} copy-done((bf16[2,32,2048]{2,1,0:T(8,128)(2,1)S(1)}, bf16[2,32,2048]{2,1,0:T(8,128)(2,1)}, u32[]{:S(2)}) %copy-start.1) | copy-done | bytes 262168
  3.2 0.9 %copy-done.2 = bf16[2,32,2048]{2,1,0:T(8,128)(2,1)S(1)} copy-done((bf16[2,32,2048]{2,1,0:T(8,128)(2,1)S(1)}, bf16[2,32,2048]{2,1,0:T(8,128)(2,1)}, u32[]{:S(2)}) %copy-start.2) | copy-done | bytes 262168
  4.2 0.9 %copy-done.3 = bf16[2,32,2048]{2,1,0:T(8,128)(2,1)S(1)} copy-done((bf16[2,32,2048]{2,1,0:T(8,128)(2,1)S(1)}, bf16[2,32,2048]{2,1,0:T(8,128)(2,1)}, u32[]{:S(2)}) %copy-start.3) | copy-done | bytes 262168
  5.1 1.0 %pack.1 = (bf16[4,2,32,512]{3,2,1,0:T(8,128)(2,1)S(1)}, bf16[4,2,32,512]{3,2,1,0:T(8,128)(2,1)S(1)}, bf16[4,2,32,512]{3,2,1,0:T(8,128)(2,1)S(1)}) custom-call(s32[3]{0:T(128)S(1)} %pad_add_fusion.place, bf16[2,32,2048]{2,1,0:T(8,128)(2,1)S(1)} %copy-done, bf16[2,32,2048]{2,1,0:T(8,128)(2,1)S(1)} %copy-done.1, bf16[2,32,2048]{2,1,0:T(8,128)(2,1)S(1)} %copy-done.2, ...), custom_call_target="tpu_custom_call" | custom-call | tf_op jit(solution)/shard_map/pack/pallas_call | solution.py:330
  6.1 3.0 %collective-permute-start.9 = (bf16[2,128,512]{2,1,0:T(8,128)(2,1)S(1)}, bf16[2,128,512]{2,1,0:T(8,128)(2,1)S(1)}, u32[]{:S(2)}, u32[]{:S(2)}) collective-permute-start(bf16[2,128,512]{2,1,0:T(8,128)(2,1)S(1)} %bitcast.11), channel_id=1, source_target_pairs={{0,2},{1,3},{2,0},{3,1},{4,6},{5,7},{6,4},{7,5},{8,10},{9,11},{10,... | collective-permute-start | bytes 786440 | tf_op jit(solution)/shard_map/ppermute | solution.py:18
  9.1 1.5 %collective-permute-start.8 = (bf16[2,128,512]{2,1,0:T(8,128)(2,1)S(1)}, bf16[2,128,512]{2,1,0:T(8,128)(2,1)S(1)}, u32[]{:S(2)}, u32[]{:S(2)}) collective-permute-start(bf16[2,128,512]{2,1,0:T(8,128)(2,1)S(1)} %bitcast.10), channel_id=1, source_target_pairs={{0,1},{1,0},{2,3},{3,2},{4,5},{5,4},{6,7},{7,6},{8,9},{9,8},{10,11... | collective-permute-start | bytes 786440 | tf_op jit(solution)/shard_map/ppermute | solution.py:18
  10.6 1.1 %collective-permute-start.10 = (bf16[2,128,512]{2,1,0:T(8,128)(2,1)S(1)}, bf16[2,128,512]{2,1,0:T(8,128)(2,1)S(1)}, u32[]{:S(2)}, u32[]{:S(2)}) collective-permute-start(bf16[2,128,512]{2,1,0:T(8,128)(2,1)S(1)} %bitcast.9), channel_id=1, source_target_pairs={{0,3},{1,2},{2,1},{3,0},{4,7},{5,6},{6,5},{7,4},{8,11},{9,10},{10,... | collective-permute-start | bytes 786440 | tf_op jit(solution)/shard_map/ppermute | solution.py:18
  11.7 2.3 %products.1 = (bf16[2,128,512]{2,1,0:T(8,128)(2,1)S(1)}, f32[2,1,512]{2,1,0:T(1,128)S(1)}, bf16[2,64,512]{2,1,0:T(8,128)(2,1)S(1)}, bf16[2,64,512]{2,1,0:T(8,128...) custom-call(s32[3]{0:T(128)S(1)} %pad_add_fusion.place, bf16[2,32,2048]{2,1,0:T(8,128)(2,1)S(1)} %copy-done, ...), custom_call_target="tpu_custom_call" | custom-call | tf_op jit(solution)/shard_map/products/pallas_call | solution.py:358
  14.6 1.0 %collective-permute-done.4.refs_3_ = f32[128,128]{1,0:T(8,128)S(1)} collective-permute-done((f32[128,128]{1,0:T(8,128)S(1)}, f32[128,128]{1,0:T(8,128)S(1)}, u32[]{:S(2)}, u32[]{:S(2)}) %collective-permute-start.4) | collective-permute-done | bytes 65568 | tf_op jit(solution)/shard_map/ppermute | solution.py:18
  16.0 1.9 %collective-permute-start.7 = (bf16[272,128]{1,0:T(8,128)(2,1)S(1)}, bf16[272,128]{1,0:T(8,128)(2,1)S(1)}, u32[]{:S(2)}, u32[]{:S(2)}) collective-permute-start(bf16[272,128]{1,0:T(8,128)(2,1)S(1)} %relay.1.refs_0_), channel_id=1, source_target_pairs={{0,3},{1,2},{2,1},{3,0},{4,7},{5,6},{6,5},{7,4},{8,11},{9,10},{10,... | collective-permute-start | bytes 208904 | tf_op jit(solution)/shard_map/ppermute | solution.py:18
  17.8 0.5 %collective-permute-start.6 = (bf16[272,128]{1,0:T(8,128)(2,1)S(1)}, bf16[272,128]{1,0:T(8,128)(2,1)S(1)}, u32[]{:S(2)}, u32[]{:S(2)}) collective-permute-start(bf16[272,128]{1,0:T(8,128)(2,1)S(1)} %relay.1.refs_0_), channel_id=1, source_target_pairs={{0,2},{1,3},{2,0},{3,1},{4,6},{5,7},{6,4},{7,5},{8,10},{9,11},{10,... | collective-permute-start | bytes 208904 | tf_op jit(solution)/shard_map/ppermute | solution.py:18
  18.3 1.2 %collective-permute-start.5 = (bf16[272,128]{1,0:T(8,128)(2,1)S(1)}, bf16[272,128]{1,0:T(8,128)(2,1)S(1)}, u32[]{:S(2)}, u32[]{:S(2)}) collective-permute-start(bf16[272,128]{1,0:T(8,128)(2,1)S(1)} %relay.1.refs_0_), channel_id=1, source_target_pairs={{0,1},{1,0},{2,3},{3,2},{4,5},{5,4},{6,7},{7,6},{8,9},{9,8},{10,11... | collective-permute-start | bytes 208904 | tf_op jit(solution)/shard_map/ppermute | solution.py:18
  19.5 4.0 %collective-permute-done.10.refs_7_ = bf16[2,128,512]{2,1,0:T(8,128)(2,1)S(1)} collective-permute-done((bf16[2,128,512]{2,1,0:T(8,128)(2,1)S(1)}, bf16[2,128,512]{2,1,0:T(8,128)(2,1)S(1)}, u32[]{:S(2)}, u32[]{:S(2)}) %collective-permute-start.10) | collective-permute-done | bytes 262176 | tf_op jit(solution)/shard_map/ppermute | solution.py:18
  23.5 1.4 %collective-permute-done.7.refs_3_ = bf16[272,128]{1,0:T(8,128)(2,1)S(1)} collective-permute-done((bf16[272,128]{1,0:T(8,128)(2,1)S(1)}, bf16[272,128]{1,0:T(8,128)(2,1)S(1)}, u32[]{:S(2)}, u32[]{:S(2)}) %collective-permute-start.7) | collective-permute-done | bytes 69664 | tf_op jit(solution)/shard_map/ppermute | solution.py:18
  25.0 1.2 %collective-permute-done.6.refs_2_ = bf16[272,128]{1,0:T(8,128)(2,1)S(1)} collective-permute-done((bf16[272,128]{1,0:T(8,128)(2,1)S(1)}, bf16[272,128]{1,0:T(8,128)(2,1)S(1)}, u32[]{:S(2)}, u32[]{:S(2)}) %collective-permute-start.6) | collective-permute-done | bytes 69664 | tf_op jit(solution)/shard_map/ppermute | solution.py:18
  26.5 1.5 %grads.1 = (bf16[2,64,256]{2,1,0:T(8,128)(2,1)S(1)}, bf16[2,64,256]{2,1,0:T(8,128)(2,1)S(1)}, bf16[2,64,256]{2,1,0:T(8,128)(2,1)S(1)}, bf16[2,64,256]{2,1,0:T(8,128)(2,1)S(1)}) custom-call(s32[3]{0:T(128)S(1)} %pad_add_fusion.place, bf16[272,128]{1,0:T(8,128)(2,1)S(1)} %relay.1.refs_0_, bf16[272,128]{1,0:T(8,128)(2,1)S(1)} %collective-permute-done.5.refs_1_, ...), custom_call_target="tpu_custom_call" | custom-call | tf_op jit(solution)/shard_map/grads/pallas_call | solution.py:422
  27.9 0.7 %collective-permute-start.11 = (bf16[2,64,256]{2,1,0:T(8,128)(2,1)S(1)}, bf16[2,64,256]{2,1,0:T(8,128)(2,1)S(1)}, u32[]{:S(2)}, u32[]{:S(2)}) collective-permute-start(bf16[2,64,256]{2,1,0:T(8,128)(2,1)S(1)} %get-tuple-element.24), channel_id=1, source_target_pairs={{0,0},{1,1},{2,2},{3,3},{4,4},{5,5},{6,6},{7,7},{8,16},{9,17},{10,... | collective-permute-start | bytes 196616 | tf_op jit(solution)/shard_map/ppermute | solution.py:452
  28.6 1.6 %collective-permute-start.12 = (bf16[2,64,256]{2,1,0:T(8,128)(2,1)S(1)}, bf16[2,64,256]{2,1,0:T(8,128)(2,1)S(1)}, u32[]{:S(2)}, u32[]{:S(2)}) collective-permute-start(bf16[2,64,256]{2,1,0:T(8,128)(2,1)S(1)} %get-tuple-element.25), channel_id=1, source_target_pairs={{0,4},{1,5},{2,6},{3,7},{4,0},{5,1},{6,2},{7,3},{8,20},{9,21},{10,... | collective-permute-start | bytes 196616 | tf_op jit(solution)/shard_map/ppermute | solution.py:452
  30.2 3.4 %collective-permute-start.13 = (bf16[2,64,256]{2,1,0:T(8,128)(2,1)S(1)}, bf16[2,64,256]{2,1,0:T(8,128)(2,1)S(1)}, u32[]{:S(2)}, u32[]{:S(2)}) collective-permute-start(bf16[2,64,256]{2,1,0:T(8,128)(2,1)S(1)} %get-tuple-element.26), channel_id=1, source_target_pairs={{0,16},{1,17},{2,18},{3,19},{4,20},{5,21},{6,22},{7,23},{8,0},{9,1... | collective-permute-start | bytes 196616 | tf_op jit(solution)/shard_map/ppermute | solution.py:452
  34.0 5.0 %collective-permute-done.13 = bf16[2,64,256]{2,1,0:T(8,128)(2,1)S(1)} collective-permute-done((bf16[2,64,256]{2,1,0:T(8,128)(2,1)S(1)}, bf16[2,64,256]{2,1,0:T(8,128)(2,1)S(1)}, u32[]{:S(2)}, u32[]{:S(2)}) %collective-permute-start.13) | collective-permute-done | bytes 65568 | tf_op jit(solution)/shard_map/ppermute | solution.py:452
  38.9 1.5 %collective-permute-done.14 = bf16[2,64,256]{2,1,0:T(8,128)(2,1)S(1)} collective-permute-done((bf16[2,64,256]{2,1,0:T(8,128)(2,1)S(1)}, bf16[2,64,256]{2,1,0:T(8,128)(2,1)S(1)}, u32[]{:S(2)}, u32[]{:S(2)}) %collective-permute-start.14) | collective-permute-done | bytes 65568 | tf_op jit(solution)/shard_map/ppermute | solution.py:452
  40.5 0.7 %fusion = (f32[1,64,256]{2,1,0:T(8,128)}, f32[1,64,256]{2,1,0:T(8,128)}) fusion(f32[2,64,256]{2,1,0:T(8,128)S(1)} %convert_add_fusion), kind=kLoop, calls=%fused_computation.2 | loop fusion | bytes 262144 | tf_op jit(solution)/shard_map/slice | solution.py:453
  (27 shorter events, 1.8 us)
Async XLA Ops:
  0.6 11.1 %collective-permute-start.1 = (bf16[1,64,4096]{2,1,0:T(8,128)(2,1)}, bf16[1,64,4096]{2,1,0:T(8,128)(2,1)S(1)}, u32[]{:S(2)}, u32[]{:S(2)}) collective-permute-start(bf16[1,64,4096]{2,1,0:T(8,128)(2,1)} %refs_5_.1), channel_id=1, source_target_pairs={{0,16},{16,0},{1,17},{17,1},{2,18},{18,2},{3,19},{19,3},{4,20},{20... | collective-permute-start | bytes 1572872 | tf_op jit(solution)/shard_map/ppermute | solution.py:18
  1.1 10.6 %collective-permute-start.2 = (bf16[1,64,4096]{2,1,0:T(8,128)(2,1)}, bf16[1,64,4096]{2,1,0:T(8,128)(2,1)S(1)}, u32[]{:S(2)}, u32[]{:S(2)}) collective-permute-start(bf16[1,64,4096]{2,1,0:T(8,128)(2,1)} %refs_6_.1), channel_id=1, source_target_pairs={{0,16},{16,0},{1,17},{17,1},{2,18},{18,2},{3,19},{19,3},{4,20},{20... | collective-permute-start | bytes 1572872 | tf_op jit(solution)/shard_map/ppermute | solution.py:18
  1.2 7.9 %copy-start.6 = (bf16[1,4096]{1,0:T(2,128)(2,1)S(1)}, bf16[1,4096]{1,0:T(2,128)(2,1)}, u32[]{:S(2)}) copy-start(bf16[1,4096]{1,0:T(2,128)(2,1)} %param.11) | copy-start | bytes 24580
  1.3 1.0 %copy-start = (bf16[2,32,2048]{2,1,0:T(8,128)(2,1)S(1)}, bf16[2,32,2048]{2,1,0:T(8,128)(2,1)}, u32[]{:S(2)}) copy-start(bf16[2,32,2048]{2,1,0:T(8,128)(2,1)} %refs_0_.3) | copy-start | bytes 786436
  2.3 0.9 %copy-start.1 = (bf16[2,32,2048]{2,1,0:T(8,128)(2,1)S(1)}, bf16[2,32,2048]{2,1,0:T(8,128)(2,1)}, u32[]{:S(2)}) copy-start(bf16[2,32,2048]{2,1,0:T(8,128)(2,1)} %refs_1_.3) | copy-start | bytes 786436
  3.2 0.9 %copy-start.2 = (bf16[2,32,2048]{2,1,0:T(8,128)(2,1)S(1)}, bf16[2,32,2048]{2,1,0:T(8,128)(2,1)}, u32[]{:S(2)}) copy-start(bf16[2,32,2048]{2,1,0:T(8,128)(2,1)} %refs_2_.3) | copy-start | bytes 786436
  4.2 0.9 %copy-start.3 = (bf16[2,32,2048]{2,1,0:T(8,128)(2,1)S(1)}, bf16[2,32,2048]{2,1,0:T(8,128)(2,1)}, u32[]{:S(2)}) copy-start(bf16[2,32,2048]{2,1,0:T(8,128)(2,1)} %refs_3_.3) | copy-start | bytes 786436
  5.1 6.6 %copy-start.4 = (bf16[1,64,4096]{2,1,0:T(8,128)(2,1)S(1)}, bf16[1,64,4096]{2,1,0:T(8,128)(2,1)}, u32[]{:S(2)}) copy-start(bf16[1,64,4096]{2,1,0:T(8,128)(2,1)} %refs_5_.1) | copy-start | bytes 1572868
  5.1 6.6 %copy-start.5 = (bf16[1,64,4096]{2,1,0:T(8,128)(2,1)S(1)}, bf16[1,64,4096]{2,1,0:T(8,128)(2,1)}, u32[]{:S(2)}) copy-start(bf16[1,64,4096]{2,1,0:T(8,128)(2,1)} %refs_6_.1) | copy-start | bytes 1572868
  6.1 12.2 %collective-permute-start.9 = (bf16[2,128,512]{2,1,0:T(8,128)(2,1)S(1)}, bf16[2,128,512]{2,1,0:T(8,128)(2,1)S(1)}, u32[]{:S(2)}, u32[]{:S(2)}) collective-permute-start(bf16[2,128,512]{2,1,0:T(8,128)(2,1)S(1)} %bitcast.11), channel_id=1, source_target_pairs={{0,2},{1,3},{2,0},{3,1},{4,6},{5,7},{6,4},{7,5},{8,10},{9,11},{10,... | collective-permute-start | bytes 786440 | tf_op jit(solution)/shard_map/ppermute | solution.py:18
  9.1 1.5 %collective-permute-start = (bf16[1,1,4096]{2,1,0:T(2,128)(2,1)S(1)}, bf16[1,1,4096]{2,1,0:T(2,128)(2,1)S(1)}, u32[]{:S(2)}, u32[]{:S(2)}) collective-permute-start(bf16[1,1,4096]{2,1,0:T(2,128)(2,1)S(1)} %bitcast.7), channel_id=1, source_target_pairs={{0,16},{16,0},{1,17},{17,1},{2,18},{18,2},{3,19},{19,3},{4,20},{20... | collective-permute-start | bytes 24584 | tf_op jit(solution)/shard_map/ppermute | solution.py:18
  9.1 10.4 %collective-permute-start.8 = (bf16[2,128,512]{2,1,0:T(8,128)(2,1)S(1)}, bf16[2,128,512]{2,1,0:T(8,128)(2,1)S(1)}, u32[]{:S(2)}, u32[]{:S(2)}) collective-permute-start(bf16[2,128,512]{2,1,0:T(8,128)(2,1)S(1)} %bitcast.10), channel_id=1, source_target_pairs={{0,1},{1,0},{2,3},{3,2},{4,5},{5,4},{6,7},{7,6},{8,9},{9,8},{10,11... | collective-permute-start | bytes 786440 | tf_op jit(solution)/shard_map/ppermute | solution.py:18
  10.6 12.9 %collective-permute-start.10 = (bf16[2,128,512]{2,1,0:T(8,128)(2,1)S(1)}, bf16[2,128,512]{2,1,0:T(8,128)(2,1)S(1)}, u32[]{:S(2)}, u32[]{:S(2)}) collective-permute-start(bf16[2,128,512]{2,1,0:T(8,128)(2,1)S(1)} %bitcast.9), channel_id=1, source_target_pairs={{0,3},{1,2},{2,1},{3,0},{4,7},{5,6},{6,5},{7,4},{8,11},{9,10},{10,... | collective-permute-start | bytes 786440 | tf_op jit(solution)/shard_map/ppermute | solution.py:18
  14.0 1.5 %collective-permute-start.3 = (f32[328,128]{1,0:T(8,128)S(1)}, f32[328,128]{1,0:T(8,128)S(1)}, u32[]{:S(2)}, u32[]{:S(2)}) collective-permute-start(f32[328,128]{1,0:T(8,128)S(1)} %get-tuple-element.15.refs_0_), channel_id=1, source_target_pairs={{0,16},{16,0},{1,17},{17,1},{2,18},{18,2},{3,19},{19,3},{4,20},{20... | collective-permute-start | bytes 503816 | tf_op jit(solution)/shard_map/ppermute | solution.py:18
  14.1 1.5 %collective-permute-start.4 = (f32[128,128]{1,0:T(8,128)S(1)}, f32[128,128]{1,0:T(8,128)S(1)}, u32[]{:S(2)}, u32[]{:S(2)}) collective-permute-start(f32[128,128]{1,0:T(8,128)S(1)} %get-tuple-element.16.refs_2_), channel_id=1, source_target_pairs={{0,16},{16,0},{1,17},{17,1},{2,18},{18,2},{3,19},{19,3},{4,20},{20... | collective-permute-start | bytes 196616 | tf_op jit(solution)/shard_map/ppermute | solution.py:18
  16.0 9.0 %collective-permute-start.7 = (bf16[272,128]{1,0:T(8,128)(2,1)S(1)}, bf16[272,128]{1,0:T(8,128)(2,1)S(1)}, u32[]{:S(2)}, u32[]{:S(2)}) collective-permute-start(bf16[272,128]{1,0:T(8,128)(2,1)S(1)} %relay.1.refs_0_), channel_id=1, source_target_pairs={{0,3},{1,2},{2,1},{3,0},{4,7},{5,6},{6,5},{7,4},{8,11},{9,10},{10,... | collective-permute-start | bytes 208904 | tf_op jit(solution)/shard_map/ppermute | solution.py:18
  17.8 8.3 %collective-permute-start.6 = (bf16[272,128]{1,0:T(8,128)(2,1)S(1)}, bf16[272,128]{1,0:T(8,128)(2,1)S(1)}, u32[]{:S(2)}, u32[]{:S(2)}) collective-permute-start(bf16[272,128]{1,0:T(8,128)(2,1)S(1)} %relay.1.refs_0_), channel_id=1, source_target_pairs={{0,2},{1,3},{2,0},{3,1},{4,6},{5,7},{6,4},{7,5},{8,10},{9,11},{10,... | collective-permute-start | bytes 208904 | tf_op jit(solution)/shard_map/ppermute | solution.py:18
  18.3 8.1 %collective-permute-start.5 = (bf16[272,128]{1,0:T(8,128)(2,1)S(1)}, bf16[272,128]{1,0:T(8,128)(2,1)S(1)}, u32[]{:S(2)}, u32[]{:S(2)}) collective-permute-start(bf16[272,128]{1,0:T(8,128)(2,1)S(1)} %relay.1.refs_0_), channel_id=1, source_target_pairs={{0,1},{1,0},{2,3},{3,2},{4,5},{5,4},{6,7},{7,6},{8,9},{9,8},{10,11... | collective-permute-start | bytes 208904 | tf_op jit(solution)/shard_map/ppermute | solution.py:18
  27.9 6.0 %collective-permute-start.11 = (bf16[2,64,256]{2,1,0:T(8,128)(2,1)S(1)}, bf16[2,64,256]{2,1,0:T(8,128)(2,1)S(1)}, u32[]{:S(2)}, u32[]{:S(2)}) collective-permute-start(bf16[2,64,256]{2,1,0:T(8,128)(2,1)S(1)} %get-tuple-element.24), channel_id=1, source_target_pairs={{0,0},{1,1},{2,2},{3,3},{4,4},{5,5},{6,6},{7,7},{8,16},{9,17},{10,... | collective-permute-start | bytes 196616 | tf_op jit(solution)/shard_map/ppermute | solution.py:452
  28.6 5.3 %collective-permute-start.12 = (bf16[2,64,256]{2,1,0:T(8,128)(2,1)S(1)}, bf16[2,64,256]{2,1,0:T(8,128)(2,1)S(1)}, u32[]{:S(2)}, u32[]{:S(2)}) collective-permute-start(bf16[2,64,256]{2,1,0:T(8,128)(2,1)S(1)} %get-tuple-element.25), channel_id=1, source_target_pairs={{0,4},{1,5},{2,6},{3,7},{4,0},{5,1},{6,2},{7,3},{8,20},{9,21},{10,... | collective-permute-start | bytes 196616 | tf_op jit(solution)/shard_map/ppermute | solution.py:452
  30.2 8.7 %collective-permute-start.13 = (bf16[2,64,256]{2,1,0:T(8,128)(2,1)S(1)}, bf16[2,64,256]{2,1,0:T(8,128)(2,1)S(1)}, u32[]{:S(2)}, u32[]{:S(2)}) collective-permute-start(bf16[2,64,256]{2,1,0:T(8,128)(2,1)S(1)} %get-tuple-element.26), channel_id=1, source_target_pairs={{0,16},{1,17},{2,18},{3,19},{4,20},{5,21},{6,22},{7,23},{8,0},{9,1... | collective-permute-start | bytes 196616 | tf_op jit(solution)/shard_map/ppermute | solution.py:452
  33.6 6.8 %collective-permute-start.14 = (bf16[2,64,256]{2,1,0:T(8,128)(2,1)S(1)}, bf16[2,64,256]{2,1,0:T(8,128)(2,1)S(1)}, u32[]{:S(2)}, u32[]{:S(2)}) collective-permute-start(bf16[2,64,256]{2,1,0:T(8,128)(2,1)S(1)} %get-tuple-element.27), channel_id=1, source_target_pairs={{0,20},{1,21},{2,22},{3,23},{4,16},{5,17},{6,18},{7,19},{8,4},{9,5... | collective-permute-start | bytes 196616 | tf_op jit(solution)/shard_map/ppermute | solution.py:452

commit v2 on v1

--- a/solution.py
+++ b/solution.py
@@ -36,71 +36,66 @@
     return dot_nn(high, right) + dot_nn(low, right)
 
 
-def rows_of(ref):
-    value = ref[...]
-    return value.reshape(-1, value.shape[-1])
-
-
 def pack_kernel(width, group, members, place, *refs):
     acts = refs[:4]
-    outs = refs[4:-1]
+    both = refs[4]
+    outs = refs[5 : 5 + members]
     sems = refs[-1]
+    micro, tokens = acts[0].shape[0], acts[0].shape[1]
     copies = []
-    for k, out in enumerate(outs):
-        index = place[1] ^ (k + 1)
-        for a, act in enumerate(acts):
+    for a, act in enumerate(acts):
+        for m in range(micro):
+            start = ((a % 2) * micro + m) * tokens
+            copies.append(
+                pltpu.make_async_copy(
+                    act.at[m], both.at[a // 2, pl.ds(start, tokens)], sems.at[len(copies)]
+                )
+            )
+            copies[-1].start()
+    for n, copy in enumerate(copies):
+        copy.wait()
+        a, m = divmod(n, micro)
+        start = ((a % 2) * micro + m) * tokens
+        for k, out in enumerate(outs):
+            index = place[1] ^ k
             for part in range(group):
                 span = pl.ds(pl.multiple_of((part * members + index) * width, width), width)
-                copies.append(
-                    pltpu.make_async_copy(
-                        act.at[:, :, span],
-                        out.at[a, :, :, pl.ds(part * width, width)],
-                        sems.at[len(copies)],
-                    )
-                )
-                copies[-1].start()
-    for copy in copies:
-        copy.wait()
+                out[a // 2, start : start + tokens, part * width : (part + 1) * width] = both[
+                    a // 2, start : start + tokens, span
+                ]
 
 
 def products_kernel(layers, width, group, members, place, *refs):
-    enter_down, enter_up, close_down, close_up = refs[:4]
-    weights = [refs[4 + 3 * k : 7 + 3 * k] for k in range(layers)]
-    piece_out, gain_out, low_out, high_out, prod_out, gram_out = refs[
-        4 + 3 * layers : 10 + 3 * layers
-    ]
-    low_scr, fine_scr, high_scr, hidden_scr, close_scr = refs[10 + 3 * layers :]
+    acts = refs[0]
+    weights = [refs[1 + 3 * k : 4 + 3 * k] for k in range(layers)]
+    gain_out, low_out, high_out, prod_out, gram_out = refs[1 + 3 * layers : 6 + 3 * layers]
+    low_scr, fine_scr, high_scr = refs[6 + 3 * layers :]
     bottle = weights[0][1].shape[1]
+    features = acts.shape[2]
     section = place[0]
     member = place[1]
+    mine = pl.ds(pl.multiple_of(section * features, features), features)
     for k in range(layers):
         gain, down, up = weights[k]
         layer = section ^ k
-        exact = gain[0].astype(f32) * down[0].astype(f32)
+        exact = gain[0, :, mine].astype(f32) * down[0, :, mine].astype(f32)
         low = exact.astype(bf16)
         low_scr[layer] = low
         fine_scr[layer] = (exact - low.astype(f32)).astype(bf16)
-        high_scr[layer] = up[0]
+        high_scr[layer] = up[0, :, mine]
         if group:
             for part in range(group):
-                span = pl.ds(pl.multiple_of((part * members + member) * width, width), width)
+                begin = section * features + (part * members + member) * width
+                span = pl.ds(pl.multiple_of(begin, width), width)
                 here = slice(part * width, (part + 1) * width)
                 gain_out[layer, :, here] = gain[0, :, span].astype(f32)
-    half = hidden_scr.shape[0] // 2
-    hidden_scr[:half] = rows_of(enter_down)
-    hidden_scr[half:] = rows_of(enter_up)
-    close_scr[:half] = rows_of(close_down)
-    close_scr[half:] = rows_of(close_up)
     if group:
         for part in range(group):
             span = pl.ds(pl.multiple_of((part * members + member) * width, width), width)
             here = slice(part * width, (part + 1) * width)
             low_out[:, :, here] = low_scr[:, :, span]
             high_out[:, :, here] = high_scr[:, :, span]
-            piece_out[0, :, here] = hidden_scr[:, span]
-            piece_out[1, :, here] = close_scr[:, span]
-    hidden = hidden_scr[...]
-    features = hidden.shape[-1]
+    hidden = acts[0]
     low_all = low_scr[...].reshape(layers * bottle, features)
     fine_all = fine_scr[...].reshape(layers * bottle, features)
     high_all = high_scr[...].reshape(layers * bottle, features)
@@ -112,7 +107,7 @@
             high_all[: (layers - 1) * bottle], hidden
         )
         at += (layers - 1) * bottle
-    prod_out[at : at + layers * bottle] = dot_nt(high_all, close_scr[...])
+    prod_out[at : at + layers * bottle] = dot_nt(high_all, acts[1])
     at += layers * bottle
     square = dot_nt(hidden, hidden)
     eye = lax.broadcasted_iota(jnp.int32, square.shape, 0) == lax.broadcasted_iota(
@@ -282,8 +277,8 @@
             out[...] = parcel[place[2] ^ r]
 
 
-def whole_spec(shape):
-    return pl.BlockSpec(shape, lambda i, place: (0,) * len(shape))
+IN_SMEM = pl.BlockSpec(memory_space=pltpu.SMEM)
+IN_VMEM = pl.BlockSpec(memory_space=pltpu.VMEM)
 
 
 def per_device(inputs_down, inputs_up, cotan_down, cotan_up, norm_gains, adapt_down, adapt_up):
@@ -326,56 +321,43 @@
     params = pltpu.CompilerParams(vmem_limit_bytes=VMEM_BYTES)
     acts = (inputs_down, inputs_up, cotan_down, cotan_up)
     if aligned:
-        cut = (4, micro, tokens, columns)
-        packed = pl.pallas_call(
+        both, piece_own, *packed = pl.pallas_call(
             functools.partial(pack_kernel, width, group, members),
-            out_shape=[jax.ShapeDtypeStruct(cut, bf16)] * (members - 1),
-            in_specs=[pl.BlockSpec(memory_space=pltpu.SMEM)]
-            + [pl.BlockSpec(memory_space=pl.ANY)] * 4,
-            out_specs=[pl.BlockSpec(memory_space=pl.ANY)] * (members - 1),
-            scratch_shapes=[pltpu.SemaphoreType.DMA((4 * group * (members - 1),))],
+            out_shape=[pltpu.VMEM((2, rows, share), bf16)]
+            + [pltpu.VMEM((2, rows, columns), bf16)] * members,
+            in_specs=[IN_SMEM] + [pl.BlockSpec(memory_space=pltpu.HBM)] * 4,
+            out_specs=[IN_VMEM] * (1 + members),
+            scratch_shapes=[pltpu.SemaphoreType.DMA((4 * micro,))],
             compiler_params=params,
             name="pack",
-        )(place, *acts)
-        packed = [v.reshape(2, rows, columns) for v in packed]
+        )(place, *[pltpu.with_memory_space_constraint(v, pltpu.HBM) for v in acts])
     else:
+        both = jnp.concatenate([v.reshape(half, share) for v in acts], axis=0)
+        both = both.reshape(2, rows, share)
         packed = [piece(k) for k in range(1, members)]
     pieces = [from_partner(v, "dp", k + 1) for k, v in enumerate(packed)]
 
     inner = max(layers - 1, 1)
     prod_rows = (3 * layers - 1) * bottle + 8
-    block = pl.BlockSpec((1, 1, share), lambda i, place: (0, 0, place[0]))
-    wide = pl.BlockSpec((1, bottle, share), lambda i, place: (0, 0, place[0]))
     own_shape = (layers, bottle, columns)
     out_shapes = [
-        ((2, rows, columns), bf16),
         ((layers, 1, columns), f32),
         (own_shape, bf16),
         (own_shape, bf16),
         ((prod_rows, rows), f32),
         ((2 * inner * bottle, 2 * inner * bottle), f32),
     ]
-    piece_own, gain_own, low_own, high_own, prod, gram = pl.pallas_call(
+    gain_own, low_own, high_own, prod, gram = pl.pallas_call(
         functools.partial(
             products_kernel, layers, width, group if aligned else 0, members
         ),
         out_shape=[jax.ShapeDtypeStruct(s, d) for s, d in out_shapes],
-        grid_spec=pltpu.PrefetchScalarGridSpec(
-            num_scalar_prefetch=1,
-            grid=(1,),
-            in_specs=[whole_spec(v.shape) for v in acts] + [block, wide, wide] * sections,
-            out_specs=[whole_spec(s) for s, _ in out_shapes],
-            scratch_shapes=[
-                pltpu.VMEM((layers, bottle, share), bf16),
-                pltpu.VMEM((layers, bottle, share), bf16),
-                pltpu.VMEM((layers, bottle, share), bf16),
-                pltpu.VMEM((rows, share), bf16),
-                pltpu.VMEM((rows, share), bf16),
-            ],
-        ),
+        in_specs=[IN_SMEM] + [IN_VMEM] * (1 + 3 * sections),
+        out_specs=[IN_VMEM] * len(out_shapes),
+        scratch_shapes=[pltpu.VMEM((layers, bottle, share), bf16)] * 3,
         compiler_params=params,
         name="products",
-    )(place, *acts, *[w for ws in weights for w in ws])
+    )(place, both, *[w for ws in weights for w in ws])
     if not aligned:
         piece_own = piece(0)
         layer_of = [section ^ k for k in range(sections)]
@@ -422,13 +404,9 @@
     parcels = pl.pallas_call(
         functools.partial(grads_kernel, layers, bottle, width, group, members),
         out_shape=[jax.ShapeDtypeStruct(s, d) for s, d in sends],
-        grid_spec=pltpu.PrefetchScalarGridSpec(
-            num_scalar_prefetch=1,
-            grid=(1,),
-            in_specs=[whole_spec(v.shape) for v in operands],
-            out_specs=[whole_spec(s) for s, _ in sends],
-            scratch_shapes=[pltpu.VMEM((lines,) + message, bf16)],
-        ),
+        in_specs=[IN_SMEM] + [IN_VMEM] * len(operands),
+        out_specs=[IN_VMEM] * len(sends),
+        scratch_shapes=[pltpu.VMEM((lines,) + message, bf16)],
         compiler_params=params,
         name="grads",
     )(place, *operands)

time: 41.4 us -> 38.4 us (0.928)
  local copies, waits for them, and re-layouts: 4.47 us -> 0.67 us
  Pallas kernels: 5.09 us -> 5.96 us
    unnamed x14 -> x6, local copies, waits for them, and re-layouts: 3.81 us -> 0.01 us
    pallas_call x1, Pallas kernels: 0.97 us -> 1.91 us  [per_device(): pl.pallas_call(functools.partial(pack_kernel, width, group, members), out...]
  transfers between devices with their start and end apart: 15 -> 15, of which waited for: 7 -> 5; matrix products, arithmetic and copies ran while one was open for 0% -> 0% of each run, Pallas kernels for 9% -> 12%
where the time goes in v2:
time: 38.4 us; the launch traced here: 38.2 us
  starting transfers between devices  16.4 us (43%)
  waiting for transfers between devices  14.4 us (38%)
  Pallas kernels  5.96 us (16%)
  between operations  0.7 us (2%)
  local copies, waits for them, and re-layouts  0.67 us (2%)
    ppermute x11, starting transfers between devices, from_partner(): lax.ppermute(value, axis, [(i, i ^ flip) for i in range(lax.axis_size(axi...  10.4 us
    ppermute x11, waiting for transfers between devices, from_partner(): lax.ppermute(value, axis, [(i, i ^ flip) for i in range(lax.axis_size(axi...  7.9 us
    ppermute x4, waiting for transfers between devices, per_device(): total = total + lax.ppermute(parcels[r], BOTH, route).astype(f32)  6.5 us
    ppermute x4, starting transfers between devices, per_device(): total = total + lax.ppermute(parcels[r], BOTH, route).astype(f32)  6.01 us
    pallas_call x1, Pallas kernels, per_device(): pl.pallas_call(functools.partial(products_kernel, layers, width, group if...  2.21 us
    pallas_call x1, Pallas kernels, per_device(): pl.pallas_call(functools.partial(pack_kernel, width, group, members), out...  1.91 us
    pallas_call x1, Pallas kernels, per_device(): pl.pallas_call(functools.partial(grads_kernel, layers, bottle, width, gro...  1.45 us
  transfers between devices with their start and end apart: 15, of which 5 were waited for; matrix products, arithmetic and copies ran while one was open for 0% of the time, Pallas kernels for 12%

profile of v2, /device:TPU:0, one launch (start us, length us, event | category | flops | bytes accessed | tf_op | source)
XLA Modules:
  0.0 38.2 jit_solution(10232772167412121059)
XLA Ops:
  0.6 0.5 %collective-permute-start.1 = (bf16[1,64,4096]{2,1,0:T(8,128)(2,1)}, bf16[1,64,4096]{2,1,0:T(8,128)(2,1)S(1)}, u32[]{:S(2)}, u32[]{:S(2)}) collective-permute-start(bf16[1,64,4096]{2,1,0:T(8,128)(2,1)} %refs_2_.3), channel_id=1, source_target_pairs={{0,16},{16,0},{1,17},{17,1},{2,18},{18,2},{3,19},{19,3},{4,20},{20... | collective-permute-start | bytes 1572872 | tf_op jit(solution)/shard_map/ppermute | solution.py:18
  1.1 0.1 collective-permute-start.2
  1.2 0.1 pad_add_fusion.place
  1.3 1.9 %pack.1 = (bf16[2,128,2048]{2,1,0:T(8,128)(2,1)S(1)}, bf16[2,128,512]{2,1,0:T(8,128)(2,1)S(1)}, bf16[2,128,512]{2,1,0:T(8,128)(2,1)S(1)}, bf16[2,128,512]{2,1,0:T(8,128)(2,1)S(1)}, bf16[2,128,512]{2,1,0:T(8,128)(2,1)S(1)}) custom-call(s32[3]{0:T(128)S(1)} %pad_add_fusion.place, bf16[2,32,2048]{2,1,0:T(8,128)(2,1)} %refs_0_.1, bf16[2,32,2048]{2,1,0:T(8,128)(2,1)} %refs_1_.1, ...), custom_call_target="tpu_custom_call" | custom-call | tf_op jit(solution)/shard_map/pack/pallas_call | solution.py:324
  3.2 3.0 %collective-permute-start.8 = (bf16[2,128,512]{2,1,0:T(8,128)(2,1)S(1)}, bf16[2,128,512]{2,1,0:T(8,128)(2,1)S(1)}, u32[]{:S(2)}, u32[]{:S(2)}) collective-permute-start(bf16[2,128,512]{2,1,0:T(8,128)(2,1)S(1)} %get-tuple-element.20), channel_id=1, source_target_pairs={{0,1},{1,0},{2,3},{3,2},{4,5},{5,4},{6,7},{7,6},{8,9},{9,8},{10,11... | collective-permute-start | bytes 786440 | tf_op jit(solution)/shard_map/ppermute | solution.py:18
  6.2 1.5 %collective-permute-start.9 = (bf16[2,128,512]{2,1,0:T(8,128)(2,1)S(1)}, bf16[2,128,512]{2,1,0:T(8,128)(2,1)S(1)}, u32[]{:S(2)}, u32[]{:S(2)}) collective-permute-start(bf16[2,128,512]{2,1,0:T(8,128)(2,1)S(1)} %get-tuple-element.21), channel_id=1, source_target_pairs={{0,2},{1,3},{2,0},{3,1},{4,6},{5,7},{6,4},{7,5},{8,10},{9,11},{10,... | collective-permute-start | bytes 786440 | tf_op jit(solution)/shard_map/ppermute | solution.py:18
  7.7 1.1 %collective-permute-start.10 = (bf16[2,128,512]{2,1,0:T(8,128)(2,1)S(1)}, bf16[2,128,512]{2,1,0:T(8,128)(2,1)S(1)}, u32[]{:S(2)}, u32[]{:S(2)}) collective-permute-start(bf16[2,128,512]{2,1,0:T(8,128)(2,1)S(1)} %get-tuple-element.22), channel_id=1, source_target_pairs={{0,3},{1,2},{2,1},{3,0},{4,7},{5,6},{6,5},{7,4},{8,11},{9,10},{10,... | collective-permute-start | bytes 786440 | tf_op jit(solution)/shard_map/ppermute | solution.py:18
  8.9 2.2 %products.1 = (f32[2,1,512]{2,1,0:T(1,128)S(1)}, bf16[2,64,512]{2,1,0:T(8,128)(2,1)S(1)}, bf16[2,64,512]{2,1,0:T(8,128)(2,1)S(1)}, f32[328,128]{1,0:T(8,128)S(1)}, f32[128,128]{1,0:T(8,128)S(1)}) custom-call(s32[3]{0:T(128)S(1)} %pad_add_fusion.place, bf16[2,128,2048]{2,1,0:T(8,128)(2,1)S(1)} %get-tuple-element.16.refs_0_, bf16[1,1,4096]{2,1,0:T(2,128)(2,1)S(1)} %bitcast.5, ...), custom_call_target="tpu_custom_call" | custom-call | tf_op jit(solution)/shard_map/products/pallas_call | solution.py:350
  11.2 0.5 %collective-permute-start.4 = (f32[128,128]{1,0:T(8,128)S(1)}, f32[128,128]{1,0:T(8,128)S(1)}, u32[]{:S(2)}, u32[]{:S(2)}) collective-permute-start(f32[128,128]{1,0:T(8,128)S(1)} %get-tuple-element.18.refs_2_), channel_id=1, source_target_pairs={{0,16},{16,0},{1,17},{17,1},{2,18},{18,2},{3,19},{19,3},{4,20},{20... | collective-permute-start | bytes 196616 | tf_op jit(solution)/shard_map/ppermute | solution.py:18
  11.7 1.0 %collective-permute-done.4.refs_3_ = f32[128,128]{1,0:T(8,128)S(1)} collective-permute-done((f32[128,128]{1,0:T(8,128)S(1)}, f32[128,128]{1,0:T(8,128)S(1)}, u32[]{:S(2)}, u32[]{:S(2)}) %collective-permute-start.4) | collective-permute-done | bytes 65568 | tf_op jit(solution)/shard_map/ppermute | solution.py:18
  12.7 0.4 %relay.1.refs_0_ = bf16[272,128]{1,0:T(8,128)(2,1)S(1)} custom-call(f32[328,128]{1,0:T(8,128)S(1)} %get-tuple-element.17.refs_0_, f32[328,128]{1,0:T(8,128)S(1)} %collective-permute-done.3.refs_1_, f32[128,128]{1,0:T(8,128)S(1)} %get-tuple-element.18.refs_2_, f32[128,128]{1,0:T(8,128)S(1)} %collective-permute-done.4.refs_3_), custom_call_target="tpu_custom_call" | custom-call | tf_op jit(solution)/shard_map/relay/pallas_call | solution.py:388
  13.1 1.9 %collective-permute-start.7 = (bf16[272,128]{1,0:T(8,128)(2,1)S(1)}, bf16[272,128]{1,0:T(8,128)(2,1)S(1)}, u32[]{:S(2)}, u32[]{:S(2)}) collective-permute-start(bf16[272,128]{1,0:T(8,128)(2,1)S(1)} %relay.1.refs_0_), channel_id=1, source_target_pairs={{0,3},{1,2},{2,1},{3,0},{4,7},{5,6},{6,5},{7,4},{8,11},{9,10},{10,... | collective-permute-start | bytes 208904 | tf_op jit(solution)/shard_map/ppermute | solution.py:18
  14.9 1.2 %collective-permute-start.6 = (bf16[272,128]{1,0:T(8,128)(2,1)S(1)}, bf16[272,128]{1,0:T(8,128)(2,1)S(1)}, u32[]{:S(2)}, u32[]{:S(2)}) collective-permute-start(bf16[272,128]{1,0:T(8,128)(2,1)S(1)} %relay.1.refs_0_), channel_id=1, source_target_pairs={{0,2},{1,3},{2,0},{3,1},{4,6},{5,7},{6,4},{7,5},{8,10},{9,11},{10,... | collective-permute-start | bytes 208904 | tf_op jit(solution)/shard_map/ppermute | solution.py:18
  16.1 0.5 %collective-permute-start.5 = (bf16[272,128]{1,0:T(8,128)(2,1)S(1)}, bf16[272,128]{1,0:T(8,128)(2,1)S(1)}, u32[]{:S(2)}, u32[]{:S(2)}) collective-permute-start(bf16[272,128]{1,0:T(8,128)(2,1)S(1)} %relay.1.refs_0_), channel_id=1, source_target_pairs={{0,1},{1,0},{2,3},{3,2},{4,5},{5,4},{6,7},{7,6},{8,9},{9,8},{10,11... | collective-permute-start | bytes 208904 | tf_op jit(solution)/shard_map/ppermute | solution.py:18
  16.6 5.8 %collective-permute-done.9.refs_6_ = bf16[2,128,512]{2,1,0:T(8,128)(2,1)S(1)} collective-permute-done((bf16[2,128,512]{2,1,0:T(8,128)(2,1)S(1)}, bf16[2,128,512]{2,1,0:T(8,128)(2,1)S(1)}, u32[]{:S(2)}, u32[]{:S(2)}) %collective-permute-start.9) | collective-permute-done | bytes 262176 | tf_op jit(solution)/shard_map/ppermute | solution.py:18
  22.4 1.1 %collective-permute-done.6.refs_2_ = bf16[272,128]{1,0:T(8,128)(2,1)S(1)} collective-permute-done((bf16[272,128]{1,0:T(8,128)(2,1)S(1)}, bf16[272,128]{1,0:T(8,128)(2,1)S(1)}, u32[]{:S(2)}, u32[]{:S(2)}) %collective-permute-start.6) | collective-permute-done | bytes 69664 | tf_op jit(solution)/shard_map/ppermute | solution.py:18
  23.5 1.4 %grads.1 = (bf16[2,64,256]{2,1,0:T(8,128)(2,1)S(1)}, bf16[2,64,256]{2,1,0:T(8,128)(2,1)S(1)}, bf16[2,64,256]{2,1,0:T(8,128)(2,1)S(1)}, bf16[2,64,256]{2,1,0:T(8,128)(2,1)S(1)}) custom-call(s32[3]{0:T(128)S(1)} %pad_add_fusion.place, bf16[272,128]{1,0:T(8,128)(2,1)S(1)} %relay.1.refs_0_, bf16[272,128]{1,0:T(8,128)(2,1)S(1)} %collective-permute-done.5.refs_1_, ...), custom_call_target="tpu_custom_call" | custom-call | tf_op jit(solution)/shard_map/grads/pallas_call | solution.py:404
  25.0 0.7 %collective-permute-start.11 = (bf16[2,64,256]{2,1,0:T(8,128)(2,1)S(1)}, bf16[2,64,256]{2,1,0:T(8,128)(2,1)S(1)}, u32[]{:S(2)}, u32[]{:S(2)}) collective-permute-start(bf16[2,64,256]{2,1,0:T(8,128)(2,1)S(1)} %get-tuple-element.26), channel_id=1, source_target_pairs={{0,0},{1,1},{2,2},{3,3},{4,4},{5,5},{6,6},{7,7},{8,16},{9,17},{10,... | collective-permute-start | bytes 196616 | tf_op jit(solution)/shard_map/ppermute | solution.py:430
  25.7 1.6 %collective-permute-start.12 = (bf16[2,64,256]{2,1,0:T(8,128)(2,1)S(1)}, bf16[2,64,256]{2,1,0:T(8,128)(2,1)S(1)}, u32[]{:S(2)}, u32[]{:S(2)}) collective-permute-start(bf16[2,64,256]{2,1,0:T(8,128)(2,1)S(1)} %get-tuple-element.27), channel_id=1, source_target_pairs={{0,4},{1,5},{2,6},{3,7},{4,0},{5,1},{6,2},{7,3},{8,20},{9,21},{10,... | collective-permute-start | bytes 196616 | tf_op jit(solution)/shard_map/ppermute | solution.py:430
  27.3 3.4 %collective-permute-start.13 = (bf16[2,64,256]{2,1,0:T(8,128)(2,1)S(1)}, bf16[2,64,256]{2,1,0:T(8,128)(2,1)S(1)}, u32[]{:S(2)}, u32[]{:S(2)}) collective-permute-start(bf16[2,64,256]{2,1,0:T(8,128)(2,1)S(1)} %get-tuple-element.28), channel_id=1, source_target_pairs={{0,16},{1,17},{2,18},{3,19},{4,20},{5,21},{6,22},{7,23},{8,0},{9,1... | collective-permute-start | bytes 196616 | tf_op jit(solution)/shard_map/ppermute | solution.py:430
  30.7 0.3 collective-permute-start.14
  31.0 5.0 %collective-permute-done.13 = bf16[2,64,256]{2,1,0:T(8,128)(2,1)S(1)} collective-permute-done((bf16[2,64,256]{2,1,0:T(8,128)(2,1)S(1)}, bf16[2,64,256]{2,1,0:T(8,128)(2,1)S(1)}, u32[]{:S(2)}, u32[]{:S(2)}) %collective-permute-start.13) | collective-permute-done | bytes 65568 | tf_op jit(solution)/shard_map/ppermute | solution.py:430
  36.0 1.5 %collective-permute-done.14 = bf16[2,64,256]{2,1,0:T(8,128)(2,1)S(1)} collective-permute-done((bf16[2,64,256]{2,1,0:T(8,128)(2,1)S(1)}, bf16[2,64,256]{2,1,0:T(8,128)(2,1)S(1)}, u32[]{:S(2)}, u32[]{:S(2)}) %collective-permute-start.14) | collective-permute-done | bytes 65568 | tf_op jit(solution)/shard_map/ppermute | solution.py:430
  37.5 0.7 %fusion = (f32[1,64,256]{2,1,0:T(8,128)}, f32[1,64,256]{2,1,0:T(8,128)}) fusion(f32[2,64,256]{2,1,0:T(8,128)S(1)} %convert_add_fusion), kind=kLoop, calls=%fused_computation.2 | loop fusion | bytes 262144 | tf_op jit(solution)/shard_map/slice | solution.py:431
  (19 shorter events, 0.1 us)
Async XLA Ops:
  0.6 8.3 %collective-permute-start.1 = (bf16[1,64,4096]{2,1,0:T(8,128)(2,1)}, bf16[1,64,4096]{2,1,0:T(8,128)(2,1)S(1)}, u32[]{:S(2)}, u32[]{:S(2)}) collective-permute-start(bf16[1,64,4096]{2,1,0:T(8,128)(2,1)} %refs_2_.3), channel_id=1, source_target_pairs={{0,16},{16,0},{1,17},{17,1},{2,18},{18,2},{3,19},{19,3},{4,20},{20... | collective-permute-start | bytes 1572872 | tf_op jit(solution)/shard_map/ppermute | solution.py:18
  1.1 7.7 %collective-permute-start.2 = (bf16[1,64,4096]{2,1,0:T(8,128)(2,1)}, bf16[1,64,4096]{2,1,0:T(8,128)(2,1)S(1)}, u32[]{:S(2)}, u32[]{:S(2)}) collective-permute-start(bf16[1,64,4096]{2,1,0:T(8,128)(2,1)} %refs_3_.3), channel_id=1, source_target_pairs={{0,16},{16,0},{1,17},{17,1},{2,18},{18,2},{3,19},{19,3},{4,20},{20... | collective-permute-start | bytes 1572872 | tf_op jit(solution)/shard_map/ppermute | solution.py:18
  1.2 5.0 %copy-start.2 = (bf16[1,4096]{1,0:T(2,128)(2,1)S(1)}, bf16[1,4096]{1,0:T(2,128)(2,1)}, u32[]{:S(2)}) copy-start(bf16[1,4096]{1,0:T(2,128)(2,1)} %param.11) | copy-start | bytes 24580
  1.3 7.6 %copy-start = (bf16[1,64,4096]{2,1,0:T(8,128)(2,1)S(1)}, bf16[1,64,4096]{2,1,0:T(8,128)(2,1)}, u32[]{:S(2)}) copy-start(bf16[1,64,4096]{2,1,0:T(8,128)(2,1)} %refs_2_.3) | copy-start | bytes 1572868
  1.3 7.6 %copy-start.1 = (bf16[1,64,4096]{2,1,0:T(8,128)(2,1)S(1)}, bf16[1,64,4096]{2,1,0:T(8,128)(2,1)}, u32[]{:S(2)}) copy-start(bf16[1,64,4096]{2,1,0:T(8,128)(2,1)} %refs_3_.3) | copy-start | bytes 1572868
  3.2 12.9 %collective-permute-start.8 = (bf16[2,128,512]{2,1,0:T(8,128)(2,1)S(1)}, bf16[2,128,512]{2,1,0:T(8,128)(2,1)S(1)}, u32[]{:S(2)}, u32[]{:S(2)}) collective-permute-start(bf16[2,128,512]{2,1,0:T(8,128)(2,1)S(1)} %get-tuple-element.20), channel_id=1, source_target_pairs={{0,1},{1,0},{2,3},{3,2},{4,5},{5,4},{6,7},{7,6},{8,9},{9,8},{10,11... | collective-permute-start | bytes 786440 | tf_op jit(solution)/shard_map/ppermute | solution.py:18
  6.2 1.5 %collective-permute-start = (bf16[1,1,4096]{2,1,0:T(2,128)(2,1)S(1)}, bf16[1,1,4096]{2,1,0:T(2,128)(2,1)S(1)}, u32[]{:S(2)}, u32[]{:S(2)}) collective-permute-start(bf16[1,1,4096]{2,1,0:T(2,128)(2,1)S(1)} %bitcast.4), channel_id=1, source_target_pairs={{0,16},{16,0},{1,17},{17,1},{2,18},{18,2},{3,19},{19,3},{4,20},{20... | collective-permute-start | bytes 24584 | tf_op jit(solution)/shard_map/ppermute | solution.py:18
  6.2 16.2 %collective-permute-start.9 = (bf16[2,128,512]{2,1,0:T(8,128)(2,1)S(1)}, bf16[2,128,512]{2,1,0:T(8,128)(2,1)S(1)}, u32[]{:S(2)}, u32[]{:S(2)}) collective-permute-start(bf16[2,128,512]{2,1,0:T(8,128)(2,1)S(1)} %get-tuple-element.21), channel_id=1, source_target_pairs={{0,2},{1,3},{2,0},{3,1},{4,6},{5,7},{6,4},{7,5},{8,10},{9,11},{10,... | collective-permute-start | bytes 786440 | tf_op jit(solution)/shard_map/ppermute | solution.py:18
  7.7 14.7 %collective-permute-start.10 = (bf16[2,128,512]{2,1,0:T(8,128)(2,1)S(1)}, bf16[2,128,512]{2,1,0:T(8,128)(2,1)S(1)}, u32[]{:S(2)}, u32[]{:S(2)}) collective-permute-start(bf16[2,128,512]{2,1,0:T(8,128)(2,1)S(1)} %get-tuple-element.22), channel_id=1, source_target_pairs={{0,3},{1,2},{2,1},{3,0},{4,7},{5,6},{6,5},{7,4},{8,11},{9,10},{10,... | collective-permute-start | bytes 786440 | tf_op jit(solution)/shard_map/ppermute | solution.py:18
  11.1 1.5 %collective-permute-start.3 = (f32[328,128]{1,0:T(8,128)S(1)}, f32[328,128]{1,0:T(8,128)S(1)}, u32[]{:S(2)}, u32[]{:S(2)}) collective-permute-start(f32[328,128]{1,0:T(8,128)S(1)} %get-tuple-element.17.refs_0_), channel_id=1, source_target_pairs={{0,16},{16,0},{1,17},{17,1},{2,18},{18,2},{3,19},{19,3},{4,20},{20... | collective-permute-start | bytes 503816 | tf_op jit(solution)/shard_map/ppermute | solution.py:18
  11.2 1.5 %collective-permute-start.4 = (f32[128,128]{1,0:T(8,128)S(1)}, f32[128,128]{1,0:T(8,128)S(1)}, u32[]{:S(2)}, u32[]{:S(2)}) collective-permute-start(f32[128,128]{1,0:T(8,128)S(1)} %get-tuple-element.18.refs_2_), channel_id=1, source_target_pairs={{0,16},{16,0},{1,17},{17,1},{2,18},{18,2},{3,19},{19,3},{4,20},{20... | collective-permute-start | bytes 196616 | tf_op jit(solution)/shard_map/ppermute | solution.py:18
  13.1 9.4 %collective-permute-start.7 = (bf16[272,128]{1,0:T(8,128)(2,1)S(1)}, bf16[272,128]{1,0:T(8,128)(2,1)S(1)}, u32[]{:S(2)}, u32[]{:S(2)}) collective-permute-start(bf16[272,128]{1,0:T(8,128)(2,1)S(1)} %relay.1.refs_0_), channel_id=1, source_target_pairs={{0,3},{1,2},{2,1},{3,0},{4,7},{5,6},{6,5},{7,4},{8,11},{9,10},{10,... | collective-permute-start | bytes 208904 | tf_op jit(solution)/shard_map/ppermute | solution.py:18
  14.9 8.6 %collective-permute-start.6 = (bf16[272,128]{1,0:T(8,128)(2,1)S(1)}, bf16[272,128]{1,0:T(8,128)(2,1)S(1)}, u32[]{:S(2)}, u32[]{:S(2)}) collective-permute-start(bf16[272,128]{1,0:T(8,128)(2,1)S(1)} %relay.1.refs_0_), channel_id=1, source_target_pairs={{0,2},{1,3},{2,0},{3,1},{4,6},{5,7},{6,4},{7,5},{8,10},{9,11},{10,... | collective-permute-start | bytes 208904 | tf_op jit(solution)/shard_map/ppermute | solution.py:18
  16.1 7.4 %collective-permute-start.5 = (bf16[272,128]{1,0:T(8,128)(2,1)S(1)}, bf16[272,128]{1,0:T(8,128)(2,1)S(1)}, u32[]{:S(2)}, u32[]{:S(2)}) collective-permute-start(bf16[272,128]{1,0:T(8,128)(2,1)S(1)} %relay.1.refs_0_), channel_id=1, source_target_pairs={{0,1},{1,0},{2,3},{3,2},{4,5},{5,4},{6,7},{7,6},{8,9},{9,8},{10,11... | collective-permute-start | bytes 208904 | tf_op jit(solution)/shard_map/ppermute | solution.py:18
  25.0 6.0 %collective-permute-start.11 = (bf16[2,64,256]{2,1,0:T(8,128)(2,1)S(1)}, bf16[2,64,256]{2,1,0:T(8,128)(2,1)S(1)}, u32[]{:S(2)}, u32[]{:S(2)}) collective-permute-start(bf16[2,64,256]{2,1,0:T(8,128)(2,1)S(1)} %get-tuple-element.26), channel_id=1, source_target_pairs={{0,0},{1,1},{2,2},{3,3},{4,4},{5,5},{6,6},{7,7},{8,16},{9,17},{10,... | collective-permute-start | bytes 196616 | tf_op jit(solution)/shard_map/ppermute | solution.py:430
  25.7 5.3 %collective-permute-start.12 = (bf16[2,64,256]{2,1,0:T(8,128)(2,1)S(1)}, bf16[2,64,256]{2,1,0:T(8,128)(2,1)S(1)}, u32[]{:S(2)}, u32[]{:S(2)}) collective-permute-start(bf16[2,64,256]{2,1,0:T(8,128)(2,1)S(1)} %get-tuple-element.27), channel_id=1, source_target_pairs={{0,4},{1,5},{2,6},{3,7},{4,0},{5,1},{6,2},{7,3},{8,20},{9,21},{10,... | collective-permute-start | bytes 196616 | tf_op jit(solution)/shard_map/ppermute | solution.py:430
  27.3 8.7 %collective-permute-start.13 = (bf16[2,64,256]{2,1,0:T(8,128)(2,1)S(1)}, bf16[2,64,256]{2,1,0:T(8,128)(2,1)S(1)}, u32[]{:S(2)}, u32[]{:S(2)}) collective-permute-start(bf16[2,64,256]{2,1,0:T(8,128)(2,1)S(1)} %get-tuple-element.28), channel_id=1, source_target_pairs={{0,16},{1,17},{2,18},{3,19},{4,20},{5,21},{6,22},{7,23},{8,0},{9,1... | collective-permute-start | bytes 196616 | tf_op jit(solution)/shard_map/ppermute | solution.py:430
  30.7 6.8 %collective-permute-start.14 = (bf16[2,64,256]{2,1,0:T(8,128)(2,1)S(1)}, bf16[2,64,256]{2,1,0:T(8,128)(2,1)S(1)}, u32[]{:S(2)}, u32[]{:S(2)}) collective-permute-start(bf16[2,64,256]{2,1,0:T(8,128)(2,1)S(1)} %get-tuple-element.29), channel_id=1, source_target_pairs={{0,20},{1,21},{2,22},{3,23},{4,16},{5,17},{6,18},{7,19},{8,4},{9,5... | collective-permute-start | bytes 196616 | tf_op jit(solution)/shard_map/ppermute | solution.py:430

commit v3 on v2

v3 whole, which is shorter than its diff:
```python
import functools

import jax
import jax.numpy as jnp
from jax import lax
from jax.experimental import pallas as pl
from jax.experimental.pallas import tpu as pltpu
from jax.sharding import PartitionSpec as P

epsilon = 1e-05
VMEM_BYTES = 32 * 1024 * 1024
MEMBERS = 4
STAR = True
TWIST = 0
COST_PRODUCTS = 12
COST_SMALL = 0.1
f32 = jnp.float32
bf16 = jnp.bfloat16
IN_VMEM = pl.BlockSpec(memory_space=pltpu.VMEM)
IN_HBM = pl.BlockSpec(memory_space=pltpu.HBM)


def cost(micros):
    return pl.CostEstimate(flops=int(micros * 1.1e9), bytes_accessed=0, transcendentals=0)


def from_partner(value, axis, flip):
    return lax.ppermute(value, axis, [(i, i ^ flip) for i in range(lax.axis_size(axis))])


def dot_nn(left, right):
    return lax.dot_general(left, right, (((1,), (0,)), ((), ())), preferred_element_type=f32)


def dot_nt(left, right):
    return lax.dot_general(left, right, (((1,), (1,)), ((), ())), preferred_element_type=f32)


def split(value):
    high = value.astype(bf16)
    return high, (value - high.astype(f32)).astype(bf16)


def dot_split(left, right):
    high, low = split(left)
    return dot_nn(high, right) + dot_nn(low, right)


LEADERS = (0, 1, 2, 4) if STAR else (0, 1, 2, 3)


def leader(label):
    return label + (label == 3) if STAR else label


def mask(slot, group, chunks):
    section, part = divmod(slot, group)
    low = (part & 1) * 7 + (part >> 1) * 8 if STAR else part * 4
    return section * chunks ^ (section & 1) * TWIST ^ low


def label_slot(replica, group, chunks):
    section = replica // chunks
    local = replica % chunks ^ (section & 1) * TWIST
    if not STAR:
        return local % 4, section * group + local // 4
    low = local & 7
    label = (low & 3) ^ (low >> 2) * 3
    odd = (low != 0) & (low != 1) & (low != 2) & (low != 4)
    return label, section * group + (local >> 3) * 2 + odd.astype(jnp.int32)


def whereabouts(group, chunks):
    section = lax.axis_index("section")
    label, slot = label_slot(lax.axis_index("dp"), group, chunks)
    return section, label, slot


def chunk_of(label, part, section):
    low = (part & 1) * 7 + (part >> 1) * 8 if STAR else part * 4
    return leader(label) ^ low ^ (section & 1) * TWIST


def pack_kernel(width, group, chunks, *refs):
    acts = refs[:4]
    both = refs[4]
    outs = refs[5:-1]
    sems = refs[-1]
    micro, tokens = acts[0].shape[0], acts[0].shape[1]
    section, label, _ = whereabouts(group, chunks)
    copies = []
    for a, act in enumerate(acts):
        for m in range(micro):
            start = ((a % 2) * micro + m) * tokens
            copies.append(
                pltpu.make_async_copy(
                    act.at[m], both.at[a // 2, pl.ds(start, tokens)], sems.at[len(copies)]
                )
            )
            copies[-1].start()
    for n, copy in enumerate(copies):
        copy.wait()
        a, m = divmod(n, micro)
        start = ((a % 2) * micro + m) * tokens
        for k, out in enumerate(outs):
            for part in range(group):
                chunk = chunk_of(label ^ k, part, section)
                span = pl.ds(pl.multiple_of(chunk * width, width), width)
                out[a // 2, start : start + tokens, part * width : (part + 1) * width] = both[
                    a // 2, start : start + tokens, span
                ]


def two_parts(refs):
    if len(refs) == 2:
        return refs
    height, side = refs[0].shape
    return refs[0].at[: height - side], refs[0].at[height - side :]


def products_kernel(layers, *refs):
    acts = refs[0]
    weights = [refs[1 + 3 * k : 4 + 3 * k] for k in range(layers)]
    outs = refs[1 + 3 * layers : -3]
    prod_out, gram_out = two_parts(outs)
    low_scr, fine_scr, high_scr = refs[-3:]
    bottle = weights[0][1].shape[1]
    features = acts.shape[2]
    section = lax.axis_index("section")
    mine = pl.ds(pl.multiple_of(section * features, features), features)
    for k in range(layers):
        gain, down, up = weights[k]
        layer = section ^ k
        exact = gain[0, :, mine].astype(f32) * down[0, :, mine].astype(f32)
        low, fine = split(exact)
        low_scr[layer] = low
        fine_scr[layer] = fine
        high_scr[layer] = up[0, :, mine]
    hidden = acts[0]
    low_all = low_scr[...].reshape(layers * bottle, features)
    fine_all = fine_scr[...].reshape(layers * bottle, features)
    high_all = high_scr[...].reshape(layers * bottle, features)
    size = (layers - 1) * bottle
    at = layers * bottle
    prod_out[:at] = dot_nt(low_all, hidden) + dot_nt(fine_all, hidden)
    if layers > 1:
        prod_out[at : at + size] = dot_nt(high_all[:size], hidden)
    at += size
    prod_out[at : at + layers * bottle] = dot_nt(high_all, acts[1])
    at += layers * bottle
    square = dot_nt(hidden, hidden)
    eye = lax.broadcasted_iota(jnp.int32, square.shape, 0) == lax.broadcasted_iota(
        jnp.int32, square.shape, 1
    )
    norms = jnp.sum(jnp.where(eye, square, 0.0), axis=0, keepdims=True)
    prod_out[at : at + 8] = jnp.broadcast_to(norms, (8, norms.shape[1]))
    if layers > 1:
        high_part = high_all[:size]
        low_part = low_all[bottle:]
        fine_part = fine_all[bottle:]
        gram_out[:size, :size] = jnp.zeros((size, size), f32)
        gram_out[:size, size:] = dot_nt(low_part, high_part) + dot_nt(fine_part, high_part)
        gram_out[size:, :size] = dot_nt(high_part, low_part) + dot_nt(high_part, fine_part)
        gram_out[size:, size:] = dot_nt(high_part, high_part)
    else:
        gram_out[...] = jnp.zeros_like(gram_out)


def relay_kernel(layers, bottle, features, sections, *refs):
    coef_out, hold = refs[-2:]
    each = (len(refs) - 2) // sections
    prods, grams = zip(
        *(two_parts(refs[each * k : each * (k + 1)]) for k in range(sections)), strict=True
    )
    section = lax.axis_index("section")
    prod = sum((ref[...] for ref in prods[1:]), prods[0][...])
    gram = sum((ref[...] for ref in grams[1:]), grams[0][...])
    K = bottle
    inner = layers - 1
    h_low = [prod[l * K : (l + 1) * K] for l in range(layers)]
    at = layers * K
    h_high = [prod[at + l * K : at + (l + 1) * K] for l in range(inner)]
    at += inner * K
    u_high = [prod[at + l * K : at + (l + 1) * K] for l in range(layers)]
    at += layers * K
    norm = prod[at : at + 1]

    def low_high(l, m):
        return gram[(l - 1) * K : l * K, (inner + m) * K : (inner + m + 1) * K]

    def high_low(m, l):
        return gram[(inner + m) * K : (inner + m + 1) * K, (l - 1) * K : l * K]

    def high_high(m, n):
        return gram[
            (inner + m) * K : (inner + m + 1) * K, (inner + n) * K : (inner + n + 1) * K
        ]

    inverses, bottles, hidden_high = [], [], []
    for l in range(layers):
        inverse = lax.rsqrt(jnp.maximum(norm, 0.0) * (1.0 / features) + epsilon)
        value = h_low[l] * inverse
        active = (value * jax.nn.sigmoid(value)).astype(bf16)
        inverses.append(inverse)
        bottles.append(value)
        hold[l] = active
        hidden_high.append(list(h_high))
        if l < inner:
            before = h_high[l]
            h_high = [h_high[n] + dot_split(high_high(n, l), active) for n in range(inner)]
            for n in range(l + 1, layers):
                h_low[n] = h_low[n] + dot_split(low_high(n, l), active)
            norm = norm + jnp.sum(
                active.astype(f32) * (before + h_high[l]), axis=0, keepdims=True
            )
    pulls = [None] * layers
    for l in range(layers - 1, -1, -1):
        sigma = jax.nn.sigmoid(bottles[l])
        coarse = (u_high[l] * sigma * (1.0 + bottles[l] * (1.0 - sigma))).astype(bf16)
        hold[layers + l] = coarse
        if l == 0:
            break
        grad = coarse.astype(f32)
        scaled, fine = split(grad * inverses[l])
        pull = (
            inverses[l]
            * inverses[l]
            * jnp.sum(grad * bottles[l], axis=0, keepdims=True)
            * (1.0 / features)
        )
        pulls[l] = pull
        for n in range(l):
            u_high[n] = (
                u_high[n]
                + dot_split(high_low(n, l), scaled)
                + dot_nn(high_low(n, l).astype(bf16), fine)
                - pull * hidden_high[l][n]
            )
    blocks = [hold[layers + section], hold[section]]
    for i in range(inner):
        other = i + jnp.where(section <= i, 1, 0)
        blocks.append(hold[jnp.where(section <= i, layers + other, other)])
    blocks += [hold[n] for n in range(1, inner)]
    for n, block in enumerate(blocks):
        coef_out[n * K : (n + 1) * K] = block

    def inverse_at(layer):
        value = inverses[0]
        for l in range(1, layers):
            value = jnp.where(layer == l, inverses[l], value)
        return value

    lines = [line.astype(bf16).astype(f32) for line in pulls[1:]]
    scales = [inverse_at(section)]
    scales += [inverse_at(i + jnp.where(section <= i, 1, 0)) for i in range(inner)]
    for scale in scales:
        lines.extend(part.astype(f32) for part in split(scale))
    tail = coef_out.shape[0] - len(blocks) * K
    lines += [jnp.zeros_like(norm)] * (tail - len(lines))
    coef_out[len(blocks) * K :] = jnp.concatenate(lines, axis=0).astype(bf16)


def cut_kernel(layers, width, group, chunks, *refs):
    weights = [refs[3 * k : 3 * k + 3] for k in range(layers)]
    gain_out, both_out = refs[3 * layers :]
    here_section, label, _ = whereabouts(group, chunks)
    for k in range(layers):
        section = here_section ^ k
        for part in range(group):
            chunk = section * chunks + chunk_of(label, part, section)
            span = pl.ds(pl.multiple_of(chunk * width, width), width)
            here = slice(part * width, (part + 1) * width)
            gain_out[k, :, here] = weights[0][0][0, :, span].astype(f32)
            for w in range(layers):
                gain, down, up = weights[w]
                layer = here_section ^ w
                low = gain[0, :, span].astype(f32) * down[0, :, span].astype(f32)
                both_out[k, layer, :, here] = low.astype(bf16)
                both_out[k, layers + layer, :, here] = up[0, :, span]


def stack_kernel(*refs):
    for k, ref in enumerate(refs[:-1]):
        refs[-1][k] = ref[...]


def grads_kernel(layers, bottle, width, group, chunks, *refs):
    K = bottle
    inner = layers - 1
    coefs = refs[:MEMBERS]
    pieces = refs[MEMBERS : MEMBERS + layers]
    gain, both = refs[MEMBERS + layers : MEMBERS + layers + 2]
    outs = refs[MEMBERS + layers + 2 : -1]
    parcel = refs[-1]
    section, _, own_slot = whereabouts(group, chunks)
    above = [section <= i for i in range(inner)]
    other_of = [i + jnp.where(above[i], 1, 0) for i in range(inner)]
    by_hidden = [0.0] * layers
    by_close = [0.0] * layers
    cross = [0.0] * inner
    drag = [0.0] * inner
    for m in range(MEMBERS):
        coef = coefs[m][...]
        grad, active = coef[:K], coef[K : 2 * K]
        others = [coef[(2 + i) * K : (3 + i) * K] for i in range(inner)]
        extras = [coef[(1 + layers + i) * K : (2 + layers + i) * K] for i in range(inner - 1)]
        at = (2 + inner + max(inner - 1, 0)) * K
        lines = coef[at:].astype(f32)
        active_f = active.astype(f32)

        def scale(i):
            row = inner + 2 * i
            return lines[row : row + 1] + lines[row + 1 : row + 2]

        def weight(n):
            total = jnp.zeros_like(lines[:1])
            for l in range(n + 1, layers):
                total = total + jnp.where(section < l, lines[l - 1 : l], 0.0)
            return total

        coarse, fine = split(grad.astype(f32) * scale(0))
        full = jnp.zeros_like(lines[:1])
        for l in range(1, layers):
            full = full + jnp.where(section < l, lines[l - 1 : l], 0.0)
        pulled = (-full * active_f).astype(bf16)
        left = jnp.concatenate([coarse, fine, pulled], axis=0)
        for k in range(layers):
            by_hidden[k] = by_hidden[k] + dot_nn(left, pieces[k][m, 0])
            by_close[k] = by_close[k] + dot_nn(active, pieces[k][m, 1])
        for i in range(inner):
            factor = jnp.where(above[i], scale(1 + i), 1.0)
            other = (others[i].astype(f32) * factor).astype(bf16)
            mate = jnp.where(above[i], active_f, coarse.astype(f32)).astype(bf16)
            cross[i] = cross[i] + dot_nt(mate, other)
        for n in range(inner):
            held = others[n]
            if n >= 1:
                held = jnp.where(section < n, extras[n - 1].astype(f32), held.astype(f32))
            held = jnp.where(section == n, active_f, held.astype(f32)).astype(bf16)
            drag[n] = drag[n] + dot_nt((-weight(n) * active_f).astype(bf16), held)
    for k in range(layers):
        down = by_hidden[k][:K] + by_hidden[k][K : 2 * K]
        up = by_close[k] + by_hidden[k][2 * K :]
        for i in range(inner):
            index = jnp.where(above[i], other_of[i], layers + other_of[i])
            term = dot_nn(cross[i].astype(bf16), both[k, index])
            up = up + jnp.where(above[i], term, 0.0)
            down = down + jnp.where(above[i], 0.0, term)
            up = up + dot_nn(drag[i].astype(bf16), both[k, layers + i])
        down = down * gain[k]
        for part in range(group):
            here = slice(part * width, (part + 1) * width)
            slot = (section ^ k) * group + part
            parcel[slot, 0] = down[:, here]
            parcel[slot, 1] = up[:, here]
    if len(outs) == 1:
        outs[0][...] = parcel[...]
    else:
        for r, out in enumerate(outs):
            out[...] = parcel[own_slot ^ r].astype(out.dtype)


def per_device(inputs_down, inputs_up, cotan_down, cotan_up, norm_gains, adapt_down, adapt_up):
    sections = lax.axis_size("section")
    replicas = lax.axis_size("dp")
    section = lax.axis_index("section")
    replica = lax.axis_index("dp")
    layers = sections
    chunks = replicas // sections
    group = chunks // MEMBERS
    slots = replicas // MEMBERS
    bottle = adapt_down.shape[1]
    features = adapt_down.shape[2]
    share = features // sections
    width = features // replicas
    columns = group * width
    label, slot = label_slot(replica, group, chunks)
    micro, tokens = inputs_down.shape[0], inputs_down.shape[1]
    half = micro * tokens
    rows = 2 * half
    inner = layers - 1
    aligned = width % 128 == 0
    params = pltpu.CompilerParams(vmem_limit_bytes=VMEM_BYTES)

    own = (norm_gains[:, None, :], adapt_down, adapt_up)
    weights = [own]
    for k in range(1, sections):
        weights.append(tuple(from_partner(w, "section", k) for w in own))
    flat = [w for ws in weights for w in ws]

    acts = (inputs_down, inputs_up, cotan_down, cotan_up)
    if aligned:
        both, *packed = pl.pallas_call(
            functools.partial(pack_kernel, width, group, chunks),
            out_shape=[pltpu.VMEM((2, rows, share), bf16)]
            + [pltpu.VMEM((2, rows, columns), bf16)] * MEMBERS,
            in_specs=[IN_HBM] * 4,
            out_specs=[IN_VMEM] * (1 + MEMBERS),
            scratch_shapes=[pltpu.SemaphoreType.DMA((4 * micro,))],
            compiler_params=params,
            name="pack",
        )(*[pltpu.with_memory_space_constraint(v, pltpu.HBM) for v in acts])
    else:
        both = jnp.concatenate([v.reshape(half, share) for v in acts], axis=0)
        both = both.reshape(2, rows, share)
        parts = both.reshape(2, rows, chunks, width)
        packed = []
        for k in range(MEMBERS):
            cuts = [
                lax.dynamic_index_in_dim(
                    parts, chunk_of(label ^ k, part, section), 2, keepdims=False
                )
                for part in range(group)
            ]
            packed.append(jnp.concatenate(cuts, axis=2))
    pieces = [packed[0]]
    for k in range(1, MEMBERS):
        pieces.append(from_partner(packed[k], "dp", LEADERS[k]))
    prod_rows = (3 * layers - 1) * bottle + 8
    gram_side = 2 * max(inner, 1) * bottle
    sides = [(prod_rows, rows), (gram_side, gram_side)]
    if rows == gram_side:
        sides = [(prod_rows + gram_side, rows)]
    sums = pl.pallas_call(
        functools.partial(products_kernel, layers),
        out_shape=[jax.ShapeDtypeStruct(side, f32) for side in sides],
        in_specs=[IN_VMEM] * (1 + 3 * sections),
        out_specs=[IN_VMEM] * len(sides),
        scratch_shapes=[pltpu.VMEM((layers, bottle, share), bf16)] * 3,
        compiler_params=params,
        cost_estimate=cost(COST_PRODUCTS),
        name="products",
    )(both, *flat)
    sums = list(sums)
    for k in range(1, sections):
        sums += [from_partner(v, "section", k) for v in sums[: len(sides)]]

    tail = inner + 2 * layers
    coef_rows = (2 + inner + max(inner - 1, 0)) * bottle + -(-tail // 16) * 16
    coef = pl.pallas_call(
        functools.partial(relay_kernel, layers, bottle, features, sections),
        out_shape=jax.ShapeDtypeStruct((coef_rows, rows), bf16),
        in_specs=[IN_VMEM] * len(sums),
        out_specs=IN_VMEM,
        scratch_shapes=[pltpu.VMEM((2 * layers, bottle, rows), bf16)],
        compiler_params=params,
        cost_estimate=cost(COST_SMALL),
        name="relay",
    )(*sums)
    coefs = [coef] + [from_partner(coef, "dp", LEADERS[k]) for k in range(1, MEMBERS)]
    cut_shapes = [
        jax.ShapeDtypeStruct((layers, 1, columns), f32),
        jax.ShapeDtypeStruct((layers, 2 * layers, bottle, columns), bf16),
    ]
    if aligned:
        gain_cut, both_cut = pl.pallas_call(
            functools.partial(cut_kernel, layers, width, group, chunks),
            out_shape=cut_shapes,
            in_specs=[IN_VMEM] * len(flat),
            out_specs=[IN_VMEM] * 2,
            compiler_params=params,
            cost_estimate=cost(COST_SMALL),
            name="cut",
        )(*flat)
    else:
        gain_cut = jnp.zeros(cut_shapes[0].shape, f32)
        both_cut = jnp.zeros(cut_shapes[1].shape, bf16)
        for k in range(layers):
            for part in range(group):
                at = section ^ k
                chunk = at * chunks + chunk_of(label, part, at)
                for w, ws in enumerate(weights):
                    gain, down, up = (
                        lax.dynamic_index_in_dim(
                            v[0].reshape(v.shape[1], replicas, width), chunk, 1, keepdims=False
                        )
                        for v in ws
                    )
                    low = (gain.astype(f32) * down.astype(f32)).astype(bf16)
                    layer = section ^ w
                    spot = (k, layer, 0, part * width)
                    both_cut = lax.dynamic_update_slice(both_cut, low[None, None], spot)
                    spot = (k, layers + layer, 0, part * width)
                    both_cut = lax.dynamic_update_slice(both_cut, up[None, None], spot)
                    if w == 0:
                        gain_cut = lax.dynamic_update_slice(
                            gain_cut, gain.astype(f32)[None], (k, 0, part * width)
                        )

    pieces = list(lax.optimization_barrier((*pieces, coef))[:-1])
    stacked = pl.pallas_call(
        stack_kernel,
        out_shape=jax.ShapeDtypeStruct((MEMBERS, 2, rows, columns), bf16),
        in_specs=[IN_VMEM] * MEMBERS,
        out_specs=IN_VMEM,
        compiler_params=params,
        cost_estimate=cost(COST_SMALL),
        name="stack",
    )(*pieces)
    pieces = [stacked] + [from_partner(stacked, "section", k) for k in range(1, sections)]

    message = (2, bottle, width)
    if aligned:
        sends = [(message, f32)] + [(message, bf16)] * (slots - 1)
    else:
        sends = [((slots,) + message, f32)]
    operands = (*coefs, *pieces, gain_cut, both_cut)
    parcels = pl.pallas_call(
        functools.partial(grads_kernel, layers, bottle, width, group, chunks),
        out_shape=[jax.ShapeDtypeStruct(s, d) for s, d in sends],
        in_specs=[IN_VMEM] * len(operands),
        out_specs=[IN_VMEM] * len(sends),
        scratch_shapes=[pltpu.VMEM((slots,) + message, f32)],
        compiler_params=params,
        name="grads",
    )(*operands)
    if not aligned:
        parcels = [
            lax.dynamic_index_in_dim(parcels[0], slot ^ r, 0, keepdims=False)
            for r in range(slots)
        ]
        parcels[1:] = [v.astype(bf16) for v in parcels[1:]]

    total = parcels[0]
    for r in range(1, slots):
        received = from_partner(parcels[r], "dp", mask(r, group, chunks))
        total = total + received.astype(f32)
    return (total[0][None], total[1][None])


def solution(mesh):
    placed = (
        P(None, "dp", "section"),
        P(None, "dp", "section"),
        P(None, "dp", "section"),
        P(None, "dp", "section"),
        P("section", None),
        P("section", None, None),
        P("section", None, None),
    )
    return jax.shard_map(
        per_device,
        mesh=mesh,
        in_specs=placed,
        out_specs=(P("section", None, "dp"), P("section", None, "dp")),
        check_vma=False,
    )
```

time: 38.4 us -> 36.6 us (0.953)
  Pallas kernels: 5.96 us -> 4.55 us
  local copies, waits for them, and re-layouts: 0.67 us -> 1.38 us
  waiting for transfers between devices: 14.4 us -> 13.7 us
  starting transfers between devices: 16.4 us -> 16 us
    ppermute x4 -> x0, waiting for transfers between devices: 6.5 us -> none  [per_device(): total = total + lax.ppermute(parcels[r], BOTH, route).astype(f32)]
    ppermute x4 -> x0, starting transfers between devices: 6.01 us -> none  [per_device(): total = total + lax.ppermute(parcels[r], BOTH, route).astype(f32)]
    ppermute x11 -> x14, waiting for transfers between devices: 7.9 us -> 13.7 us  [from_partner(): lax.ppermute(value, axis, [(i, i ^ flip) for i in range(lax.axis_size(axi...]
    ppermute x11 -> x14, starting transfers between devices: 10.4 us -> 16 us  [from_partner(): lax.ppermute(value, axis, [(i, i ^ flip) for i in range(lax.axis_size(axi...]
    pallas_call x2 -> x4, Pallas kernels: 4.11 us -> 3.14 us  [the longest x1 1.62 us: per_device(): pl.pallas_call(functools.partial(products_kernel, layers), out_shape=[jax...]
    unnamed x6, local copies, waits for them, and re-layouts: 0.01 us -> 0.72 us
    pallas_call x1, Pallas kernels: 1.45 us -> 0.99 us  [per_device(): pl.pallas_call(functools.partial(grads_kernel, layers, bottle, width, gro...]
  transfers between devices with their start and end apart: 15 -> 14, of which waited for: 5 -> 9; matrix products, arithmetic and copies ran while one was open for 0% -> 0% of each run, Pallas kernels for 12% -> 10%
where the time goes in v3:
time: 36.6 us; the launch traced here: 36.3 us
  starting transfers between devices  16 us (44%)
  waiting for transfers between devices  13.7 us (37%)
  Pallas kernels  4.55 us (12%)
  local copies, waits for them, and re-layouts  1.38 us (4%)
  between operations  0.73 us (2%)
    ppermute x14, starting transfers between devices, from_partner(): lax.ppermute(value, axis, [(i, i ^ flip) for i in range(lax.axis_size(axi...  16 us
    ppermute x14, waiting for transfers between devices, from_partner(): lax.ppermute(value, axis, [(i, i ^ flip) for i in range(lax.axis_size(axi...  13.7 us
    pallas_call x1, Pallas kernels, per_device(): pl.pallas_call(functools.partial(products_kernel, layers), out_shape=[jax...  1.62 us
    pallas_call x1, Pallas kernels, per_device(): pl.pallas_call(functools.partial(pack_kernel, width, group, chunks), out_...  1.37 us
    pallas_call x1, Pallas kernels, per_device(): pl.pallas_call(functools.partial(grads_kernel, layers, bottle, width, gro...  0.99 us
  transfers between devices with their start and end apart: 14, of which 9 were waited for; matrix products, arithmetic and copies ran while one was open for 0% of the time, Pallas kernels for 10%

profile of v3, /device:TPU:0, one launch (start us, length us, event | category | flops | bytes accessed | tf_op | source)
XLA Modules:
  0.0 36.3 jit_solution(11104869594515312432)
XLA Ops:
  0.6 0.5 %collective-permute-start.1 = (bf16[1,64,4096]{2,1,0:T(8,128)(2,1)}, bf16[1,64,4096]{2,1,0:T(8,128)(2,1)S(1)}, u32[]{:S(2)}, u32[]{:S(2)}) collective-permute-start(bf16[1,64,4096]{2,1,0:T(8,128)(2,1)} %refs_1_.3), channel_id=1, source_target_pairs={{0,16},{16,0},{1,17},{17,1},{2,18},{18,2},{3,19},{19,3},{4,20},{20... | collective-permute-start | bytes 1572872 | tf_op jit(solution)/shard_map/ppermute | solution.py:28
  1.2 0.4 %collective-permute-start = (bf16[1,1,4096]{2,1,0:T(2,128)(2,1)}, bf16[1,1,4096]{2,1,0:T(2,128)(2,1)S(1)}, u32[]{:S(2)}, u32[]{:S(2)}) collective-permute-start(bf16[1,1,4096]{2,1,0:T(2,128)(2,1)} %bitcast.1), channel_id=1, source_target_pairs={{0,16},{16,0},{1,17},{17,1},{2,18},{18,2},{3,19},{19,3},{4,20},{20... | collective-permute-start | bytes 24584 | tf_op jit(solution)/shard_map/ppermute | solution.py:28
  1.7 1.4 %pack.1 = (bf16[2,128,2048]{2,1,0:T(8,128)(2,1)S(1)}, bf16[2,128,512]{2,1,0:T(8,128)(2,1)S(1)}, bf16[2,128,512]{2,1,0:T(8,128)(2,1)S(1)}, bf16[2,128,512]{2,1,0:T(8,128)(2,1)S(1)}, bf16[2,128,512]{2,1,0:T(8,128)(2,1)S(1)}) custom-call(bf16[2,32,2048]{2,1,0:T(8,128)(2,1)} %refs_0_.1, bf16[2,32,2048]{2,1,0:T(8,128)(2,1)} %refs_1_.2, ...), custom_call_target="tpu_custom_call" | custom-call | tf_op jit(solution)/shard_map/pack/pallas_call | solution.py:393
  3.0 2.7 %collective-permute-start.7 = (bf16[2,128,512]{2,1,0:T(8,128)(2,1)S(1)}, bf16[2,128,512]{2,1,0:T(8,128)(2,1)S(1)}, u32[]{:S(2)}, u32[]{:S(2)}) collective-permute-start(bf16[2,128,512]{2,1,0:T(8,128)(2,1)S(1)} %get-tuple-element.19), channel_id=1, source_target_pairs={{0,1},{1,0},{2,3},{3,2},{4,5},{5,4},{6,7},{7,6},{8,9},{9,8},{10,11... | collective-permute-start | bytes 786440 | tf_op jit(solution)/shard_map/ppermute | solution.py:28
  5.7 1.5 %collective-permute-start.8 = (bf16[2,128,512]{2,1,0:T(8,128)(2,1)S(1)}, bf16[2,128,512]{2,1,0:T(8,128)(2,1)S(1)}, u32[]{:S(2)}, u32[]{:S(2)}) collective-permute-start(bf16[2,128,512]{2,1,0:T(8,128)(2,1)S(1)} %get-tuple-element.20), channel_id=1, source_target_pairs={{0,2},{1,3},{2,0},{3,1},{4,6},{5,7},{6,4},{7,5},{8,10},{9,11},{10,... | collective-permute-start | bytes 786440 | tf_op jit(solution)/shard_map/ppermute | solution.py:28
  7.3 1.6 %collective-permute-start.9 = (bf16[2,128,512]{2,1,0:T(8,128)(2,1)S(1)}, bf16[2,128,512]{2,1,0:T(8,128)(2,1)S(1)}, u32[]{:S(2)}, u32[]{:S(2)}) collective-permute-start(bf16[2,128,512]{2,1,0:T(8,128)(2,1)S(1)} %get-tuple-element.21), channel_id=1, source_target_pairs={{0,4},{1,5},{2,6},{3,7},{4,0},{5,1},{6,2},{7,3},{8,12},{9,13},{10,... | collective-permute-start | bytes 786440 | tf_op jit(solution)/shard_map/ppermute | solution.py:28
  8.9 0.7 %copy-done.2 = bf16[1,4096]{1,0:T(2,128)(2,1)S(1)} copy-done((bf16[1,4096]{1,0:T(2,128)(2,1)S(1)}, bf16[1,4096]{1,0:T(2,128)(2,1)}, u32[]{:S(2)}) %copy-start.2) | copy-done | bytes 8216
  9.6 1.6 %products.1.refs_0_ = f32[456,128]{1,0:T(8,128)S(1)} custom-call(bf16[2,128,2048]{2,1,0:T(8,128)(2,1)S(1)} %get-tuple-element.17.refs_0_, bf16[1,1,4096]{2,1,0:T(2,128)(2,1)S(1)} %bitcast.2, bf16[1,64,4096]{2,1,0:T(8,128)(2,1)S(1)} %copy-done, bf16[1,64,4096]{2,1,0:T(8,128)(2,1)S(1)} %copy-done.1, ...), custom_call_target="tpu_custom_call" | custom-call | flops 13200000000 | tf_op jit(solution)/shard_map/products/pallas_call | solution.py:424
  11.3 1.5 %collective-permute-done.3.refs_1_ = f32[456,128]{1,0:T(8,128)S(1)} collective-permute-done((f32[456,128]{1,0:T(8,128)S(1)}, f32[456,128]{1,0:T(8,128)S(1)}, u32[]{:S(2)}, u32[]{:S(2)}) %collective-permute-start.3) | collective-permute-done | bytes 233504 | tf_op jit(solution)/shard_map/ppermute | solution.py:28
  13.2 0.9 %collective-permute-done.8.refs_2_ = bf16[2,128,512]{2,1,0:T(8,128)(2,1)S(1)} collective-permute-done((bf16[2,128,512]{2,1,0:T(8,128)(2,1)S(1)}, bf16[2,128,512]{2,1,0:T(8,128)(2,1)S(1)}, u32[]{:S(2)}, u32[]{:S(2)}) %collective-permute-start.8) | collective-permute-done | bytes 262176 | tf_op jit(solution)/shard_map/ppermute | solution.py:28
  14.0 1.2 %collective-permute-done.9.refs_3_ = bf16[2,128,512]{2,1,0:T(8,128)(2,1)S(1)} collective-permute-done((bf16[2,128,512]{2,1,0:T(8,128)(2,1)S(1)}, bf16[2,128,512]{2,1,0:T(8,128)(2,1)S(1)}, u32[]{:S(2)}, u32[]{:S(2)}) %collective-permute-start.9) | collective-permute-done | bytes 262176 | tf_op jit(solution)/shard_map/ppermute | solution.py:28
  15.4 0.6 %collective-permute-start.4 = (bf16[208,128]{1,0:T(8,128)(2,1)S(1)}, bf16[208,128]{1,0:T(8,128)(2,1)S(1)}, u32[]{:S(2)}, u32[]{:S(2)}) collective-permute-start(bf16[208,128]{1,0:T(8,128)(2,1)S(1)} %relay.1.refs_0_), channel_id=1, source_target_pairs={{0,1},{1,0},{2,3},{3,2},{4,5},{5,4},{6,7},{7,6},{8,9},{9,8},{10,11... | collective-permute-start | bytes 159752 | tf_op jit(solution)/shard_map/ppermute | solution.py:28
  16.0 0.6 %collective-permute-start.5 = (bf16[208,128]{1,0:T(8,128)(2,1)S(1)}, bf16[208,128]{1,0:T(8,128)(2,1)S(1)}, u32[]{:S(2)}, u32[]{:S(2)}) collective-permute-start(bf16[208,128]{1,0:T(8,128)(2,1)S(1)} %relay.1.refs_0_), channel_id=1, source_target_pairs={{0,2},{1,3},{2,0},{3,1},{4,6},{5,7},{6,4},{7,5},{8,10},{9,11},{10,... | collective-permute-start | bytes 159752 | tf_op jit(solution)/shard_map/ppermute | solution.py:28
  16.6 1.6 %collective-permute-start.6 = (bf16[208,128]{1,0:T(8,128)(2,1)S(1)}, bf16[208,128]{1,0:T(8,128)(2,1)S(1)}, u32[]{:S(2)}, u32[]{:S(2)}) collective-permute-start(bf16[208,128]{1,0:T(8,128)(2,1)S(1)} %relay.1.refs_0_), channel_id=1, source_target_pairs={{0,4},{1,5},{2,6},{3,7},{4,0},{5,1},{6,2},{7,3},{8,12},{9,13},{10,... | collective-permute-start | bytes 159752 | tf_op jit(solution)/shard_map/ppermute | solution.py:28
  18.3 1.4 %collective-permute-done.4.refs_1_ = bf16[208,128]{1,0:T(8,128)(2,1)S(1)} collective-permute-done((bf16[208,128]{1,0:T(8,128)(2,1)S(1)}, bf16[208,128]{1,0:T(8,128)(2,1)S(1)}, u32[]{:S(2)}, u32[]{:S(2)}) %collective-permute-start.4) | collective-permute-done | bytes 53280 | tf_op jit(solution)/shard_map/ppermute | solution.py:28
  19.7 0.5 %collective-permute-done.5.refs_2_ = bf16[208,128]{1,0:T(8,128)(2,1)S(1)} collective-permute-done((bf16[208,128]{1,0:T(8,128)(2,1)S(1)}, bf16[208,128]{1,0:T(8,128)(2,1)S(1)}, u32[]{:S(2)}, u32[]{:S(2)}) %collective-permute-start.5) | collective-permute-done | bytes 53280 | tf_op jit(solution)/shard_map/ppermute | solution.py:28
  20.2 0.6 %collective-permute-done.6.refs_3_ = bf16[208,128]{1,0:T(8,128)(2,1)S(1)} collective-permute-done((bf16[208,128]{1,0:T(8,128)(2,1)S(1)}, bf16[208,128]{1,0:T(8,128)(2,1)S(1)}, u32[]{:S(2)}, u32[]{:S(2)}) %collective-permute-start.6) | collective-permute-done | bytes 53280 | tf_op jit(solution)/shard_map/ppermute | solution.py:28
  20.8 1.0 %grads.1 = (f32[2,64,256]{2,1,0:T(8,128)S(1)}, bf16[2,64,256]{2,1,0:T(8,128)(2,1)S(1)}, bf16[2,64,256]{2,1,0:T(8,128)(2,1)S(1)}, bf16[2,64,256]{2,1,0:T(8,128)(2,1)S(1)}) custom-call(bf16[208,128]{1,0:T(8,128)(2,1)S(1)} %relay.1.refs_0_, bf16[208,128]{1,0:T(8,128)(2,1)S(1)} %collective-permute-done.4.refs_1_, ...), custom_call_target="tpu_custom_call" | custom-call | tf_op jit(solution)/shard_map/grads/pallas_call | solution.py:508
  21.8 3.4 %collective-permute-start.11 = (bf16[2,64,256]{2,1,0:T(8,128)(2,1)S(1)}, bf16[2,64,256]{2,1,0:T(8,128)(2,1)S(1)}, u32[]{:S(2)}, u32[]{:S(2)}) collective-permute-start(bf16[2,64,256]{2,1,0:T(8,128)(2,1)S(1)} %get-tuple-element.29), channel_id=1, source_target_pairs={{0,7},{1,6},{2,5},{3,4},{4,3},{5,2},{6,1},{7,0},{8,15},{9,14},{10,... | collective-permute-start | bytes 196616 | tf_op jit(solution)/shard_map/ppermute | solution.py:28
  25.2 2.6 %collective-permute-start.12 = (bf16[2,64,256]{2,1,0:T(8,128)(2,1)S(1)}, bf16[2,64,256]{2,1,0:T(8,128)(2,1)S(1)}, u32[]{:S(2)}, u32[]{:S(2)}) collective-permute-start(bf16[2,64,256]{2,1,0:T(8,128)(2,1)S(1)} %get-tuple-element.30), channel_id=1, source_target_pairs={{0,8},{1,9},{2,10},{3,11},{4,12},{5,13},{6,14},{7,15},{8,0},{9,1},... | collective-permute-start | bytes 196616 | tf_op jit(solution)/shard_map/ppermute | solution.py:28
  28.0 0.5 %collective-permute-done.11 = bf16[2,64,256]{2,1,0:T(8,128)(2,1)S(1)} collective-permute-done((bf16[2,64,256]{2,1,0:T(8,128)(2,1)S(1)}, bf16[2,64,256]{2,1,0:T(8,128)(2,1)S(1)}, u32[]{:S(2)}, u32[]{:S(2)}) %collective-permute-start.11) | collective-permute-done | bytes 65568 | tf_op jit(solution)/shard_map/ppermute | solution.py:28
  28.5 3.2 %collective-permute-done.12 = bf16[2,64,256]{2,1,0:T(8,128)(2,1)S(1)} collective-permute-done((bf16[2,64,256]{2,1,0:T(8,128)(2,1)S(1)}, bf16[2,64,256]{2,1,0:T(8,128)(2,1)S(1)}, u32[]{:S(2)}, u32[]{:S(2)}) %collective-permute-start.12) | collective-permute-done | bytes 65568 | tf_op jit(solution)/shard_map/ppermute | solution.py:28
  31.8 3.9 %collective-permute-done.13 = bf16[2,64,256]{2,1,0:T(8,128)(2,1)S(1)} collective-permute-done((bf16[2,64,256]{2,1,0:T(8,128)(2,1)S(1)}, bf16[2,64,256]{2,1,0:T(8,128)(2,1)S(1)}, u32[]{:S(2)}, u32[]{:S(2)}) %collective-permute-start.13) | collective-permute-done | bytes 65568 | tf_op jit(solution)/shard_map/ppermute | solution.py:28
  35.7 0.7 %fusion = (f32[1,64,256]{2,1,0:T(8,128)}, f32[1,64,256]{2,1,0:T(8,128)}) fusion(f32[2,64,256]{2,1,0:T(8,128)S(1)} %convert_add_fusion), kind=kLoop, calls=%fused_computation.1 | loop fusion | bytes 262144 | tf_op jit(solution)/shard_map/slice | solution.py:528
  (18 shorter events, 1.0 us)
Async XLA Ops:
  0.6 8.2 %collective-permute-start.1 = (bf16[1,64,4096]{2,1,0:T(8,128)(2,1)}, bf16[1,64,4096]{2,1,0:T(8,128)(2,1)S(1)}, u32[]{:S(2)}, u32[]{:S(2)}) collective-permute-start(bf16[1,64,4096]{2,1,0:T(8,128)(2,1)} %refs_1_.3), channel_id=1, source_target_pairs={{0,16},{16,0},{1,17},{17,1},{2,18},{18,2},{3,19},{19,3},{4,20},{20... | collective-permute-start | bytes 1572872 | tf_op jit(solution)/shard_map/ppermute | solution.py:28
  1.1 7.7 %collective-permute-start.2 = (bf16[1,64,4096]{2,1,0:T(8,128)(2,1)}, bf16[1,64,4096]{2,1,0:T(8,128)(2,1)S(1)}, u32[]{:S(2)}, u32[]{:S(2)}) collective-permute-start(bf16[1,64,4096]{2,1,0:T(8,128)(2,1)} %refs_2_.5), channel_id=1, source_target_pairs={{0,16},{16,0},{1,17},{17,1},{2,18},{18,2},{3,19},{19,3},{4,20},{20... | collective-permute-start | bytes 1572872 | tf_op jit(solution)/shard_map/ppermute | solution.py:28
  1.2 7.6 %copy-start = (bf16[1,64,4096]{2,1,0:T(8,128)(2,1)S(1)}, bf16[1,64,4096]{2,1,0:T(8,128)(2,1)}, u32[]{:S(2)}) copy-start(bf16[1,64,4096]{2,1,0:T(8,128)(2,1)} %refs_1_.3) | copy-start | bytes 1572868
  1.2 7.6 %copy-start.1 = (bf16[1,64,4096]{2,1,0:T(8,128)(2,1)S(1)}, bf16[1,64,4096]{2,1,0:T(8,128)(2,1)}, u32[]{:S(2)}) copy-start(bf16[1,64,4096]{2,1,0:T(8,128)(2,1)} %refs_2_.5) | copy-start | bytes 1572868
  1.2 6.0 %collective-permute-start = (bf16[1,1,4096]{2,1,0:T(2,128)(2,1)}, bf16[1,1,4096]{2,1,0:T(2,128)(2,1)S(1)}, u32[]{:S(2)}, u32[]{:S(2)}) collective-permute-start(bf16[1,1,4096]{2,1,0:T(2,128)(2,1)} %bitcast.1), channel_id=1, source_target_pairs={{0,16},{16,0},{1,17},{17,1},{2,18},{18,2},{3,19},{19,3},{4,20},{20... | collective-permute-start | bytes 24584 | tf_op jit(solution)/shard_map/ppermute | solution.py:28
  3.0 10.1 %collective-permute-start.7 = (bf16[2,128,512]{2,1,0:T(8,128)(2,1)S(1)}, bf16[2,128,512]{2,1,0:T(8,128)(2,1)S(1)}, u32[]{:S(2)}, u32[]{:S(2)}) collective-permute-start(bf16[2,128,512]{2,1,0:T(8,128)(2,1)S(1)} %get-tuple-element.19), channel_id=1, source_target_pairs={{0,1},{1,0},{2,3},{3,2},{4,5},{5,4},{6,7},{7,6},{8,9},{9,8},{10,11... | collective-permute-start | bytes 786440 | tf_op jit(solution)/shard_map/ppermute | solution.py:28
  5.7 8.3 %collective-permute-start.8 = (bf16[2,128,512]{2,1,0:T(8,128)(2,1)S(1)}, bf16[2,128,512]{2,1,0:T(8,128)(2,1)S(1)}, u32[]{:S(2)}, u32[]{:S(2)}) collective-permute-start(bf16[2,128,512]{2,1,0:T(8,128)(2,1)S(1)} %get-tuple-element.20), channel_id=1, source_target_pairs={{0,2},{1,3},{2,0},{3,1},{4,6},{5,7},{6,4},{7,5},{8,10},{9,11},{10,... | collective-permute-start | bytes 786440 | tf_op jit(solution)/shard_map/ppermute | solution.py:28
  7.3 8.0 %collective-permute-start.9 = (bf16[2,128,512]{2,1,0:T(8,128)(2,1)S(1)}, bf16[2,128,512]{2,1,0:T(8,128)(2,1)S(1)}, u32[]{:S(2)}, u32[]{:S(2)}) collective-permute-start(bf16[2,128,512]{2,1,0:T(8,128)(2,1)S(1)} %get-tuple-element.21), channel_id=1, source_target_pairs={{0,4},{1,5},{2,6},{3,7},{4,0},{5,1},{6,2},{7,3},{8,12},{9,13},{10,... | collective-permute-start | bytes 786440 | tf_op jit(solution)/shard_map/ppermute | solution.py:28
  8.9 0.7 %copy-start.2 = (bf16[1,4096]{1,0:T(2,128)(2,1)S(1)}, bf16[1,4096]{1,0:T(2,128)(2,1)}, u32[]{:S(2)}) copy-start(bf16[1,4096]{1,0:T(2,128)(2,1)} %param.11) | copy-start | bytes 24580
  11.2 1.5 %collective-permute-start.3 = (f32[456,128]{1,0:T(8,128)S(1)}, f32[456,128]{1,0:T(8,128)S(1)}, u32[]{:S(2)}, u32[]{:S(2)}) collective-permute-start(f32[456,128]{1,0:T(8,128)S(1)} %products.1.refs_0_), channel_id=1, source_target_pairs={{0,16},{16,0},{1,17},{17,1},{2,18},{18,2},{3,19},{19,3},{4,20},{20... | collective-permute-start | bytes 700424 | tf_op jit(solution)/shard_map/ppermute | solution.py:28
  15.3 5.4 %collective-permute-start.10 = (bf16[4,2,128,512]{3,2,1,0:T(8,128)(2,1)S(1)}, bf16[4,2,128,512]{3,2,1,0:T(8,128)(2,1)S(1)}, u32[]{:S(2)}, u32[]{:S(2)}) collective-permute-start(bf16[4,2,128,512]{3,2,1,0:T(8,128)(2,1)S(1)} %stack.1.refs_4_), channel_id=1, source_target_pairs={{0,16},{16,0},{1,17},{17,1},{2,18},{18,2},{3,19},{19,3},{4,20},{20... | collective-permute-start | bytes 3145736 | tf_op jit(solution)/shard_map/ppermute | solution.py:28
  15.4 4.2 %collective-permute-start.4 = (bf16[208,128]{1,0:T(8,128)(2,1)S(1)}, bf16[208,128]{1,0:T(8,128)(2,1)S(1)}, u32[]{:S(2)}, u32[]{:S(2)}) collective-permute-start(bf16[208,128]{1,0:T(8,128)(2,1)S(1)} %relay.1.refs_0_), channel_id=1, source_target_pairs={{0,1},{1,0},{2,3},{3,2},{4,5},{5,4},{6,7},{7,6},{8,9},{9,8},{10,11... | collective-permute-start | bytes 159752 | tf_op jit(solution)/shard_map/ppermute | solution.py:28
  16.0 4.1 %collective-permute-start.5 = (bf16[208,128]{1,0:T(8,128)(2,1)S(1)}, bf16[208,128]{1,0:T(8,128)(2,1)S(1)}, u32[]{:S(2)}, u32[]{:S(2)}) collective-permute-start(bf16[208,128]{1,0:T(8,128)(2,1)S(1)} %relay.1.refs_0_), channel_id=1, source_target_pairs={{0,2},{1,3},{2,0},{3,1},{4,6},{5,7},{6,4},{7,5},{8,10},{9,11},{10,... | collective-permute-start | bytes 159752 | tf_op jit(solution)/shard_map/ppermute | solution.py:28
  16.6 4.1 %collective-permute-start.6 = (bf16[208,128]{1,0:T(8,128)(2,1)S(1)}, bf16[208,128]{1,0:T(8,128)(2,1)S(1)}, u32[]{:S(2)}, u32[]{:S(2)}) collective-permute-start(bf16[208,128]{1,0:T(8,128)(2,1)S(1)} %relay.1.refs_0_), channel_id=1, source_target_pairs={{0,4},{1,5},{2,6},{3,7},{4,0},{5,1},{6,2},{7,3},{8,12},{9,13},{10,... | collective-permute-start | bytes 159752 | tf_op jit(solution)/shard_map/ppermute | solution.py:28
  21.8 6.8 %collective-permute-start.11 = (bf16[2,64,256]{2,1,0:T(8,128)(2,1)S(1)}, bf16[2,64,256]{2,1,0:T(8,128)(2,1)S(1)}, u32[]{:S(2)}, u32[]{:S(2)}) collective-permute-start(bf16[2,64,256]{2,1,0:T(8,128)(2,1)S(1)} %get-tuple-element.29), channel_id=1, source_target_pairs={{0,7},{1,6},{2,5},{3,4},{4,3},{5,2},{6,1},{7,0},{8,15},{9,14},{10,... | collective-permute-start | bytes 196616 | tf_op jit(solution)/shard_map/ppermute | solution.py:28
  25.2 6.6 %collective-permute-start.12 = (bf16[2,64,256]{2,1,0:T(8,128)(2,1)S(1)}, bf16[2,64,256]{2,1,0:T(8,128)(2,1)S(1)}, u32[]{:S(2)}, u32[]{:S(2)}) collective-permute-start(bf16[2,64,256]{2,1,0:T(8,128)(2,1)S(1)} %get-tuple-element.30), channel_id=1, source_target_pairs={{0,8},{1,9},{2,10},{3,11},{4,12},{5,13},{6,14},{7,15},{8,0},{9,1},... | collective-permute-start | bytes 196616 | tf_op jit(solution)/shard_map/ppermute | solution.py:28
  27.8 7.9 %collective-permute-start.13 = (bf16[2,64,256]{2,1,0:T(8,128)(2,1)S(1)}, bf16[2,64,256]{2,1,0:T(8,128)(2,1)S(1)}, u32[]{:S(2)}, u32[]{:S(2)}) collective-permute-start(bf16[2,64,256]{2,1,0:T(8,128)(2,1)S(1)} %get-tuple-element.31), channel_id=1, source_target_pairs={{0,15},{1,14},{2,13},{3,12},{4,11},{5,10},{6,9},{7,8},{8,7},{9,6},... | collective-permute-start | bytes 196616 | tf_op jit(solution)/shard_map/ppermute | solution.py:28

commit v4 on v3

--- a/solution.py
+++ b/solution.py
@@ -14,6 +14,7 @@
 TWIST = 0
 COST_PRODUCTS = 12
 COST_SMALL = 0.1
+COST_GRADS = 10
 f32 = jnp.float32
 bf16 = jnp.bfloat16
 IN_VMEM = pl.BlockSpec(memory_space=pltpu.VMEM)
@@ -41,9 +42,13 @@
     return high, (value - high.astype(f32)).astype(bf16)
 
 
-def dot_split(left, right):
+def dot_tn(left, right):
+    return lax.dot_general(left, right, (((0,), (0,)), ((), ())), preferred_element_type=f32)
+
+
+def dot_split(left, right, dot=dot_nn):
     high, low = split(left)
-    return dot_nn(high, right) + dot_nn(low, right)
+    return dot(high, right) + dot(low, right)
 
 
 LEADERS = (0, 1, 2, 4) if STAR else (0, 1, 2, 3)
@@ -82,9 +87,9 @@
 
 
 def pack_kernel(width, group, chunks, *refs):
-    acts = refs[:4]
-    both = refs[4]
-    outs = refs[5:-1]
+    acts, gain = refs[:4], refs[4]
+    both, gain_out = refs[5:7]
+    outs = refs[7:-1]
     sems = refs[-1]
     micro, tokens = acts[0].shape[0], acts[0].shape[1]
     section, label, _ = whereabouts(group, chunks)
@@ -98,6 +103,8 @@
                 )
             )
             copies[-1].start()
+    last = pltpu.make_async_copy(gain, gain_out, sems.at[len(copies)])
+    last.start()
     for n, copy in enumerate(copies):
         copy.wait()
         a, m = divmod(n, micro)
@@ -109,13 +116,14 @@
                 out[a // 2, start : start + tokens, part * width : (part + 1) * width] = both[
                     a // 2, start : start + tokens, span
                 ]
+    last.wait()
 
 
 def two_parts(refs):
     if len(refs) == 2:
         return refs
     height, side = refs[0].shape
-    return refs[0].at[: height - side], refs[0].at[height - side :]
+    return refs[0].at[: height - side // 2], refs[0].at[height - side // 2 :]
 
 
 def products_kernel(layers, *refs):
@@ -158,10 +166,8 @@
         high_part = high_all[:size]
         low_part = low_all[bottle:]
         fine_part = fine_all[bottle:]
-        gram_out[:size, :size] = jnp.zeros((size, size), f32)
-        gram_out[:size, size:] = dot_nt(low_part, high_part) + dot_nt(fine_part, high_part)
-        gram_out[size:, :size] = dot_nt(high_part, low_part) + dot_nt(high_part, fine_part)
-        gram_out[size:, size:] = dot_nt(high_part, high_part)
+        gram_out[:, :size] = dot_nt(high_part, low_part) + dot_nt(high_part, fine_part)
+        gram_out[:, size:] = dot_nt(high_part, high_part)
     else:
         gram_out[...] = jnp.zeros_like(gram_out)
 
@@ -185,16 +191,11 @@
     at += layers * K
     norm = prod[at : at + 1]
 
-    def low_high(l, m):
-        return gram[(l - 1) * K : l * K, (inner + m) * K : (inner + m + 1) * K]
-
     def high_low(m, l):
-        return gram[(inner + m) * K : (inner + m + 1) * K, (l - 1) * K : l * K]
+        return gram[m * K : (m + 1) * K, (l - 1) * K : l * K]
 
     def high_high(m, n):
-        return gram[
-            (inner + m) * K : (inner + m + 1) * K, (inner + n) * K : (inner + n + 1) * K
-        ]
+        return gram[m * K : (m + 1) * K, (inner + n) * K : (inner + n + 1) * K]
 
     inverses, bottles, hidden_high = [], [], []
     for l in range(layers):
@@ -209,7 +210,7 @@
             before = h_high[l]
             h_high = [h_high[n] + dot_split(high_high(n, l), active) for n in range(inner)]
             for n in range(l + 1, layers):
-                h_low[n] = h_low[n] + dot_split(low_high(n, l), active)
+                h_low[n] = h_low[n] + dot_split(high_low(l, n), active, dot_tn)
             norm = norm + jnp.sum(
                 active.astype(f32) * (before + h_high[l]), axis=0, keepdims=True
             )
@@ -284,19 +285,10 @@
         refs[-1][k] = ref[...]
 
 
-def grads_kernel(layers, bottle, width, group, chunks, *refs):
+def factors_kernel_part(layers, bottle, section, coefs, lefts, mates):
     K = bottle
     inner = layers - 1
-    coefs = refs[:MEMBERS]
-    pieces = refs[MEMBERS : MEMBERS + layers]
-    gain, both = refs[MEMBERS + layers : MEMBERS + layers + 2]
-    outs = refs[MEMBERS + layers + 2 : -1]
-    parcel = refs[-1]
-    section, _, own_slot = whereabouts(group, chunks)
     above = [section <= i for i in range(inner)]
-    other_of = [i + jnp.where(above[i], 1, 0) for i in range(inner)]
-    by_hidden = [0.0] * layers
-    by_close = [0.0] * layers
     cross = [0.0] * inner
     drag = [0.0] * inner
     for m in range(MEMBERS):
@@ -319,14 +311,10 @@
             return total
 
         coarse, fine = split(grad.astype(f32) * scale(0))
-        full = jnp.zeros_like(lines[:1])
-        for l in range(1, layers):
-            full = full + jnp.where(section < l, lines[l - 1 : l], 0.0)
-        pulled = (-full * active_f).astype(bf16)
-        left = jnp.concatenate([coarse, fine, pulled], axis=0)
-        for k in range(layers):
-            by_hidden[k] = by_hidden[k] + dot_nn(left, pieces[k][m, 0])
-            by_close[k] = by_close[k] + dot_nn(active, pieces[k][m, 1])
+        lefts[m, :K] = coarse
+        lefts[m, K : 2 * K] = fine
+        lefts[m, 2 * K : 3 * K] = (-weight(0) * active_f).astype(bf16)
+        lefts[m, 3 * K :] = active
         for i in range(inner):
             factor = jnp.where(above[i], scale(1 + i), 1.0)
             other = (others[i].astype(f32) * factor).astype(bf16)
@@ -338,21 +326,52 @@
                 held = jnp.where(section < n, extras[n - 1].astype(f32), held.astype(f32))
             held = jnp.where(section == n, active_f, held.astype(f32)).astype(bf16)
             drag[n] = drag[n] + dot_nt((-weight(n) * active_f).astype(bf16), held)
-    for k in range(layers):
-        down = by_hidden[k][:K] + by_hidden[k][K : 2 * K]
-        up = by_close[k] + by_hidden[k][2 * K :]
-        for i in range(inner):
-            index = jnp.where(above[i], other_of[i], layers + other_of[i])
-            term = dot_nn(cross[i].astype(bf16), both[k, index])
-            up = up + jnp.where(above[i], term, 0.0)
-            down = down + jnp.where(above[i], 0.0, term)
-            up = up + dot_nn(drag[i].astype(bf16), both[k, layers + i])
-        down = down * gain[k]
+    for i in range(inner):
+        mates[2 * i] = cross[i].astype(bf16)
+        mates[2 * i + 1] = drag[i].astype(bf16)
+
+
+def grads_kernel(layers, bottle, width, group, chunks, turn, *refs):
+    K = bottle
+    inner = layers - 1
+    section, _, own_slot = whereabouts(group, chunks)
+    final = turn == layers - 1
+    if turn == 0:
+        coefs, refs = refs[:MEMBERS], refs[MEMBERS:]
+        pieces, refs = refs[:MEMBERS], refs[MEMBERS:]
+        gain, both, *outs, lefts, mates = refs
+        factors_kernel_part(layers, bottle, section, coefs, lefts, mates)
+        pieces = [ref[...] for ref in pieces]
+        before = []
+    else:
+        lefts, mates, pieces, gain, both = refs[:5]
+        before, outs = refs[5 : 5 + turn], list(refs[5 + turn :])
+        pieces = [pieces[m] for m in range(MEMBERS)]
+    parcel = outs.pop() if final else outs[0]
+    by_hidden, by_close = 0.0, 0.0
+    for m in range(MEMBERS):
+        by_hidden = by_hidden + dot_nn(lefts[m, : 3 * K], pieces[m][0])
+        by_close = by_close + dot_nn(lefts[m, 3 * K :], pieces[m][1])
+    down = by_hidden[:K] + by_hidden[K : 2 * K]
+    up = by_close + by_hidden[2 * K :]
+    for i in range(inner):
+        above = section <= i
+        other = i + jnp.where(above, 1, 0)
+        term = dot_nn(mates[2 * i], both[turn, jnp.where(above, other, layers + other)])
+        up = up + jnp.where(above, term, 0.0)
+        down = down + jnp.where(above, 0.0, term)
+        up = up + dot_nn(mates[2 * i + 1], both[turn, layers + i])
+    down = down * gain[turn]
+    start = (section ^ turn) * group if final else 0
+    for part in range(group):
+        here = slice(part * width, (part + 1) * width)
+        parcel[start + part, 0] = down[:, here]
+        parcel[start + part, 1] = up[:, here]
+    if not final:
+        return
+    for k, ref in enumerate(before):
         for part in range(group):
-            here = slice(part * width, (part + 1) * width)
-            slot = (section ^ k) * group + part
-            parcel[slot, 0] = down[:, here]
-            parcel[slot, 1] = up[:, here]
+            parcel[(section ^ k) * group + part] = ref[part]
     if len(outs) == 1:
         outs[0][...] = parcel[...]
     else:
@@ -386,20 +405,19 @@
     weights = [own]
     for k in range(1, sections):
         weights.append(tuple(from_partner(w, "section", k) for w in own))
-    flat = [w for ws in weights for w in ws]
-
     acts = (inputs_down, inputs_up, cotan_down, cotan_up)
     if aligned:
-        both, *packed = pl.pallas_call(
+        both, gain, *packed = pl.pallas_call(
             functools.partial(pack_kernel, width, group, chunks),
-            out_shape=[pltpu.VMEM((2, rows, share), bf16)]
+            out_shape=[pltpu.VMEM((2, rows, share), bf16), pltpu.VMEM(own[0].shape, bf16)]
             + [pltpu.VMEM((2, rows, columns), bf16)] * MEMBERS,
-            in_specs=[IN_HBM] * 4,
-            out_specs=[IN_VMEM] * (1 + MEMBERS),
-            scratch_shapes=[pltpu.SemaphoreType.DMA((4 * micro,))],
+            in_specs=[IN_HBM] * 5,
+            out_specs=[IN_VMEM] * (2 + MEMBERS),
+            scratch_shapes=[pltpu.SemaphoreType.DMA((4 * micro + 1,))],
             compiler_params=params,
             name="pack",
-        )(*[pltpu.with_memory_space_constraint(v, pltpu.HBM) for v in acts])
+        )(*[pltpu.with_memory_space_constraint(v, pltpu.HBM) for v in (*acts, own[0])])
+        weights[0] = (gain, *own[1:])
     else:
         both = jnp.concatenate([v.reshape(half, share) for v in acts], axis=0)
         both = both.reshape(2, rows, share)
@@ -413,14 +431,15 @@
                 for part in range(group)
             ]
             packed.append(jnp.concatenate(cuts, axis=2))
+    flat = [w for ws in weights for w in ws]
     pieces = [packed[0]]
     for k in range(1, MEMBERS):
         pieces.append(from_partner(packed[k], "dp", LEADERS[k]))
     prod_rows = (3 * layers - 1) * bottle + 8
-    gram_side = 2 * max(inner, 1) * bottle
-    sides = [(prod_rows, rows), (gram_side, gram_side)]
-    if rows == gram_side:
-        sides = [(prod_rows + gram_side, rows)]
+    gram_rows = max(inner, 1) * bottle
+    sides = [(prod_rows, rows), (gram_rows, 2 * gram_rows)]
+    if rows == 2 * gram_rows:
+        sides = [(prod_rows + gram_rows, rows)]
     sums = pl.pallas_call(
         functools.partial(products_kernel, layers),
         out_shape=[jax.ShapeDtypeStruct(side, f32) for side in sides],
@@ -487,7 +506,7 @@
                             gain_cut, gain.astype(f32)[None], (k, 0, part * width)
                         )
 
-    pieces = list(lax.optimization_barrier((*pieces, coef))[:-1])
+    gated = list(lax.optimization_barrier((*pieces, coef))[:-1])
     stacked = pl.pallas_call(
         stack_kernel,
         out_shape=jax.ShapeDtypeStruct((MEMBERS, 2, rows, columns), bf16),
@@ -496,24 +515,41 @@
         compiler_params=params,
         cost_estimate=cost(COST_SMALL),
         name="stack",
-    )(*pieces)
-    pieces = [stacked] + [from_partner(stacked, "section", k) for k in range(1, sections)]
+    )(*gated)
+    handed = [None] + [from_partner(stacked, "section", k) for k in range(1, sections)]
 
     message = (2, bottle, width)
-    if aligned:
-        sends = [(message, f32)] + [(message, bf16)] * (slots - 1)
-    else:
-        sends = [((slots,) + message, f32)]
-    operands = (*coefs, *pieces, gain_cut, both_cut)
-    parcels = pl.pallas_call(
-        functools.partial(grads_kernel, layers, bottle, width, group, chunks),
-        out_shape=[jax.ShapeDtypeStruct(s, d) for s, d in sends],
-        in_specs=[IN_VMEM] * len(operands),
-        out_specs=[IN_VMEM] * len(sends),
-        scratch_shapes=[pltpu.VMEM((slots,) + message, f32)],
-        compiler_params=params,
-        name="grads",
-    )(*operands)
+    left_shape = jax.ShapeDtypeStruct((MEMBERS, 4 * bottle, rows), bf16)
+    mate_shape = jax.ShapeDtypeStruct((max(2 * inner, 1), bottle, bottle), bf16)
+    held = jax.ShapeDtypeStruct((group,) + message, f32)
+    before = []
+    for k in range(sections):
+        shapes, scratch = [held], []
+        if k == sections - 1:
+            scratch = [pltpu.VMEM((slots,) + message, f32)]
+            shapes = [jax.ShapeDtypeStruct((slots,) + message, f32)]
+            if aligned:
+                shapes = [jax.ShapeDtypeStruct(message, f32)]
+                shapes += [jax.ShapeDtypeStruct(message, bf16)] * (slots - 1)
+        if k == 0:
+            shapes += [left_shape, mate_shape]
+            operands = (*coefs, *pieces, gain_cut, both_cut)
+        else:
+            operands = (lefts, mates, handed[k], gain_cut, both_cut, *before)
+        parcels = pl.pallas_call(
+            functools.partial(grads_kernel, layers, bottle, width, group, chunks, k),
+            out_shape=shapes,
+            in_specs=[IN_VMEM] * len(operands),
+            out_specs=[IN_VMEM] * len(shapes),
+            scratch_shapes=scratch,
+            compiler_params=params,
+            cost_estimate=cost(COST_GRADS),
+            name="grads",
+        )(*operands)
+        if k == 0:
+            *parcels, lefts, mates = parcels
+        if k < sections - 1:
+            before += parcels
     if not aligned:
         parcels = [
             lax.dynamic_index_in_dim(parcels[0], slot ^ r, 0, keepdims=False)

time: 36.6 us -> 32.9 us (0.90)
  waiting for transfers between devices: 13.7 us -> 11.6 us
  starting transfers between devices: 16 us -> 15.2 us
  local copies, waits for them, and re-layouts: 1.38 us -> 0.67 us
    ppermute x14, waiting for transfers between devices: 13.7 us -> 11.6 us  [from_partner(): lax.ppermute(value, axis, [(i, i ^ flip) for i in range(lax.axis_size(axi...]
    ppermute x14, starting transfers between devices: 16 us -> 15.2 us  [from_partner(): lax.ppermute(value, axis, [(i, i ^ flip) for i in range(lax.axis_size(axi...]
    unnamed x6 -> x4, local copies, waits for them, and re-layouts: 0.72 us -> 0.01 us
    pallas_call x1 -> x2, Pallas kernels: 0.99 us -> 1.04 us  [per_device(): pl.pallas_call(functools.partial(grads_kernel, layers, bottle, width, gro...]
  transfers between devices with their start and end apart: 14 -> 14, of which waited for: 9 -> 8; matrix products, arithmetic and copies ran while one was open for 0% -> 0% of each run, Pallas kernels for 10% -> 12%
where the time goes in v4:
time: 32.9 us; the launch traced here: 32.7 us
  starting transfers between devices  15.2 us (46%)
  waiting for transfers between devices  11.6 us (35%)
  Pallas kernels  4.48 us (14%)
  between operations  0.72 us (2%)
  local copies, waits for them, and re-layouts  0.67 us (2%)
    ppermute x14, starting transfers between devices, from_partner(): lax.ppermute(value, axis, [(i, i ^ flip) for i in range(lax.axis_size(axi...  15.2 us
    ppermute x14, waiting for transfers between devices, from_partner(): lax.ppermute(value, axis, [(i, i ^ flip) for i in range(lax.axis_size(axi...  11.6 us
    pallas_call x1, Pallas kernels, per_device(): pl.pallas_call(functools.partial(products_kernel, layers), out_shape=[jax...  1.48 us
    pallas_call x1, Pallas kernels, per_device(): pl.pallas_call(functools.partial(pack_kernel, width, group, chunks), out_...  1.38 us
    pallas_call x2, Pallas kernels, per_device(): pl.pallas_call(functools.partial(grads_kernel, layers, bottle, width, gro...  1.04 us
    slice x1, local copies, waits for them, and re-layouts, per_device(): return (total[0][None], total[1][None])  0.66 us
  transfers between devices with their start and end apart: 14, of which 8 were waited for; matrix products, arithmetic and copies ran while one was open for 0% of the time, Pallas kernels for 12%

profile of v4, /device:TPU:0, one launch (start us, length us, event | category | flops | bytes accessed | tf_op | source)
XLA Modules:
  0.0 32.7 jit_solution(1231600470822078100)
XLA Ops:
  0.6 0.5 %collective-permute-start.1 = (bf16[1,64,4096]{2,1,0:T(8,128)(2,1)}, bf16[1,64,4096]{2,1,0:T(8,128)(2,1)S(1)}, u32[]{:S(2)}, u32[]{:S(2)}) collective-permute-start(bf16[1,64,4096]{2,1,0:T(8,128)(2,1)} %refs_1_.3), channel_id=1, source_target_pairs={{0,16},{16,0},{1,17},{17,1},{2,18},{18,2},{3,19},{19,3},{4,20},{20... | collective-permute-start | bytes 1572872 | tf_op jit(solution)/shard_map/ppermute | solution.py:29
  1.2 0.4 %collective-permute-start = (bf16[1,1,4096]{2,1,0:T(2,128)(2,1)}, bf16[1,1,4096]{2,1,0:T(2,128)(2,1)S(1)}, u32[]{:S(2)}, u32[]{:S(2)}) collective-permute-start(bf16[1,1,4096]{2,1,0:T(2,128)(2,1)} %bitcast.1), channel_id=1, source_target_pairs={{0,16},{16,0},{1,17},{17,1},{2,18},{18,2},{3,19},{19,3},{4,20},{20... | collective-permute-start | bytes 24584 | tf_op jit(solution)/shard_map/ppermute | solution.py:29
  1.7 1.4 %pack.1 = (bf16[2,128,2048]{2,1,0:T(8,128)(2,1)S(1)}, bf16[1,1,4096]{2,1,0:T(2,128)(2,1)S(1)}, bf16[2,128,512]{2,1,0:T(8,128)(2,1)S(1)}, bf16[2,128,512]{2,1,0:T...) custom-call(bf16[2,32,2048]{2,1,0:T(8,128)(2,1)} %refs_0_.1, ...), custom_call_target="tpu_custom_call" | custom-call | tf_op jit(solution)/shard_map/pack/pallas_call | solution.py:410
  3.0 2.7 %collective-permute-start.7 = (bf16[2,128,512]{2,1,0:T(8,128)(2,1)S(1)}, bf16[2,128,512]{2,1,0:T(8,128)(2,1)S(1)}, u32[]{:S(2)}, u32[]{:S(2)}) collective-permute-start(bf16[2,128,512]{2,1,0:T(8,128)(2,1)S(1)} %get-tuple-element.24), channel_id=1, source_target_pairs={{0,1},{1,0},{2,3},{3,2},{4,5},{5,4},{6,7},{7,6},{8,9},{9,8},{10,11... | collective-permute-start | bytes 786440 | tf_op jit(solution)/shard_map/ppermute | solution.py:29
  5.8 1.5 %collective-permute-start.8 = (bf16[2,128,512]{2,1,0:T(8,128)(2,1)S(1)}, bf16[2,128,512]{2,1,0:T(8,128)(2,1)S(1)}, u32[]{:S(2)}, u32[]{:S(2)}) collective-permute-start(bf16[2,128,512]{2,1,0:T(8,128)(2,1)S(1)} %get-tuple-element.25), channel_id=1, source_target_pairs={{0,2},{1,3},{2,0},{3,1},{4,6},{5,7},{6,4},{7,5},{8,10},{9,11},{10,... | collective-permute-start | bytes 786440 | tf_op jit(solution)/shard_map/ppermute | solution.py:29
  7.3 1.6 %collective-permute-start.9 = (bf16[2,128,512]{2,1,0:T(8,128)(2,1)S(1)}, bf16[2,128,512]{2,1,0:T(8,128)(2,1)S(1)}, u32[]{:S(2)}, u32[]{:S(2)}) collective-permute-start(bf16[2,128,512]{2,1,0:T(8,128)(2,1)S(1)} %get-tuple-element.26), channel_id=1, source_target_pairs={{0,4},{1,5},{2,6},{3,7},{4,0},{5,1},{6,2},{7,3},{8,12},{9,13},{10,... | collective-permute-start | bytes 786440 | tf_op jit(solution)/shard_map/ppermute | solution.py:29
  8.9 1.5 %products.1.refs_0_ = f32[392,128]{1,0:T(8,128)S(1)} custom-call(bf16[2,128,2048]{2,1,0:T(8,128)(2,1)S(1)} %get-tuple-element.21.refs_0_, bf16[1,1,4096]{2,1,0:T(2,128)(2,1)S(1)} %get-tuple-element.22.refs_1_.refs_0_, bf16[1,64,4096]{2,1,0:T(8,128)(2,1)S(1)} %copy-done, bf16[1,64,4096]{2,1,0:T(8,128)(2,1)S(1)} %copy-done.1, ...), custom_call_target="tpu_custom_call" | custom-call | flops 13200000000 | tf_op jit(solution)/shard_map/products/pallas_call | solution.py:443
  10.4 1.4 %collective-permute-done.3.refs_1_ = f32[392,128]{1,0:T(8,128)S(1)} collective-permute-done((f32[392,128]{1,0:T(8,128)S(1)}, f32[392,128]{1,0:T(8,128)S(1)}, u32[]{:S(2)}, u32[]{:S(2)}) %collective-permute-start.3) | collective-permute-done | bytes 200736 | tf_op jit(solution)/shard_map/ppermute | solution.py:29
  11.9 0.4 %relay.1.refs_0_ = bf16[208,128]{1,0:T(8,128)(2,1)S(1)} custom-call(f32[392,128]{1,0:T(8,128)S(1)} %products.1.refs_0_, f32[392,128]{1,0:T(8,128)S(1)} %collective-permute-done.3.refs_1_), custom_call_target="tpu_custom_call" | custom-call | flops 110000000 | tf_op jit(solution)/shard_map/relay/pallas_call | solution.py:459
  12.3 0.5 %collective-permute-start.6 = (bf16[208,128]{1,0:T(8,128)(2,1)S(1)}, bf16[208,128]{1,0:T(8,128)(2,1)S(1)}, u32[]{:S(2)}, u32[]{:S(2)}) collective-permute-start(bf16[208,128]{1,0:T(8,128)(2,1)S(1)} %relay.1.refs_0_), channel_id=1, source_target_pairs={{0,4},{1,5},{2,6},{3,7},{4,0},{5,1},{6,2},{7,3},{8,12},{9,13},{10,... | collective-permute-start | bytes 159752 | tf_op jit(solution)/shard_map/ppermute | solution.py:29
  12.8 0.5 %collective-permute-start.5 = (bf16[208,128]{1,0:T(8,128)(2,1)S(1)}, bf16[208,128]{1,0:T(8,128)(2,1)S(1)}, u32[]{:S(2)}, u32[]{:S(2)}) collective-permute-start(bf16[208,128]{1,0:T(8,128)(2,1)S(1)} %relay.1.refs_0_), channel_id=1, source_target_pairs={{0,2},{1,3},{2,0},{3,1},{4,6},{5,7},{6,4},{7,5},{8,10},{9,11},{10,... | collective-permute-start | bytes 159752 | tf_op jit(solution)/shard_map/ppermute | solution.py:29
  13.3 1.0 %collective-permute-start.4 = (bf16[208,128]{1,0:T(8,128)(2,1)S(1)}, bf16[208,128]{1,0:T(8,128)(2,1)S(1)}, u32[]{:S(2)}, u32[]{:S(2)}) collective-permute-start(bf16[208,128]{1,0:T(8,128)(2,1)S(1)} %relay.1.refs_0_), channel_id=1, source_target_pairs={{0,1},{1,0},{2,3},{3,2},{4,5},{5,4},{6,7},{7,6},{8,9},{9,8},{10,11... | collective-permute-start | bytes 159752 | tf_op jit(solution)/shard_map/ppermute | solution.py:29
  14.3 1.1 %collective-permute-done.9.refs_7_.refs_3_ = bf16[2,128,512]{2,1,0:T(8,128)(2,1)S(1)} collective-permute-done((bf16[2,128,512]{2,1,0:T(8,128)(2,1)S(1)}, bf16[2,128,512]{2,1,0:T(8,128)(2,1)S(1)}, u32[]{:S(2)}, u32[]{:S(2)}) %collective-permute-start.9) | collective-permute-done | bytes 262176 | tf_op jit(solution)/shard_map/ppermute | solution.py:29
  15.7 0.8 %collective-permute-done.6.refs_3_ = bf16[208,128]{1,0:T(8,128)(2,1)S(1)} collective-permute-done((bf16[208,128]{1,0:T(8,128)(2,1)S(1)}, bf16[208,128]{1,0:T(8,128)(2,1)S(1)}, u32[]{:S(2)}, u32[]{:S(2)}) %collective-permute-start.6) | collective-permute-done | bytes 53280 | tf_op jit(solution)/shard_map/ppermute | solution.py:29
  16.5 0.4 %collective-permute-done.5.refs_2_ = bf16[208,128]{1,0:T(8,128)(2,1)S(1)} collective-permute-done((bf16[208,128]{1,0:T(8,128)(2,1)S(1)}, bf16[208,128]{1,0:T(8,128)(2,1)S(1)}, u32[]{:S(2)}, u32[]{:S(2)}) %collective-permute-start.5) | collective-permute-done | bytes 53280 | tf_op jit(solution)/shard_map/ppermute | solution.py:29
  16.9 0.5 %collective-permute-done.4.refs_1_ = bf16[208,128]{1,0:T(8,128)(2,1)S(1)} collective-permute-done((bf16[208,128]{1,0:T(8,128)(2,1)S(1)}, bf16[208,128]{1,0:T(8,128)(2,1)S(1)}, u32[]{:S(2)}, u32[]{:S(2)}) %collective-permute-start.4) | collective-permute-done | bytes 53280 | tf_op jit(solution)/shard_map/ppermute | solution.py:29
  17.4 0.5 %grads.2 = (f32[2,2,64,256]{3,2,1,0:T(8,128)S(1)}, bf16[4,256,128]{2,1,0:T(8,128)(2,1)S(1)}, bf16[2,64,64]{2,1,0:T(8,128)(2,1)S(1)}) custom-call(bf16[208,128]{1,0:T(8,128)(2,1)S(1)} %relay.1.refs_0_, bf16[208,128]{1,0:T(8,128)(2,1)S(1)} %collective-permute-done.4.refs_1_, bf16[208,128]{1,0:T(8,128)(2,1)S(1)} %collective-permute-done.5.refs_2_, ...), custom_call_target="tpu_custom_call" | custom-call | flops 11000000512 | tf_op jit(solution)/shard_map/grads/pallas_call | solution.py:539
  18.2 0.5 %grads.3 = (f32[2,64,256]{2,1,0:T(8,128)S(1)}, bf16[2,64,256]{2,1,0:T(8,128)(2,1)S(1)}, bf16[2,64,256]{2,1,0:T(8,128)(2,1)S(1)}, bf16[2,64,256]{2,1,0:T(8,128)(2,1)S(1)}) custom-call(bf16[4,256,128]{2,1,0:T(8,128)(2,1)S(1)} %get-tuple-element.29.refs_0_, bf16[2,64,64]{2,1,0:T(8,128)(2,1)S(1)} %get-tuple-element.30.refs_1_, ...), custom_call_target="tpu_custom_call" | custom-call | flops 11000000512 | tf_op jit(solution)/shard_map/grads/pallas_call | solution.py:539
  18.7 2.8 %collective-permute-start.11 = (bf16[2,64,256]{2,1,0:T(8,128)(2,1)S(1)}, bf16[2,64,256]{2,1,0:T(8,128)(2,1)S(1)}, u32[]{:S(2)}, u32[]{:S(2)}) collective-permute-start(bf16[2,64,256]{2,1,0:T(8,128)(2,1)S(1)} %get-tuple-element.37), channel_id=1, source_target_pairs={{0,7},{1,6},{2,5},{3,4},{4,3},{5,2},{6,1},{7,0},{8,15},{9,14},{10,... | collective-permute-start | bytes 196616 | tf_op jit(solution)/shard_map/ppermute | solution.py:29
  21.6 2.6 %collective-permute-start.12 = (bf16[2,64,256]{2,1,0:T(8,128)(2,1)S(1)}, bf16[2,64,256]{2,1,0:T(8,128)(2,1)S(1)}, u32[]{:S(2)}, u32[]{:S(2)}) collective-permute-start(bf16[2,64,256]{2,1,0:T(8,128)(2,1)S(1)} %get-tuple-element.38), channel_id=1, source_target_pairs={{0,8},{1,9},{2,10},{3,11},{4,12},{5,13},{6,14},{7,15},{8,0},{9,1},... | collective-permute-start | bytes 196616 | tf_op jit(solution)/shard_map/ppermute | solution.py:29
  24.2 0.8 %collective-permute-start.13 = (bf16[2,64,256]{2,1,0:T(8,128)(2,1)S(1)}, bf16[2,64,256]{2,1,0:T(8,128)(2,1)S(1)}, u32[]{:S(2)}, u32[]{:S(2)}) collective-permute-start(bf16[2,64,256]{2,1,0:T(8,128)(2,1)S(1)} %get-tuple-element.39), channel_id=1, source_target_pairs={{0,15},{1,14},{2,13},{3,12},{4,11},{5,10},{6,9},{7,8},{8,7},{9,6},... | collective-permute-start | bytes 196616 | tf_op jit(solution)/shard_map/ppermute | solution.py:29
  25.0 2.8 %collective-permute-done.12 = bf16[2,64,256]{2,1,0:T(8,128)(2,1)S(1)} collective-permute-done((bf16[2,64,256]{2,1,0:T(8,128)(2,1)S(1)}, bf16[2,64,256]{2,1,0:T(8,128)(2,1)S(1)}, u32[]{:S(2)}, u32[]{:S(2)}) %collective-permute-start.12) | collective-permute-done | bytes 65568 | tf_op jit(solution)/shard_map/ppermute | solution.py:29
  27.8 4.2 %collective-permute-done.13 = bf16[2,64,256]{2,1,0:T(8,128)(2,1)S(1)} collective-permute-done((bf16[2,64,256]{2,1,0:T(8,128)(2,1)S(1)}, bf16[2,64,256]{2,1,0:T(8,128)(2,1)S(1)}, u32[]{:S(2)}, u32[]{:S(2)}) %collective-permute-start.13) | collective-permute-done | bytes 65568 | tf_op jit(solution)/shard_map/ppermute | solution.py:29
  32.0 0.7 %fusion = (f32[1,64,256]{2,1,0:T(8,128)}, f32[1,64,256]{2,1,0:T(8,128)}) fusion(f32[2,64,256]{2,1,0:T(8,128)S(1)} %convert_add_fusion), kind=kLoop, calls=%fused_computation.1 | loop fusion | bytes 262144 | tf_op jit(solution)/shard_map/slice | solution.py:564
  (17 shorter events, 0.7 us)
Async XLA Ops:
  0.6 8.2 %collective-permute-start.1 = (bf16[1,64,4096]{2,1,0:T(8,128)(2,1)}, bf16[1,64,4096]{2,1,0:T(8,128)(2,1)S(1)}, u32[]{:S(2)}, u32[]{:S(2)}) collective-permute-start(bf16[1,64,4096]{2,1,0:T(8,128)(2,1)} %refs_1_.3), channel_id=1, source_target_pairs={{0,16},{16,0},{1,17},{17,1},{2,18},{18,2},{3,19},{19,3},{4,20},{20... | collective-permute-start | bytes 1572872 | tf_op jit(solution)/shard_map/ppermute | solution.py:29
  1.1 7.7 %collective-permute-start.2 = (bf16[1,64,4096]{2,1,0:T(8,128)(2,1)}, bf16[1,64,4096]{2,1,0:T(8,128)(2,1)S(1)}, u32[]{:S(2)}, u32[]{:S(2)}) collective-permute-start(bf16[1,64,4096]{2,1,0:T(8,128)(2,1)} %refs_2_.5), channel_id=1, source_target_pairs={{0,16},{16,0},{1,17},{17,1},{2,18},{18,2},{3,19},{19,3},{4,20},{20... | collective-permute-start | bytes 1572872 | tf_op jit(solution)/shard_map/ppermute | solution.py:29
  1.2 7.6 %copy-start = (bf16[1,64,4096]{2,1,0:T(8,128)(2,1)S(1)}, bf16[1,64,4096]{2,1,0:T(8,128)(2,1)}, u32[]{:S(2)}) copy-start(bf16[1,64,4096]{2,1,0:T(8,128)(2,1)} %refs_1_.3) | copy-start | bytes 1572868
  1.2 7.6 %copy-start.1 = (bf16[1,64,4096]{2,1,0:T(8,128)(2,1)S(1)}, bf16[1,64,4096]{2,1,0:T(8,128)(2,1)}, u32[]{:S(2)}) copy-start(bf16[1,64,4096]{2,1,0:T(8,128)(2,1)} %refs_2_.5) | copy-start | bytes 1572868
  1.2 6.0 %collective-permute-start = (bf16[1,1,4096]{2,1,0:T(2,128)(2,1)}, bf16[1,1,4096]{2,1,0:T(2,128)(2,1)S(1)}, u32[]{:S(2)}, u32[]{:S(2)}) collective-permute-start(bf16[1,1,4096]{2,1,0:T(2,128)(2,1)} %bitcast.1), channel_id=1, source_target_pairs={{0,16},{16,0},{1,17},{17,1},{2,18},{18,2},{3,19},{19,3},{4,20},{20... | collective-permute-start | bytes 24584 | tf_op jit(solution)/shard_map/ppermute | solution.py:29
  3.0 10.2 %collective-permute-start.7 = (bf16[2,128,512]{2,1,0:T(8,128)(2,1)S(1)}, bf16[2,128,512]{2,1,0:T(8,128)(2,1)S(1)}, u32[]{:S(2)}, u32[]{:S(2)}) collective-permute-start(bf16[2,128,512]{2,1,0:T(8,128)(2,1)S(1)} %get-tuple-element.24), channel_id=1, source_target_pairs={{0,1},{1,0},{2,3},{3,2},{4,5},{5,4},{6,7},{7,6},{8,9},{9,8},{10,11... | collective-permute-start | bytes 786440 | tf_op jit(solution)/shard_map/ppermute | solution.py:29
  5.8 8.6 %collective-permute-start.8 = (bf16[2,128,512]{2,1,0:T(8,128)(2,1)S(1)}, bf16[2,128,512]{2,1,0:T(8,128)(2,1)S(1)}, u32[]{:S(2)}, u32[]{:S(2)}) collective-permute-start(bf16[2,128,512]{2,1,0:T(8,128)(2,1)S(1)} %get-tuple-element.25), channel_id=1, source_target_pairs={{0,2},{1,3},{2,0},{3,1},{4,6},{5,7},{6,4},{7,5},{8,10},{9,11},{10,... | collective-permute-start | bytes 786440 | tf_op jit(solution)/shard_map/ppermute | solution.py:29
  7.3 8.2 %collective-permute-start.9 = (bf16[2,128,512]{2,1,0:T(8,128)(2,1)S(1)}, bf16[2,128,512]{2,1,0:T(8,128)(2,1)S(1)}, u32[]{:S(2)}, u32[]{:S(2)}) collective-permute-start(bf16[2,128,512]{2,1,0:T(8,128)(2,1)S(1)} %get-tuple-element.26), channel_id=1, source_target_pairs={{0,4},{1,5},{2,6},{3,7},{4,0},{5,1},{6,2},{7,3},{8,12},{9,13},{10,... | collective-permute-start | bytes 786440 | tf_op jit(solution)/shard_map/ppermute | solution.py:29
  10.4 1.5 %collective-permute-start.3 = (f32[392,128]{1,0:T(8,128)S(1)}, f32[392,128]{1,0:T(8,128)S(1)}, u32[]{:S(2)}, u32[]{:S(2)}) collective-permute-start(f32[392,128]{1,0:T(8,128)S(1)} %products.1.refs_0_), channel_id=1, source_target_pairs={{0,16},{16,0},{1,17},{17,1},{2,18},{18,2},{3,19},{19,3},{4,20},{20... | collective-permute-start | bytes 602120 | tf_op jit(solution)/shard_map/ppermute | solution.py:29
  12.3 4.2 %collective-permute-start.6 = (bf16[208,128]{1,0:T(8,128)(2,1)S(1)}, bf16[208,128]{1,0:T(8,128)(2,1)S(1)}, u32[]{:S(2)}, u32[]{:S(2)}) collective-permute-start(bf16[208,128]{1,0:T(8,128)(2,1)S(1)} %relay.1.refs_0_), channel_id=1, source_target_pairs={{0,4},{1,5},{2,6},{3,7},{4,0},{5,1},{6,2},{7,3},{8,12},{9,13},{10,... | collective-permute-start | bytes 159752 | tf_op jit(solution)/shard_map/ppermute | solution.py:29
  12.8 4.1 %collective-permute-start.5 = (bf16[208,128]{1,0:T(8,128)(2,1)S(1)}, bf16[208,128]{1,0:T(8,128)(2,1)S(1)}, u32[]{:S(2)}, u32[]{:S(2)}) collective-permute-start(bf16[208,128]{1,0:T(8,128)(2,1)S(1)} %relay.1.refs_0_), channel_id=1, source_target_pairs={{0,2},{1,3},{2,0},{3,1},{4,6},{5,7},{6,4},{7,5},{8,10},{9,11},{10,... | collective-permute-start | bytes 159752 | tf_op jit(solution)/shard_map/ppermute | solution.py:29
  13.3 4.1 %collective-permute-start.4 = (bf16[208,128]{1,0:T(8,128)(2,1)S(1)}, bf16[208,128]{1,0:T(8,128)(2,1)S(1)}, u32[]{:S(2)}, u32[]{:S(2)}) collective-permute-start(bf16[208,128]{1,0:T(8,128)(2,1)S(1)} %relay.1.refs_0_), channel_id=1, source_target_pairs={{0,1},{1,0},{2,3},{3,2},{4,5},{5,4},{6,7},{7,6},{8,9},{9,8},{10,11... | collective-permute-start | bytes 159752 | tf_op jit(solution)/shard_map/ppermute | solution.py:29
  15.5 2.7 %collective-permute-start.10 = (bf16[4,2,128,512]{3,2,1,0:T(8,128)(2,1)S(1)}, bf16[4,2,128,512]{3,2,1,0:T(8,128)(2,1)S(1)}, u32[]{:S(2)}, u32[]{:S(2)}) collective-permute-start(bf16[4,2,128,512]{3,2,1,0:T(8,128)(2,1)S(1)} %stack.1), channel_id=1, source_target_pairs={{0,16},{16,0},{1,17},{17,1},{2,18},{18,2},{3,19},{19,3},{4,20},{20... | collective-permute-start | bytes 3145736 | tf_op jit(solution)/shard_map/ppermute | solution.py:29
  18.7 6.3 %collective-permute-start.11 = (bf16[2,64,256]{2,1,0:T(8,128)(2,1)S(1)}, bf16[2,64,256]{2,1,0:T(8,128)(2,1)S(1)}, u32[]{:S(2)}, u32[]{:S(2)}) collective-permute-start(bf16[2,64,256]{2,1,0:T(8,128)(2,1)S(1)} %get-tuple-element.37), channel_id=1, source_target_pairs={{0,7},{1,6},{2,5},{3,4},{4,3},{5,2},{6,1},{7,0},{8,15},{9,14},{10,... | collective-permute-start | bytes 196616 | tf_op jit(solution)/shard_map/ppermute | solution.py:29
  21.6 6.2 %collective-permute-start.12 = (bf16[2,64,256]{2,1,0:T(8,128)(2,1)S(1)}, bf16[2,64,256]{2,1,0:T(8,128)(2,1)S(1)}, u32[]{:S(2)}, u32[]{:S(2)}) collective-permute-start(bf16[2,64,256]{2,1,0:T(8,128)(2,1)S(1)} %get-tuple-element.38), channel_id=1, source_target_pairs={{0,8},{1,9},{2,10},{3,11},{4,12},{5,13},{6,14},{7,15},{8,0},{9,1},... | collective-permute-start | bytes 196616 | tf_op jit(solution)/shard_map/ppermute | solution.py:29
  24.2 7.9 %collective-permute-start.13 = (bf16[2,64,256]{2,1,0:T(8,128)(2,1)S(1)}, bf16[2,64,256]{2,1,0:T(8,128)(2,1)S(1)}, u32[]{:S(2)}, u32[]{:S(2)}) collective-permute-start(bf16[2,64,256]{2,1,0:T(8,128)(2,1)S(1)} %get-tuple-element.39), channel_id=1, source_target_pairs={{0,15},{1,14},{2,13},{3,12},{4,11},{5,10},{6,9},{7,8},{8,7},{9,6},... | collective-permute-start | bytes 196616 | tf_op jit(solution)/shard_map/ppermute | solution.py:29

commit v5 on v4

--- a/solution.py
+++ b/solution.py
@@ -87,11 +87,12 @@
 
 
 def pack_kernel(width, group, chunks, *refs):
-    acts, gain = refs[:4], refs[4]
-    both, gain_out = refs[5:7]
-    outs = refs[7:-1]
-    sems = refs[-1]
+    acts, gain, down = refs[:4], refs[4], refs[5]
+    both, tall = refs[6:8]
+    outs = refs[8:-2]
+    line, sems = refs[-2:]
     micro, tokens = acts[0].shape[0], acts[0].shape[1]
+    bottle = down.shape[1]
     section, label, _ = whereabouts(group, chunks)
     copies = []
     for a, act in enumerate(acts):
@@ -102,11 +103,15 @@
                     act.at[m], both.at[a // 2, pl.ds(start, tokens)], sems.at[len(copies)]
                 )
             )
-            copies[-1].start()
-    last = pltpu.make_async_copy(gain, gain_out, sems.at[len(copies)])
-    last.start()
-    for n, copy in enumerate(copies):
-        copy.wait()
+    count = len(copies)
+    copies.append(pltpu.make_async_copy(gain.at[0], line, sems.at[count]))
+    copies.append(
+        pltpu.make_async_copy(down.at[0], tall.at[pl.ds(0, bottle)], sems.at[count + 1])
+    )
+    for copy in copies:
+        copy.start()
+    for n in range(count):
+        copies[n].wait()
         a, m = divmod(n, micro)
         start = ((a % 2) * micro + m) * tokens
         for k, out in enumerate(outs):
@@ -116,7 +121,9 @@
                 out[a // 2, start : start + tokens, part * width : (part + 1) * width] = both[
                     a // 2, start : start + tokens, span
                 ]
-    last.wait()
+    copies[count].wait()
+    tall[bottle:] = jnp.broadcast_to(line[...], (tall.shape[0] - bottle, tall.shape[1]))
+    copies[count + 1].wait()
 
 
 def two_parts(refs):
@@ -128,18 +135,19 @@
 
 def products_kernel(layers, *refs):
     acts = refs[0]
-    weights = [refs[1 + 3 * k : 4 + 3 * k] for k in range(layers)]
-    outs = refs[1 + 3 * layers : -3]
+    weights = [refs[1 + 2 * k : 3 + 2 * k] for k in range(layers)]
+    outs = refs[1 + 2 * layers : -3]
     prod_out, gram_out = two_parts(outs)
     low_scr, fine_scr, high_scr = refs[-3:]
     bottle = weights[0][1].shape[1]
+    gain_row = slice(bottle, bottle + 1)
     features = acts.shape[2]
     section = lax.axis_index("section")
     mine = pl.ds(pl.multiple_of(section * features, features), features)
     for k in range(layers):
-        gain, down, up = weights[k]
+        tall, up = weights[k]
         layer = section ^ k
-        exact = gain[0, :, mine].astype(f32) * down[0, :, mine].astype(f32)
+        exact = tall[gain_row, mine].astype(f32) * tall[:bottle, mine].astype(f32)
         low, fine = split(exact)
         low_scr[layer] = low
         fine_scr[layer] = fine
@@ -262,8 +270,10 @@
 
 
 def cut_kernel(layers, width, group, chunks, *refs):
-    weights = [refs[3 * k : 3 * k + 3] for k in range(layers)]
-    gain_out, both_out = refs[3 * layers :]
+    weights = [refs[2 * k : 2 * k + 2] for k in range(layers)]
+    gain_out, both_out = refs[2 * layers :]
+    bottle = weights[0][1].shape[1]
+    gain_row = slice(bottle, bottle + 1)
     here_section, label, _ = whereabouts(group, chunks)
     for k in range(layers):
         section = here_section ^ k
@@ -271,11 +281,11 @@
             chunk = section * chunks + chunk_of(label, part, section)
             span = pl.ds(pl.multiple_of(chunk * width, width), width)
             here = slice(part * width, (part + 1) * width)
-            gain_out[k, :, here] = weights[0][0][0, :, span].astype(f32)
+            gain_out[k, :, here] = weights[0][0][gain_row, span].astype(f32)
             for w in range(layers):
-                gain, down, up = weights[w]
+                tall, up = weights[w]
                 layer = here_section ^ w
-                low = gain[0, :, span].astype(f32) * down[0, :, span].astype(f32)
+                low = tall[gain_row, span].astype(f32) * tall[:bottle, span].astype(f32)
                 both_out[k, layer, :, here] = low.astype(bf16)
                 both_out[k, layers + layer, :, here] = up[0, :, span]
 
@@ -401,24 +411,29 @@
     aligned = width % 128 == 0
     params = pltpu.CompilerParams(vmem_limit_bytes=VMEM_BYTES)
 
-    own = (norm_gains[:, None, :], adapt_down, adapt_up)
-    weights = [own]
-    for k in range(1, sections):
-        weights.append(tuple(from_partner(w, "section", k) for w in own))
     acts = (inputs_down, inputs_up, cotan_down, cotan_up)
     if aligned:
-        both, gain, *packed = pl.pallas_call(
+        taken = (*acts, norm_gains[:, None, :], adapt_down)
+        both, tall, *packed = pl.pallas_call(
             functools.partial(pack_kernel, width, group, chunks),
-            out_shape=[pltpu.VMEM((2, rows, share), bf16), pltpu.VMEM(own[0].shape, bf16)]
+            out_shape=[
+                pltpu.VMEM((2, rows, share), bf16),
+                pltpu.VMEM((bottle + 16, features), bf16),
+            ]
             + [pltpu.VMEM((2, rows, columns), bf16)] * MEMBERS,
-            in_specs=[IN_HBM] * 5,
+            in_specs=[IN_HBM] * 6,
             out_specs=[IN_VMEM] * (2 + MEMBERS),
-            scratch_shapes=[pltpu.SemaphoreType.DMA((4 * micro + 1,))],
+            scratch_shapes=[
+                pltpu.VMEM((1, features), bf16),
+                pltpu.SemaphoreType.DMA((4 * micro + 2,)),
+            ],
             compiler_params=params,
             name="pack",
-        )(*[pltpu.with_memory_space_constraint(v, pltpu.HBM) for v in (*acts, own[0])])
-        weights[0] = (gain, *own[1:])
+        )(*[pltpu.with_memory_space_constraint(v, pltpu.HBM) for v in taken])
     else:
+        tall = jnp.concatenate(
+            [adapt_down[0], jnp.broadcast_to(norm_gains, (16, features))], axis=0
+        )
         both = jnp.concatenate([v.reshape(half, share) for v in acts], axis=0)
         both = both.reshape(2, rows, share)
         parts = both.reshape(2, rows, chunks, width)
@@ -431,6 +446,11 @@
                 for part in range(group)
             ]
             packed.append(jnp.concatenate(cuts, axis=2))
+
+    own = (tall, lax.optimization_barrier((adapt_up, packed[1]))[0])
+    weights = [(tall, adapt_up)]
+    for k in range(1, sections):
+        weights.append(tuple(from_partner(w, "section", k) for w in own))
     flat = [w for ws in weights for w in ws]
     pieces = [packed[0]]
     for k in range(1, MEMBERS):
@@ -443,7 +463,7 @@
     sums = pl.pallas_call(
         functools.partial(products_kernel, layers),
         out_shape=[jax.ShapeDtypeStruct(side, f32) for side in sides],
-        in_specs=[IN_VMEM] * (1 + 3 * sections),
+        in_specs=[IN_VMEM] * (1 + 2 * sections),
         out_specs=[IN_VMEM] * len(sides),
         scratch_shapes=[pltpu.VMEM((layers, bottle, share), bf16)] * 3,
         compiler_params=params,
@@ -489,12 +509,13 @@
                 at = section ^ k
                 chunk = at * chunks + chunk_of(label, part, at)
                 for w, ws in enumerate(weights):
-                    gain, down, up = (
+                    down, up = (
                         lax.dynamic_index_in_dim(
-                            v[0].reshape(v.shape[1], replicas, width), chunk, 1, keepdims=False
+                            v.reshape(-1, replicas, width), chunk, 1, keepdims=False
                         )
                         for v in ws
                     )
+                    down, gain = down[:bottle], down[bottle : bottle + 1]
                     low = (gain.astype(f32) * down.astype(f32)).astype(bf16)
                     layer = section ^ w
                     spot = (k, layer, 0, part * width)
@@ -558,7 +579,7 @@
         parcels[1:] = [v.astype(bf16) for v in parcels[1:]]
 
     total = parcels[0]
-    for r in range(1, slots):
+    for r in (*range(slots // 2, slots), *range(1, slots // 2)):
         received = from_partner(parcels[r], "dp", mask(r, group, chunks))
         total = total + received.astype(f32)
     return (total[0][None], total[1][None])

time: 32.9 us -> 31.3 us (0.951)
  starting transfers between devices: 15.2 us -> 14 us
  waiting for transfers between devices: 11.6 us -> 11.1 us
    ppermute x14 -> x13, starting transfers between devices: 15.2 us -> 14 us  [from_partner(): lax.ppermute(value, axis, [(i, i ^ flip) for i in range(lax.axis_size(axi...]
    ppermute x14 -> x13, waiting for transfers between devices: 11.6 us -> 11.1 us  [from_partner(): lax.ppermute(value, axis, [(i, i ^ flip) for i in range(lax.axis_size(axi...]
  transfers between devices with their start and end apart: 14 -> 13, of which waited for: 8 -> 9; matrix products, arithmetic and copies ran while one was open for 0% -> 0% of each run, Pallas kernels for 12% -> 8%
where the time goes in v5:
time: 31.3 us; the launch traced here: 31.1 us
  starting transfers between devices  14 us (45%)
  waiting for transfers between devices  11.1 us (35%)
  Pallas kernels  4.68 us (15%)
  between operations  0.72 us (2%)
  local copies, waits for them, and re-layouts  0.66 us (2%)
    ppermute x13, starting transfers between devices, from_partner(): lax.ppermute(value, axis, [(i, i ^ flip) for i in range(lax.axis_size(axi...  14 us
    ppermute x13, waiting for transfers between devices, from_partner(): lax.ppermute(value, axis, [(i, i ^ flip) for i in range(lax.axis_size(axi...  11.1 us
    pallas_call x1, Pallas kernels, per_device(): pl.pallas_call(functools.partial(pack_kernel, width, group, chunks), out_...  1.6 us
    pallas_call x1, Pallas kernels, per_device(): pl.pallas_call(functools.partial(products_kernel, layers), out_shape=[jax...  1.46 us
    pallas_call x2, Pallas kernels, per_device(): pl.pallas_call(functools.partial(grads_kernel, layers, bottle, width, gro...  1.03 us
    slice x1, local copies, waits for them, and re-layouts, per_device(): return (total[0][None], total[1][None])  0.66 us
  transfers between devices with their start and end apart: 13, of which 9 were waited for; matrix products, arithmetic and copies ran while one was open for 0% of the time, Pallas kernels for 8%

profile of v5, /device:TPU:0, one launch (start us, length us, event | category | flops | bytes accessed | tf_op | source)
XLA Modules:
  0.0 31.1 jit_solution(6472506786948142099)
XLA Ops:
  0.6 1.6 %pack.1 = (bf16[2,128,2048]{2,1,0:T(8,128)(2,1)S(1)}, bf16[80,4096]{1,0:T(8,128)(2,1)S(1)}, bf16[2,128,512]{2,1,0:T(8,128)(2,1)S(1)}, bf16[2,128,512]{2,1,0:T(8,...) custom-call(bf16[2,32,2048]{2,1,0:T(8,128)(2,1)} %refs_0_.1, ...), custom_call_target="tpu_custom_call" | custom-call | tf_op jit(solution)/shard_map/pack/pallas_call | solution.py:417
  2.3 0.5 %collective-permute-start = (bf16[80,4096]{1,0:T(8,128)(2,1)S(1)}, bf16[80,4096]{1,0:T(8,128)(2,1)S(1)}, u32[]{:S(2)}, u32[]{:S(2)}) collective-permute-start(bf16[80,4096]{1,0:T(8,128)(2,1)S(1)} %get-tuple-element.23.refs_1_.refs_0_), channel_id=1, source_target_pairs={{0,16},{16,0},{1,17},{17,1},{2,18},{18,2},{3,19},{19,3},{4,20},{20... | collective-permute-start | bytes 1966088 | tf_op jit(solution)/shard_map/ppermute | solution.py:29
  2.9 2.9 %collective-permute-start.6 = (bf16[2,128,512]{2,1,0:T(8,128)(2,1)S(1)}, bf16[2,128,512]{2,1,0:T(8,128)(2,1)S(1)}, u32[]{:S(2)}, u32[]{:S(2)}) collective-permute-start(bf16[2,128,512]{2,1,0:T(8,128)(2,1)S(1)} %get-tuple-element.24), channel_id=1, source_target_pairs={{0,1},{1,0},{2,3},{3,2},{4,5},{5,4},{6,7},{7,6},{8,9},{9,8},{10,11... | collective-permute-start | bytes 786440 | tf_op jit(solution)/shard_map/ppermute | solution.py:29
  5.8 1.5 %collective-permute-start.7 = (bf16[2,128,512]{2,1,0:T(8,128)(2,1)S(1)}, bf16[2,128,512]{2,1,0:T(8,128)(2,1)S(1)}, u32[]{:S(2)}, u32[]{:S(2)}) collective-permute-start(bf16[2,128,512]{2,1,0:T(8,128)(2,1)S(1)} %get-tuple-element.27), channel_id=1, source_target_pairs={{0,2},{1,3},{2,0},{3,1},{4,6},{5,7},{6,4},{7,5},{8,10},{9,11},{10,... | collective-permute-start | bytes 786440 | tf_op jit(solution)/shard_map/ppermute | solution.py:29
  7.3 1.6 %collective-permute-start.8 = (bf16[2,128,512]{2,1,0:T(8,128)(2,1)S(1)}, bf16[2,128,512]{2,1,0:T(8,128)(2,1)S(1)}, u32[]{:S(2)}, u32[]{:S(2)}) collective-permute-start(bf16[2,128,512]{2,1,0:T(8,128)(2,1)S(1)} %get-tuple-element.28), channel_id=1, source_target_pairs={{0,4},{1,5},{2,6},{3,7},{4,0},{5,1},{6,2},{7,3},{8,12},{9,13},{10,... | collective-permute-start | bytes 786440 | tf_op jit(solution)/shard_map/ppermute | solution.py:29
  8.9 1.5 %products.1.refs_0_ = f32[392,128]{1,0:T(8,128)S(1)} custom-call(bf16[2,128,2048]{2,1,0:T(8,128)(2,1)S(1)} %get-tuple-element.22.refs_0_, bf16[80,4096]{1,0:T(8,128)(2,1)S(1)} %get-tuple-element.23.refs_1_.refs_0_, bf16[1,64,4096]{2,1,0:T(8,128)(2,1)S(1)} %copy-done, bf16[80,4096]{1,0:T(8,128)(2,1)S(1)} %collective-permute-done.refs_3_.refs_2_, ...), custom_call_target="tpu_custom_call" | custom-call | flops 13200000000 | tf_op jit(solution)/shard_map/products/pallas_call | solution.py:463
  10.4 1.4 %collective-permute-done.2.refs_1_ = f32[392,128]{1,0:T(8,128)S(1)} collective-permute-done((f32[392,128]{1,0:T(8,128)S(1)}, f32[392,128]{1,0:T(8,128)S(1)}, u32[]{:S(2)}, u32[]{:S(2)}) %collective-permute-start.2) | collective-permute-done | bytes 200736 | tf_op jit(solution)/shard_map/ppermute | solution.py:29
  11.8 0.4 %relay.1.refs_0_ = bf16[208,128]{1,0:T(8,128)(2,1)S(1)} custom-call(f32[392,128]{1,0:T(8,128)S(1)} %products.1.refs_0_, f32[392,128]{1,0:T(8,128)S(1)} %collective-permute-done.2.refs_1_), custom_call_target="tpu_custom_call" | custom-call | flops 110000000 | tf_op jit(solution)/shard_map/relay/pallas_call | solution.py:479
  12.2 0.5 %collective-permute-start.5 = (bf16[208,128]{1,0:T(8,128)(2,1)S(1)}, bf16[208,128]{1,0:T(8,128)(2,1)S(1)}, u32[]{:S(2)}, u32[]{:S(2)}) collective-permute-start(bf16[208,128]{1,0:T(8,128)(2,1)S(1)} %relay.1.refs_0_), channel_id=1, source_target_pairs={{0,4},{1,5},{2,6},{3,7},{4,0},{5,1},{6,2},{7,3},{8,12},{9,13},{10,... | collective-permute-start | bytes 159752 | tf_op jit(solution)/shard_map/ppermute | solution.py:29
  12.8 0.5 %collective-permute-start.4 = (bf16[208,128]{1,0:T(8,128)(2,1)S(1)}, bf16[208,128]{1,0:T(8,128)(2,1)S(1)}, u32[]{:S(2)}, u32[]{:S(2)}) collective-permute-start(bf16[208,128]{1,0:T(8,128)(2,1)S(1)} %relay.1.refs_0_), channel_id=1, source_target_pairs={{0,2},{1,3},{2,0},{3,1},{4,6},{5,7},{6,4},{7,5},{8,10},{9,11},{10,... | collective-permute-start | bytes 159752 | tf_op jit(solution)/shard_map/ppermute | solution.py:29
  13.3 0.5 %collective-permute-done.7.refs_6_.refs_2_ = bf16[2,128,512]{2,1,0:T(8,128)(2,1)S(1)} collective-permute-done((bf16[2,128,512]{2,1,0:T(8,128)(2,1)S(1)}, bf16[2,128,512]{2,1,0:T(8,128)(2,1)S(1)}, u32[]{:S(2)}, u32[]{:S(2)}) %collective-permute-start.7) | collective-permute-done | bytes 262176 | tf_op jit(solution)/shard_map/ppermute | solution.py:29
  13.8 0.9 %collective-permute-start.3 = (bf16[208,128]{1,0:T(8,128)(2,1)S(1)}, bf16[208,128]{1,0:T(8,128)(2,1)S(1)}, u32[]{:S(2)}, u32[]{:S(2)}) collective-permute-start(bf16[208,128]{1,0:T(8,128)(2,1)S(1)} %relay.1.refs_0_), channel_id=1, source_target_pairs={{0,1},{1,0},{2,3},{3,2},{4,5},{5,4},{6,7},{7,6},{8,9},{9,8},{10,11... | collective-permute-start | bytes 159752 | tf_op jit(solution)/shard_map/ppermute | solution.py:29
  14.6 0.4 %collective-permute-done.8.refs_7_.refs_3_ = bf16[2,128,512]{2,1,0:T(8,128)(2,1)S(1)} collective-permute-done((bf16[2,128,512]{2,1,0:T(8,128)(2,1)S(1)}, bf16[2,128,512]{2,1,0:T(8,128)(2,1)S(1)}, u32[]{:S(2)}, u32[]{:S(2)}) %collective-permute-start.8) | collective-permute-done | bytes 262176 | tf_op jit(solution)/shard_map/ppermute | solution.py:29
  15.3 1.1 %collective-permute-done.5.refs_3_ = bf16[208,128]{1,0:T(8,128)(2,1)S(1)} collective-permute-done((bf16[208,128]{1,0:T(8,128)(2,1)S(1)}, bf16[208,128]{1,0:T(8,128)(2,1)S(1)}, u32[]{:S(2)}, u32[]{:S(2)}) %collective-permute-start.5) | collective-permute-done | bytes 53280 | tf_op jit(solution)/shard_map/ppermute | solution.py:29
  16.4 0.5 %collective-permute-done.4.refs_2_ = bf16[208,128]{1,0:T(8,128)(2,1)S(1)} collective-permute-done((bf16[208,128]{1,0:T(8,128)(2,1)S(1)}, bf16[208,128]{1,0:T(8,128)(2,1)S(1)}, u32[]{:S(2)}, u32[]{:S(2)}) %collective-permute-start.4) | collective-permute-done | bytes 53280 | tf_op jit(solution)/shard_map/ppermute | solution.py:29
  16.9 1.0 %collective-permute-done.3.refs_1_ = bf16[208,128]{1,0:T(8,128)(2,1)S(1)} collective-permute-done((bf16[208,128]{1,0:T(8,128)(2,1)S(1)}, bf16[208,128]{1,0:T(8,128)(2,1)S(1)}, u32[]{:S(2)}, u32[]{:S(2)}) %collective-permute-start.3) | collective-permute-done | bytes 53280 | tf_op jit(solution)/shard_map/ppermute | solution.py:29
  17.9 0.5 %grads.2 = (f32[2,2,64,256]{3,2,1,0:T(8,128)S(1)}, bf16[4,256,128]{2,1,0:T(8,128)(2,1)S(1)}, bf16[2,64,64]{2,1,0:T(8,128)(2,1)S(1)}) custom-call(bf16[208,128]{1,0:T(8,128)(2,1)S(1)} %relay.1.refs_0_, bf16[208,128]{1,0:T(8,128)(2,1)S(1)} %collective-permute-done.3.refs_1_, bf16[208,128]{1,0:T(8,128)(2,1)S(1)} %collective-permute-done.4.refs_2_, ...), custom_call_target="tpu_custom_call" | custom-call | flops 11000000512 | tf_op jit(solution)/shard_map/grads/pallas_call | solution.py:560
  18.5 0.5 %grads.3 = (f32[2,64,256]{2,1,0:T(8,128)S(1)}, bf16[2,64,256]{2,1,0:T(8,128)(2,1)S(1)}, bf16[2,64,256]{2,1,0:T(8,128)(2,1)S(1)}, bf16[2,64,256]{2,1,0:T(8,128)(2,1)S(1)}) custom-call(bf16[4,256,128]{2,1,0:T(8,128)(2,1)S(1)} %get-tuple-element.31.refs_0_, bf16[2,64,64]{2,1,0:T(8,128)(2,1)S(1)} %get-tuple-element.32.refs_1_, ...), custom_call_target="tpu_custom_call" | custom-call | flops 11000000512 | tf_op jit(solution)/shard_map/grads/pallas_call | solution.py:560
  19.0 2.7 %collective-permute-start.10 = (bf16[2,64,256]{2,1,0:T(8,128)(2,1)S(1)}, bf16[2,64,256]{2,1,0:T(8,128)(2,1)S(1)}, u32[]{:S(2)}, u32[]{:S(2)}) collective-permute-start(bf16[2,64,256]{2,1,0:T(8,128)(2,1)S(1)} %get-tuple-element.39), channel_id=1, source_target_pairs={{0,8},{1,9},{2,10},{3,11},{4,12},{5,13},{6,14},{7,15},{8,0},{9,1},... | collective-permute-start | bytes 196616 | tf_op jit(solution)/shard_map/ppermute | solution.py:29
  21.6 2.3 %collective-permute-start.11 = (bf16[2,64,256]{2,1,0:T(8,128)(2,1)S(1)}, bf16[2,64,256]{2,1,0:T(8,128)(2,1)S(1)}, u32[]{:S(2)}, u32[]{:S(2)}) collective-permute-start(bf16[2,64,256]{2,1,0:T(8,128)(2,1)S(1)} %get-tuple-element.40), channel_id=1, source_target_pairs={{0,15},{1,14},{2,13},{3,12},{4,11},{5,10},{6,9},{7,8},{8,7},{9,6},... | collective-permute-start | bytes 196616 | tf_op jit(solution)/shard_map/ppermute | solution.py:29
  23.9 0.4 %collective-permute-start.12 = (bf16[2,64,256]{2,1,0:T(8,128)(2,1)S(1)}, bf16[2,64,256]{2,1,0:T(8,128)(2,1)S(1)}, u32[]{:S(2)}, u32[]{:S(2)}) collective-permute-start(bf16[2,64,256]{2,1,0:T(8,128)(2,1)S(1)} %get-tuple-element.41), channel_id=1, source_target_pairs={{0,7},{1,6},{2,5},{3,4},{4,3},{5,2},{6,1},{7,0},{8,15},{9,14},{10,... | collective-permute-start | bytes 196616 | tf_op jit(solution)/shard_map/ppermute | solution.py:29
  24.3 1.3 %collective-permute-done.10 = bf16[2,64,256]{2,1,0:T(8,128)(2,1)S(1)} collective-permute-done((bf16[2,64,256]{2,1,0:T(8,128)(2,1)S(1)}, bf16[2,64,256]{2,1,0:T(8,128)(2,1)S(1)}, u32[]{:S(2)}, u32[]{:S(2)}) %collective-permute-start.10) | collective-permute-done | bytes 65568 | tf_op jit(solution)/shard_map/ppermute | solution.py:29
  25.6 4.5 %collective-permute-done.11 = bf16[2,64,256]{2,1,0:T(8,128)(2,1)S(1)} collective-permute-done((bf16[2,64,256]{2,1,0:T(8,128)(2,1)S(1)}, bf16[2,64,256]{2,1,0:T(8,128)(2,1)S(1)}, u32[]{:S(2)}, u32[]{:S(2)}) %collective-permute-start.11) | collective-permute-done | bytes 65568 | tf_op jit(solution)/shard_map/ppermute | solution.py:29
  30.5 0.7 %fusion = (f32[1,64,256]{2,1,0:T(8,128)}, f32[1,64,256]{2,1,0:T(8,128)}) fusion(f32[2,64,256]{2,1,0:T(8,128)S(1)} %convert_add_fusion), kind=kLoop, calls=%fused_computation.1 | loop fusion | bytes 262144 | tf_op jit(solution)/shard_map/slice | solution.py:585
  (13 shorter events, 0.7 us)
Async XLA Ops:
  0.6 2.1 %copy-start = (bf16[1,64,4096]{2,1,0:T(8,128)(2,1)S(1)}, bf16[1,64,4096]{2,1,0:T(8,128)(2,1)}, u32[]{:S(2)}) copy-start(bf16[1,64,4096]{2,1,0:T(8,128)(2,1)} %refs_1_.3) | copy-start | bytes 1572868
  2.3 6.6 %collective-permute-start = (bf16[80,4096]{1,0:T(8,128)(2,1)S(1)}, bf16[80,4096]{1,0:T(8,128)(2,1)S(1)}, u32[]{:S(2)}, u32[]{:S(2)}) collective-permute-start(bf16[80,4096]{1,0:T(8,128)(2,1)S(1)} %get-tuple-element.23.refs_1_.refs_0_), channel_id=1, source_target_pairs={{0,16},{16,0},{1,17},{17,1},{2,18},{18,2},{3,19},{19,3},{4,20},{20... | collective-permute-start | bytes 1966088 | tf_op jit(solution)/shard_map/ppermute | solution.py:29
  2.8 6.1 %collective-permute-start.1 = (bf16[1,64,4096]{2,1,0:T(8,128)(2,1)S(1)}, bf16[1,64,4096]{2,1,0:T(8,128)(2,1)S(1)}, u32[]{:S(2)}, u32[]{:S(2)}) collective-permute-start(bf16[1,64,4096]{2,1,0:T(8,128)(2,1)S(1)} %copy-done), channel_id=1, source_target_pairs={{0,16},{16,0},{1,17},{17,1},{2,18},{18,2},{3,19},{19,3},{4,20},{20... | collective-permute-start | bytes 1572872 | tf_op jit(solution)/shard_map/ppermute | solution.py:29
  2.9 12.2 %collective-permute-start.6 = (bf16[2,128,512]{2,1,0:T(8,128)(2,1)S(1)}, bf16[2,128,512]{2,1,0:T(8,128)(2,1)S(1)}, u32[]{:S(2)}, u32[]{:S(2)}) collective-permute-start(bf16[2,128,512]{2,1,0:T(8,128)(2,1)S(1)} %get-tuple-element.24), channel_id=1, source_target_pairs={{0,1},{1,0},{2,3},{3,2},{4,5},{5,4},{6,7},{7,6},{8,9},{9,8},{10,11... | collective-permute-start | bytes 786440 | tf_op jit(solution)/shard_map/ppermute | solution.py:29
  5.8 8.0 %collective-permute-start.7 = (bf16[2,128,512]{2,1,0:T(8,128)(2,1)S(1)}, bf16[2,128,512]{2,1,0:T(8,128)(2,1)S(1)}, u32[]{:S(2)}, u32[]{:S(2)}) collective-permute-start(bf16[2,128,512]{2,1,0:T(8,128)(2,1)S(1)} %get-tuple-element.27), channel_id=1, source_target_pairs={{0,2},{1,3},{2,0},{3,1},{4,6},{5,7},{6,4},{7,5},{8,10},{9,11},{10,... | collective-permute-start | bytes 786440 | tf_op jit(solution)/shard_map/ppermute | solution.py:29
  7.3 7.7 %collective-permute-start.8 = (bf16[2,128,512]{2,1,0:T(8,128)(2,1)S(1)}, bf16[2,128,512]{2,1,0:T(8,128)(2,1)S(1)}, u32[]{:S(2)}, u32[]{:S(2)}) collective-permute-start(bf16[2,128,512]{2,1,0:T(8,128)(2,1)S(1)} %get-tuple-element.28), channel_id=1, source_target_pairs={{0,4},{1,5},{2,6},{3,7},{4,0},{5,1},{6,2},{7,3},{8,12},{9,13},{10,... | collective-permute-start | bytes 786440 | tf_op jit(solution)/shard_map/ppermute | solution.py:29
  10.3 1.5 %collective-permute-start.2 = (f32[392,128]{1,0:T(8,128)S(1)}, f32[392,128]{1,0:T(8,128)S(1)}, u32[]{:S(2)}, u32[]{:S(2)}) collective-permute-start(f32[392,128]{1,0:T(8,128)S(1)} %products.1.refs_0_), channel_id=1, source_target_pairs={{0,16},{16,0},{1,17},{17,1},{2,18},{18,2},{3,19},{19,3},{4,20},{20... | collective-permute-start | bytes 602120 | tf_op jit(solution)/shard_map/ppermute | solution.py:29
  12.2 4.2 %collective-permute-start.5 = (bf16[208,128]{1,0:T(8,128)(2,1)S(1)}, bf16[208,128]{1,0:T(8,128)(2,1)S(1)}, u32[]{:S(2)}, u32[]{:S(2)}) collective-permute-start(bf16[208,128]{1,0:T(8,128)(2,1)S(1)} %relay.1.refs_0_), channel_id=1, source_target_pairs={{0,4},{1,5},{2,6},{3,7},{4,0},{5,1},{6,2},{7,3},{8,12},{9,13},{10,... | collective-permute-start | bytes 159752 | tf_op jit(solution)/shard_map/ppermute | solution.py:29
  12.8 4.1 %collective-permute-start.4 = (bf16[208,128]{1,0:T(8,128)(2,1)S(1)}, bf16[208,128]{1,0:T(8,128)(2,1)S(1)}, u32[]{:S(2)}, u32[]{:S(2)}) collective-permute-start(bf16[208,128]{1,0:T(8,128)(2,1)S(1)} %relay.1.refs_0_), channel_id=1, source_target_pairs={{0,2},{1,3},{2,0},{3,1},{4,6},{5,7},{6,4},{7,5},{8,10},{9,11},{10,... | collective-permute-start | bytes 159752 | tf_op jit(solution)/shard_map/ppermute | solution.py:29
  13.8 4.1 %collective-permute-start.3 = (bf16[208,128]{1,0:T(8,128)(2,1)S(1)}, bf16[208,128]{1,0:T(8,128)(2,1)S(1)}, u32[]{:S(2)}, u32[]{:S(2)}) collective-permute-start(bf16[208,128]{1,0:T(8,128)(2,1)S(1)} %relay.1.refs_0_), channel_id=1, source_target_pairs={{0,1},{1,0},{2,3},{3,2},{4,5},{5,4},{6,7},{7,6},{8,9},{9,8},{10,11... | collective-permute-start | bytes 159752 | tf_op jit(solution)/shard_map/ppermute | solution.py:29
  15.1 3.4 %collective-permute-start.9 = (bf16[4,2,128,512]{3,2,1,0:T(8,128)(2,1)S(1)}, bf16[4,2,128,512]{3,2,1,0:T(8,128)(2,1)S(1)}, u32[]{:S(2)}, u32[]{:S(2)}) collective-permute-start(bf16[4,2,128,512]{3,2,1,0:T(8,128)(2,1)S(1)} %stack.1), channel_id=1, source_target_pairs={{0,16},{16,0},{1,17},{17,1},{2,18},{18,2},{3,19},{19,3},{4,20},{20... | collective-permute-start | bytes 3145736 | tf_op jit(solution)/shard_map/ppermute | solution.py:29
  19.0 6.6 %collective-permute-start.10 = (bf16[2,64,256]{2,1,0:T(8,128)(2,1)S(1)}, bf16[2,64,256]{2,1,0:T(8,128)(2,1)S(1)}, u32[]{:S(2)}, u32[]{:S(2)}) collective-permute-start(bf16[2,64,256]{2,1,0:T(8,128)(2,1)S(1)} %get-tuple-element.39), channel_id=1, source_target_pairs={{0,8},{1,9},{2,10},{3,11},{4,12},{5,13},{6,14},{7,15},{8,0},{9,1},... | collective-permute-start | bytes 196616 | tf_op jit(solution)/shard_map/ppermute | solution.py:29
  21.6 8.5 %collective-permute-start.11 = (bf16[2,64,256]{2,1,0:T(8,128)(2,1)S(1)}, bf16[2,64,256]{2,1,0:T(8,128)(2,1)S(1)}, u32[]{:S(2)}, u32[]{:S(2)}) collective-permute-start(bf16[2,64,256]{2,1,0:T(8,128)(2,1)S(1)} %get-tuple-element.40), channel_id=1, source_target_pairs={{0,15},{1,14},{2,13},{3,12},{4,11},{5,10},{6,9},{7,8},{8,7},{9,6},... | collective-permute-start | bytes 196616 | tf_op jit(solution)/shard_map/ppermute | solution.py:29
  23.9 6.5 %collective-permute-start.12 = (bf16[2,64,256]{2,1,0:T(8,128)(2,1)S(1)}, bf16[2,64,256]{2,1,0:T(8,128)(2,1)S(1)}, u32[]{:S(2)}, u32[]{:S(2)}) collective-permute-start(bf16[2,64,256]{2,1,0:T(8,128)(2,1)S(1)} %get-tuple-element.41), channel_id=1, source_target_pairs={{0,7},{1,6},{2,5},{3,4},{4,3},{5,2},{6,1},{7,0},{8,15},{9,14},{10,... | collective-permute-start | bytes 196616 | tf_op jit(solution)/shard_map/ppermute | solution.py:29

commit v6 on v5

--- a/solution.py
+++ b/solution.py
@@ -447,8 +447,8 @@
             ]
             packed.append(jnp.concatenate(cuts, axis=2))
 
-    own = (tall, lax.optimization_barrier((adapt_up, packed[1]))[0])
-    weights = [(tall, adapt_up)]
+    own = (tall, lax.optimization_barrier((adapt_up, *packed))[0])
+    weights = [own]
     for k in range(1, sections):
         weights.append(tuple(from_partner(w, "section", k) for w in own))
     flat = [w for ws in weights for w in ws]

time: 31.3 us -> 30.9 us (0.987)
  waiting for transfers between devices: 11.1 us -> 10.1 us
  starting transfers between devices: 14 us -> 14.6 us
    ppermute x13, waiting for transfers between devices: 11.1 us -> 10.1 us  [from_partner(): lax.ppermute(value, axis, [(i, i ^ flip) for i in range(lax.axis_size(axi...]
    ppermute x13, starting transfers between devices: 14 us -> 14.6 us  [from_partner(): lax.ppermute(value, axis, [(i, i ^ flip) for i in range(lax.axis_size(axi...]
  transfers between devices with their start and end apart: 13 -> 13, of which waited for: 9 -> 7; matrix products, arithmetic and copies ran while one was open for 0% -> 0% of each run, Pallas kernels for 8% -> 8%
where the time goes in v6:
time: 30.9 us; the launch traced here: 30.7 us
  starting transfers between devices  14.6 us (47%)
  waiting for transfers between devices  10.1 us (33%)
  Pallas kernels  4.68 us (15%)
  between operations  0.72 us (2%)
  local copies, waits for them, and re-layouts  0.66 us (2%)
    ppermute x13, starting transfers between devices, from_partner(): lax.ppermute(value, axis, [(i, i ^ flip) for i in range(lax.axis_size(axi...  14.6 us
    ppermute x13, waiting for transfers between devices, from_partner(): lax.ppermute(value, axis, [(i, i ^ flip) for i in range(lax.axis_size(axi...  10.1 us
    pallas_call x1, Pallas kernels, per_device(): pl.pallas_call(functools.partial(pack_kernel, width, group, chunks), out_...  1.6 us
    pallas_call x1, Pallas kernels, per_device(): pl.pallas_call(functools.partial(products_kernel, layers), out_shape=[jax...  1.46 us
    pallas_call x2, Pallas kernels, per_device(): pl.pallas_call(functools.partial(grads_kernel, layers, bottle, width, gro...  1.03 us
    slice x1, local copies, waits for them, and re-layouts, per_device(): return (total[0][None], total[1][None])  0.66 us
  transfers between devices with their start and end apart: 13, of which 7 were waited for; matrix products, arithmetic and copies ran while one was open for 0% of the time, Pallas kernels for 8%

profile of v6, /device:TPU:0, one launch (start us, length us, event | category | flops | bytes accessed | tf_op | source)
XLA Modules:
  0.0 30.7 jit_solution(8517305667540070989)
XLA Ops:
  0.6 1.6 %pack.1 = (bf16[2,128,2048]{2,1,0:T(8,128)(2,1)S(1)}, bf16[80,4096]{1,0:T(8,128)(2,1)S(1)}, bf16[2,128,512]{2,1,0:T(8,128)(2,1)S(1)}, bf16[2,128,512]{2,1,0:T(8,...) custom-call(bf16[2,32,2048]{2,1,0:T(8,128)(2,1)} %refs_0_.1, ...), custom_call_target="tpu_custom_call" | custom-call | tf_op jit(solution)/shard_map/pack/pallas_call | solution.py:417
  2.3 0.5 %collective-permute-start = (bf16[80,4096]{1,0:T(8,128)(2,1)S(1)}, bf16[80,4096]{1,0:T(8,128)(2,1)S(1)}, u32[]{:S(2)}, u32[]{:S(2)}) collective-permute-start(bf16[80,4096]{1,0:T(8,128)(2,1)S(1)} %get-tuple-element.23.refs_1_.refs_0_), channel_id=1, source_target_pairs={{0,16},{16,0},{1,17},{17,1},{2,18},{18,2},{3,19},{19,3},{4,20},{20... | collective-permute-start | bytes 1966088 | tf_op jit(solution)/shard_map/ppermute | solution.py:29
  2.9 2.9 %collective-permute-start.6 = (bf16[2,128,512]{2,1,0:T(8,128)(2,1)S(1)}, bf16[2,128,512]{2,1,0:T(8,128)(2,1)S(1)}, u32[]{:S(2)}, u32[]{:S(2)}) collective-permute-start(bf16[2,128,512]{2,1,0:T(8,128)(2,1)S(1)} %get-tuple-element.25), channel_id=1, source_target_pairs={{0,1},{1,0},{2,3},{3,2},{4,5},{5,4},{6,7},{7,6},{8,9},{9,8},{10,11... | collective-permute-start | bytes 786440 | tf_op jit(solution)/shard_map/ppermute | solution.py:29
  5.8 1.5 %collective-permute-start.7 = (bf16[2,128,512]{2,1,0:T(8,128)(2,1)S(1)}, bf16[2,128,512]{2,1,0:T(8,128)(2,1)S(1)}, u32[]{:S(2)}, u32[]{:S(2)}) collective-permute-start(bf16[2,128,512]{2,1,0:T(8,128)(2,1)S(1)} %get-tuple-element.26), channel_id=1, source_target_pairs={{0,2},{1,3},{2,0},{3,1},{4,6},{5,7},{6,4},{7,5},{8,10},{9,11},{10,... | collective-permute-start | bytes 786440 | tf_op jit(solution)/shard_map/ppermute | solution.py:29
  7.3 1.6 %collective-permute-start.8 = (bf16[2,128,512]{2,1,0:T(8,128)(2,1)S(1)}, bf16[2,128,512]{2,1,0:T(8,128)(2,1)S(1)}, u32[]{:S(2)}, u32[]{:S(2)}) collective-permute-start(bf16[2,128,512]{2,1,0:T(8,128)(2,1)S(1)} %get-tuple-element.27), channel_id=1, source_target_pairs={{0,4},{1,5},{2,6},{3,7},{4,0},{5,1},{6,2},{7,3},{8,12},{9,13},{10,... | collective-permute-start | bytes 786440 | tf_op jit(solution)/shard_map/ppermute | solution.py:29
  8.9 1.5 %products.1.refs_0_ = f32[392,128]{1,0:T(8,128)S(1)} custom-call(bf16[2,128,2048]{2,1,0:T(8,128)(2,1)S(1)} %get-tuple-element.22.refs_0_, bf16[80,4096]{1,0:T(8,128)(2,1)S(1)} %get-tuple-element.23.refs_1_.refs_0_, bf16[1,64,4096]{2,1,0:T(8,128)(2,1)S(1)} %copy-done, bf16[80,4096]{1,0:T(8,128)(2,1)S(1)} %collective-permute-done.refs_3_.refs_2_, ...), custom_call_target="tpu_custom_call" | custom-call | flops 13200000000 | tf_op jit(solution)/shard_map/products/pallas_call | solution.py:463
  10.4 1.4 %collective-permute-done.2.refs_1_ = f32[392,128]{1,0:T(8,128)S(1)} collective-permute-done((f32[392,128]{1,0:T(8,128)S(1)}, f32[392,128]{1,0:T(8,128)S(1)}, u32[]{:S(2)}, u32[]{:S(2)}) %collective-permute-start.2) | collective-permute-done | bytes 200736 | tf_op jit(solution)/shard_map/ppermute | solution.py:29
  11.8 0.4 %relay.1.refs_0_ = bf16[208,128]{1,0:T(8,128)(2,1)S(1)} custom-call(f32[392,128]{1,0:T(8,128)S(1)} %products.1.refs_0_, f32[392,128]{1,0:T(8,128)S(1)} %collective-permute-done.2.refs_1_), custom_call_target="tpu_custom_call" | custom-call | flops 110000000 | tf_op jit(solution)/shard_map/relay/pallas_call | solution.py:479
  12.2 0.5 %collective-permute-start.5 = (bf16[208,128]{1,0:T(8,128)(2,1)S(1)}, bf16[208,128]{1,0:T(8,128)(2,1)S(1)}, u32[]{:S(2)}, u32[]{:S(2)}) collective-permute-start(bf16[208,128]{1,0:T(8,128)(2,1)S(1)} %relay.1.refs_0_), channel_id=1, source_target_pairs={{0,4},{1,5},{2,6},{3,7},{4,0},{5,1},{6,2},{7,3},{8,12},{9,13},{10,... | collective-permute-start | bytes 159752 | tf_op jit(solution)/shard_map/ppermute | solution.py:29
  12.8 0.5 %collective-permute-start.4 = (bf16[208,128]{1,0:T(8,128)(2,1)S(1)}, bf16[208,128]{1,0:T(8,128)(2,1)S(1)}, u32[]{:S(2)}, u32[]{:S(2)}) collective-permute-start(bf16[208,128]{1,0:T(8,128)(2,1)S(1)} %relay.1.refs_0_), channel_id=1, source_target_pairs={{0,2},{1,3},{2,0},{3,1},{4,6},{5,7},{6,4},{7,5},{8,10},{9,11},{10,... | collective-permute-start | bytes 159752 | tf_op jit(solution)/shard_map/ppermute | solution.py:29
  13.3 1.4 %collective-permute-start.3 = (bf16[208,128]{1,0:T(8,128)(2,1)S(1)}, bf16[208,128]{1,0:T(8,128)(2,1)S(1)}, u32[]{:S(2)}, u32[]{:S(2)}) collective-permute-start(bf16[208,128]{1,0:T(8,128)(2,1)S(1)} %relay.1.refs_0_), channel_id=1, source_target_pairs={{0,1},{1,0},{2,3},{3,2},{4,5},{5,4},{6,7},{7,6},{8,9},{9,8},{10,11... | collective-permute-start | bytes 159752 | tf_op jit(solution)/shard_map/ppermute | solution.py:29
  14.6 0.4 %collective-permute-done.8.refs_7_.refs_3_ = bf16[2,128,512]{2,1,0:T(8,128)(2,1)S(1)} collective-permute-done((bf16[2,128,512]{2,1,0:T(8,128)(2,1)S(1)}, bf16[2,128,512]{2,1,0:T(8,128)(2,1)S(1)}, u32[]{:S(2)}, u32[]{:S(2)}) %collective-permute-start.8) | collective-permute-done | bytes 262176 | tf_op jit(solution)/shard_map/ppermute | solution.py:29
  15.2 0.1 cut.1
  15.3 1.1 %collective-permute-done.5.refs_3_ = bf16[208,128]{1,0:T(8,128)(2,1)S(1)} collective-permute-done((bf16[208,128]{1,0:T(8,128)(2,1)S(1)}, bf16[208,128]{1,0:T(8,128)(2,1)S(1)}, u32[]{:S(2)}, u32[]{:S(2)}) %collective-permute-start.5) | collective-permute-done | bytes 53280 | tf_op jit(solution)/shard_map/ppermute | solution.py:29
  16.4 0.5 %collective-permute-done.4.refs_2_ = bf16[208,128]{1,0:T(8,128)(2,1)S(1)} collective-permute-done((bf16[208,128]{1,0:T(8,128)(2,1)S(1)}, bf16[208,128]{1,0:T(8,128)(2,1)S(1)}, u32[]{:S(2)}, u32[]{:S(2)}) %collective-permute-start.4) | collective-permute-done | bytes 53280 | tf_op jit(solution)/shard_map/ppermute | solution.py:29
  16.9 0.5 %collective-permute-done.3.refs_1_ = bf16[208,128]{1,0:T(8,128)(2,1)S(1)} collective-permute-done((bf16[208,128]{1,0:T(8,128)(2,1)S(1)}, bf16[208,128]{1,0:T(8,128)(2,1)S(1)}, u32[]{:S(2)}, u32[]{:S(2)}) %collective-permute-start.3) | collective-permute-done | bytes 53280 | tf_op jit(solution)/shard_map/ppermute | solution.py:29
  17.4 0.5 %grads.2 = (f32[2,2,64,256]{3,2,1,0:T(8,128)S(1)}, bf16[4,256,128]{2,1,0:T(8,128)(2,1)S(1)}, bf16[2,64,64]{2,1,0:T(8,128)(2,1)S(1)}) custom-call(bf16[208,128]{1,0:T(8,128)(2,1)S(1)} %relay.1.refs_0_, bf16[208,128]{1,0:T(8,128)(2,1)S(1)} %collective-permute-done.3.refs_1_, bf16[208,128]{1,0:T(8,128)(2,1)S(1)} %collective-permute-done.4.refs_2_, ...), custom_call_target="tpu_custom_call" | custom-call | flops 11000000512 | tf_op jit(solution)/shard_map/grads/pallas_call | solution.py:560
  18.0 0.5 %grads.3 = (f32[2,64,256]{2,1,0:T(8,128)S(1)}, bf16[2,64,256]{2,1,0:T(8,128)(2,1)S(1)}, bf16[2,64,256]{2,1,0:T(8,128)(2,1)S(1)}, bf16[2,64,256]{2,1,0:T(8,128)(2,1)S(1)}) custom-call(bf16[4,256,128]{2,1,0:T(8,128)(2,1)S(1)} %get-tuple-element.31.refs_0_, bf16[2,64,64]{2,1,0:T(8,128)(2,1)S(1)} %get-tuple-element.32.refs_1_, ...), custom_call_target="tpu_custom_call" | custom-call | flops 11000000512 | tf_op jit(solution)/shard_map/grads/pallas_call | solution.py:560
  18.5 2.7 %collective-permute-start.10 = (bf16[2,64,256]{2,1,0:T(8,128)(2,1)S(1)}, bf16[2,64,256]{2,1,0:T(8,128)(2,1)S(1)}, u32[]{:S(2)}, u32[]{:S(2)}) collective-permute-start(bf16[2,64,256]{2,1,0:T(8,128)(2,1)S(1)} %get-tuple-element.39), channel_id=1, source_target_pairs={{0,8},{1,9},{2,10},{3,11},{4,12},{5,13},{6,14},{7,15},{8,0},{9,1},... | collective-permute-start | bytes 196616 | tf_op jit(solution)/shard_map/ppermute | solution.py:29
  21.1 2.5 %collective-permute-start.11 = (bf16[2,64,256]{2,1,0:T(8,128)(2,1)S(1)}, bf16[2,64,256]{2,1,0:T(8,128)(2,1)S(1)}, u32[]{:S(2)}, u32[]{:S(2)}) collective-permute-start(bf16[2,64,256]{2,1,0:T(8,128)(2,1)S(1)} %get-tuple-element.40), channel_id=1, source_target_pairs={{0,15},{1,14},{2,13},{3,12},{4,11},{5,10},{6,9},{7,8},{8,7},{9,6},... | collective-permute-start | bytes 196616 | tf_op jit(solution)/shard_map/ppermute | solution.py:29
  23.7 0.2 collective-permute-start.12
  23.9 5.7 %collective-permute-done.11 = bf16[2,64,256]{2,1,0:T(8,128)(2,1)S(1)} collective-permute-done((bf16[2,64,256]{2,1,0:T(8,128)(2,1)S(1)}, bf16[2,64,256]{2,1,0:T(8,128)(2,1)S(1)}, u32[]{:S(2)}, u32[]{:S(2)}) %collective-permute-start.11) | collective-permute-done | bytes 65568 | tf_op jit(solution)/shard_map/ppermute | solution.py:29
  29.6 0.4 %collective-permute-done.12 = bf16[2,64,256]{2,1,0:T(8,128)(2,1)S(1)} collective-permute-done((bf16[2,64,256]{2,1,0:T(8,128)(2,1)S(1)}, bf16[2,64,256]{2,1,0:T(8,128)(2,1)S(1)}, u32[]{:S(2)}, u32[]{:S(2)}) %collective-permute-start.12) | collective-permute-done | bytes 65568 | tf_op jit(solution)/shard_map/ppermute | solution.py:29
  30.1 0.7 %fusion = (f32[1,64,256]{2,1,0:T(8,128)}, f32[1,64,256]{2,1,0:T(8,128)}) fusion(f32[2,64,256]{2,1,0:T(8,128)S(1)} %convert_add_fusion), kind=kLoop, calls=%fused_computation.1 | loop fusion | bytes 262144 | tf_op jit(solution)/shard_map/slice | solution.py:585
  (13 shorter events, 0.3 us)
Async XLA Ops:
  0.6 2.1 %copy-start = (bf16[1,64,4096]{2,1,0:T(8,128)(2,1)S(1)}, bf16[1,64,4096]{2,1,0:T(8,128)(2,1)}, u32[]{:S(2)}) copy-start(bf16[1,64,4096]{2,1,0:T(8,128)(2,1)} %refs_1_.2) | copy-start | bytes 1572868
  2.3 6.6 %collective-permute-start = (bf16[80,4096]{1,0:T(8,128)(2,1)S(1)}, bf16[80,4096]{1,0:T(8,128)(2,1)S(1)}, u32[]{:S(2)}, u32[]{:S(2)}) collective-permute-start(bf16[80,4096]{1,0:T(8,128)(2,1)S(1)} %get-tuple-element.23.refs_1_.refs_0_), channel_id=1, source_target_pairs={{0,16},{16,0},{1,17},{17,1},{2,18},{18,2},{3,19},{19,3},{4,20},{20... | collective-permute-start | bytes 1966088 | tf_op jit(solution)/shard_map/ppermute | solution.py:29
  2.8 6.1 %collective-permute-start.1 = (bf16[1,64,4096]{2,1,0:T(8,128)(2,1)S(1)}, bf16[1,64,4096]{2,1,0:T(8,128)(2,1)S(1)}, u32[]{:S(2)}, u32[]{:S(2)}) collective-permute-start(bf16[1,64,4096]{2,1,0:T(8,128)(2,1)S(1)} %copy-done), channel_id=1, source_target_pairs={{0,16},{16,0},{1,17},{17,1},{2,18},{18,2},{3,19},{19,3},{4,20},{20... | collective-permute-start | bytes 1572872 | tf_op jit(solution)/shard_map/ppermute | solution.py:29
  2.9 10.4 %collective-permute-start.6 = (bf16[2,128,512]{2,1,0:T(8,128)(2,1)S(1)}, bf16[2,128,512]{2,1,0:T(8,128)(2,1)S(1)}, u32[]{:S(2)}, u32[]{:S(2)}) collective-permute-start(bf16[2,128,512]{2,1,0:T(8,128)(2,1)S(1)} %get-tuple-element.25), channel_id=1, source_target_pairs={{0,1},{1,0},{2,3},{3,2},{4,5},{5,4},{6,7},{7,6},{8,9},{9,8},{10,11... | collective-permute-start | bytes 786440 | tf_op jit(solution)/shard_map/ppermute | solution.py:29
  5.8 8.9 %collective-permute-start.7 = (bf16[2,128,512]{2,1,0:T(8,128)(2,1)S(1)}, bf16[2,128,512]{2,1,0:T(8,128)(2,1)S(1)}, u32[]{:S(2)}, u32[]{:S(2)}) collective-permute-start(bf16[2,128,512]{2,1,0:T(8,128)(2,1)S(1)} %get-tuple-element.26), channel_id=1, source_target_pairs={{0,2},{1,3},{2,0},{3,1},{4,6},{5,7},{6,4},{7,5},{8,10},{9,11},{10,... | collective-permute-start | bytes 786440 | tf_op jit(solution)/shard_map/ppermute | solution.py:29
  7.3 7.7 %collective-permute-start.8 = (bf16[2,128,512]{2,1,0:T(8,128)(2,1)S(1)}, bf16[2,128,512]{2,1,0:T(8,128)(2,1)S(1)}, u32[]{:S(2)}, u32[]{:S(2)}) collective-permute-start(bf16[2,128,512]{2,1,0:T(8,128)(2,1)S(1)} %get-tuple-element.27), channel_id=1, source_target_pairs={{0,4},{1,5},{2,6},{3,7},{4,0},{5,1},{6,2},{7,3},{8,12},{9,13},{10,... | collective-permute-start | bytes 786440 | tf_op jit(solution)/shard_map/ppermute | solution.py:29
  10.3 1.5 %collective-permute-start.2 = (f32[392,128]{1,0:T(8,128)S(1)}, f32[392,128]{1,0:T(8,128)S(1)}, u32[]{:S(2)}, u32[]{:S(2)}) collective-permute-start(f32[392,128]{1,0:T(8,128)S(1)} %products.1.refs_0_), channel_id=1, source_target_pairs={{0,16},{16,0},{1,17},{17,1},{2,18},{18,2},{3,19},{19,3},{4,20},{20... | collective-permute-start | bytes 602120 | tf_op jit(solution)/shard_map/ppermute | solution.py:29
  12.2 4.2 %collective-permute-start.5 = (bf16[208,128]{1,0:T(8,128)(2,1)S(1)}, bf16[208,128]{1,0:T(8,128)(2,1)S(1)}, u32[]{:S(2)}, u32[]{:S(2)}) collective-permute-start(bf16[208,128]{1,0:T(8,128)(2,1)S(1)} %relay.1.refs_0_), channel_id=1, source_target_pairs={{0,4},{1,5},{2,6},{3,7},{4,0},{5,1},{6,2},{7,3},{8,12},{9,13},{10,... | collective-permute-start | bytes 159752 | tf_op jit(solution)/shard_map/ppermute | solution.py:29
  12.8 4.1 %collective-permute-start.4 = (bf16[208,128]{1,0:T(8,128)(2,1)S(1)}, bf16[208,128]{1,0:T(8,128)(2,1)S(1)}, u32[]{:S(2)}, u32[]{:S(2)}) collective-permute-start(bf16[208,128]{1,0:T(8,128)(2,1)S(1)} %relay.1.refs_0_), channel_id=1, source_target_pairs={{0,2},{1,3},{2,0},{3,1},{4,6},{5,7},{6,4},{7,5},{8,10},{9,11},{10,... | collective-permute-start | bytes 159752 | tf_op jit(solution)/shard_map/ppermute | solution.py:29
  13.3 4.1 %collective-permute-start.3 = (bf16[208,128]{1,0:T(8,128)(2,1)S(1)}, bf16[208,128]{1,0:T(8,128)(2,1)S(1)}, u32[]{:S(2)}, u32[]{:S(2)}) collective-permute-start(bf16[208,128]{1,0:T(8,128)(2,1)S(1)} %relay.1.refs_0_), channel_id=1, source_target_pairs={{0,1},{1,0},{2,3},{3,2},{4,5},{5,4},{6,7},{7,6},{8,9},{9,8},{10,11... | collective-permute-start | bytes 159752 | tf_op jit(solution)/shard_map/ppermute | solution.py:29
  15.1 2.8 %collective-permute-start.9 = (bf16[4,2,128,512]{3,2,1,0:T(8,128)(2,1)S(1)}, bf16[4,2,128,512]{3,2,1,0:T(8,128)(2,1)S(1)}, u32[]{:S(2)}, u32[]{:S(2)}) collective-permute-start(bf16[4,2,128,512]{3,2,1,0:T(8,128)(2,1)S(1)} %stack.1), channel_id=1, source_target_pairs={{0,16},{16,0},{1,17},{17,1},{2,18},{18,2},{3,19},{19,3},{4,20},{20... | collective-permute-start | bytes 3145736 | tf_op jit(solution)/shard_map/ppermute | solution.py:29
  18.5 5.4 %collective-permute-start.10 = (bf16[2,64,256]{2,1,0:T(8,128)(2,1)S(1)}, bf16[2,64,256]{2,1,0:T(8,128)(2,1)S(1)}, u32[]{:S(2)}, u32[]{:S(2)}) collective-permute-start(bf16[2,64,256]{2,1,0:T(8,128)(2,1)S(1)} %get-tuple-element.39), channel_id=1, source_target_pairs={{0,8},{1,9},{2,10},{3,11},{4,12},{5,13},{6,14},{7,15},{8,0},{9,1},... | collective-permute-start | bytes 196616 | tf_op jit(solution)/shard_map/ppermute | solution.py:29
  21.1 8.5 %collective-permute-start.11 = (bf16[2,64,256]{2,1,0:T(8,128)(2,1)S(1)}, bf16[2,64,256]{2,1,0:T(8,128)(2,1)S(1)}, u32[]{:S(2)}, u32[]{:S(2)}) collective-permute-start(bf16[2,64,256]{2,1,0:T(8,128)(2,1)S(1)} %get-tuple-element.40), channel_id=1, source_target_pairs={{0,15},{1,14},{2,13},{3,12},{4,11},{5,10},{6,9},{7,8},{8,7},{9,6},... | collective-permute-start | bytes 196616 | tf_op jit(solution)/shard_map/ppermute | solution.py:29
  23.7 6.4 %collective-permute-start.12 = (bf16[2,64,256]{2,1,0:T(8,128)(2,1)S(1)}, bf16[2,64,256]{2,1,0:T(8,128)(2,1)S(1)}, u32[]{:S(2)}, u32[]{:S(2)}) collective-permute-start(bf16[2,64,256]{2,1,0:T(8,128)(2,1)S(1)} %get-tuple-element.41), channel_id=1, source_target_pairs={{0,7},{1,6},{2,5},{3,4},{4,3},{5,2},{6,1},{7,0},{8,15},{9,14},{10,... | collective-permute-start | bytes 196616 | tf_op jit(solution)/shard_map/ppermute | solution.py:29

commit v7 on v6

--- a/solution.py
+++ b/solution.py
@@ -291,16 +291,16 @@
 
 
 def stack_kernel(*refs):
+    rows = refs[0].shape[1]
     for k, ref in enumerate(refs[:-1]):
-        refs[-1][k] = ref[...]
+        refs[-1][:, k * rows : (k + 1) * rows] = ref[...]
 
 
 def factors_kernel_part(layers, bottle, section, coefs, lefts, mates):
     K = bottle
     inner = layers - 1
     above = [section <= i for i in range(inner)]
-    cross = [0.0] * inner
-    drag = [0.0] * inner
+    mates_of = [([], [], [], []) for _ in range(inner)]
     for m in range(MEMBERS):
         coef = coefs[m][...]
         grad, active = coef[:K], coef[K : 2 * K]
@@ -321,24 +321,26 @@
             return total
 
         coarse, fine = split(grad.astype(f32) * scale(0))
-        lefts[m, :K] = coarse
-        lefts[m, K : 2 * K] = fine
-        lefts[m, 2 * K : 3 * K] = (-weight(0) * active_f).astype(bf16)
-        lefts[m, 3 * K :] = active
+        here = slice(m * coef.shape[1], (m + 1) * coef.shape[1])
+        lefts[:K, here] = coarse
+        lefts[K : 2 * K, here] = fine
+        lefts[2 * K : 3 * K, here] = (-weight(0) * active_f).astype(bf16)
+        lefts[3 * K :, here] = active
         for i in range(inner):
             factor = jnp.where(above[i], scale(1 + i), 1.0)
             other = (others[i].astype(f32) * factor).astype(bf16)
             mate = jnp.where(above[i], active_f, coarse.astype(f32)).astype(bf16)
-            cross[i] = cross[i] + dot_nt(mate, other)
-        for n in range(inner):
-            held = others[n]
-            if n >= 1:
-                held = jnp.where(section < n, extras[n - 1].astype(f32), held.astype(f32))
-            held = jnp.where(section == n, active_f, held.astype(f32)).astype(bf16)
-            drag[n] = drag[n] + dot_nt((-weight(n) * active_f).astype(bf16), held)
+            held = others[i]
+            if i >= 1:
+                held = jnp.where(section < i, extras[i - 1].astype(f32), held.astype(f32))
+            held = jnp.where(section == i, active_f, held.astype(f32)).astype(bf16)
+            pulled = (-weight(i) * active_f).astype(bf16)
+            for values, value in zip(mates_of[i], (mate, other, pulled, held), strict=True):
+                values.append(value)
     for i in range(inner):
-        mates[2 * i] = cross[i].astype(bf16)
-        mates[2 * i + 1] = drag[i].astype(bf16)
+        mate, other, pulled, held = (jnp.concatenate(v, axis=1) for v in mates_of[i])
+        mates[2 * i] = dot_nt(mate, other).astype(bf16)
+        mates[2 * i + 1] = dot_nt(pulled, held).astype(bf16)
 
 
 def grads_kernel(layers, bottle, width, group, chunks, turn, *refs):
@@ -348,20 +350,15 @@
     final = turn == layers - 1
     if turn == 0:
         coefs, refs = refs[:MEMBERS], refs[MEMBERS:]
-        pieces, refs = refs[:MEMBERS], refs[MEMBERS:]
-        gain, both, *outs, lefts, mates = refs
+        pieces, gain, both, *outs, lefts, mates = refs
         factors_kernel_part(layers, bottle, section, coefs, lefts, mates)
-        pieces = [ref[...] for ref in pieces]
         before = []
     else:
         lefts, mates, pieces, gain, both = refs[:5]
         before, outs = refs[5 : 5 + turn], list(refs[5 + turn :])
-        pieces = [pieces[m] for m in range(MEMBERS)]
     parcel = outs.pop() if final else outs[0]
-    by_hidden, by_close = 0.0, 0.0
-    for m in range(MEMBERS):
-        by_hidden = by_hidden + dot_nn(lefts[m, : 3 * K], pieces[m][0])
-        by_close = by_close + dot_nn(lefts[m, 3 * K :], pieces[m][1])
+    by_hidden = dot_nn(lefts[: 3 * K], pieces[0])
+    by_close = dot_nn(lefts[3 * K :], pieces[1])
     down = by_hidden[:K] + by_hidden[K : 2 * K]
     up = by_close + by_hidden[2 * K :]
     for i in range(inner):
@@ -530,7 +527,7 @@
     gated = list(lax.optimization_barrier((*pieces, coef))[:-1])
     stacked = pl.pallas_call(
         stack_kernel,
-        out_shape=jax.ShapeDtypeStruct((MEMBERS, 2, rows, columns), bf16),
+        out_shape=jax.ShapeDtypeStruct((2, MEMBERS * rows, columns), bf16),
         in_specs=[IN_VMEM] * MEMBERS,
         out_specs=IN_VMEM,
         compiler_params=params,
@@ -540,7 +537,7 @@
     handed = [None] + [from_partner(stacked, "section", k) for k in range(1, sections)]
 
     message = (2, bottle, width)
-    left_shape = jax.ShapeDtypeStruct((MEMBERS, 4 * bottle, rows), bf16)
+    left_shape = jax.ShapeDtypeStruct((4 * bottle, MEMBERS * rows), bf16)
     mate_shape = jax.ShapeDtypeStruct((max(2 * inner, 1), bottle, bottle), bf16)
     held = jax.ShapeDtypeStruct((group,) + message, f32)
     before = []
@@ -554,7 +551,7 @@
                 shapes += [jax.ShapeDtypeStruct(message, bf16)] * (slots - 1)
         if k == 0:
             shapes += [left_shape, mate_shape]
-            operands = (*coefs, *pieces, gain_cut, both_cut)
+            operands = (*coefs, stacked, gain_cut, both_cut)
         else:
             operands = (lefts, mates, handed[k], gain_cut, both_cut, *before)
         parcels = pl.pallas_call(

time: 30.9 us -> 30.8 us (level)
  no operation moved by 1% of the time
where the time goes in v7:
time: 30.8 us; the launch traced here: 30.6 us
  starting transfers between devices  14.6 us (47%)
  waiting for transfers between devices  10.1 us (33%)
  Pallas kernels  4.53 us (15%)
  between operations  0.72 us (2%)
  local copies, waits for them, and re-layouts  0.66 us (2%)
    ppermute x13, starting transfers between devices, from_partner(): lax.ppermute(value, axis, [(i, i ^ flip) for i in range(lax.axis_size(axi...  14.6 us
    ppermute x13, waiting for transfers between devices, from_partner(): lax.ppermute(value, axis, [(i, i ^ flip) for i in range(lax.axis_size(axi...  10.1 us
    pallas_call x1, Pallas kernels, per_device(): pl.pallas_call(functools.partial(pack_kernel, width, group, chunks), out_...  1.6 us
    pallas_call x1, Pallas kernels, per_device(): pl.pallas_call(functools.partial(products_kernel, layers), out_shape=[jax...  1.46 us
    pallas_call x2, Pallas kernels, per_device(): pl.pallas_call(functools.partial(grads_kernel, layers, bottle, width, gro...  0.88 us
    slice x1, local copies, waits for them, and re-layouts, per_device(): return (total[0][None], total[1][None])  0.66 us
  transfers between devices with their start and end apart: 13, of which 7 were waited for; matrix products, arithmetic and copies ran while one was open for 0% of the time, Pallas kernels for 8%

profile of v7, /device:TPU:0, one launch (start us, length us, event | category | flops | bytes accessed | tf_op | source)
XLA Modules:
  0.0 30.6 jit_solution(1467777162684866131)
XLA Ops:
  0.6 1.6 %pack.1 = (bf16[2,128,2048]{2,1,0:T(8,128)(2,1)S(1)}, bf16[80,4096]{1,0:T(8,128)(2,1)S(1)}, bf16[2,128,512]{2,1,0:T(8,128)(2,1)S(1)}, bf16[2,128,512]{2,1,0:T(8,...) custom-call(bf16[2,32,2048]{2,1,0:T(8,128)(2,1)} %refs_0_.1, ...), custom_call_target="tpu_custom_call" | custom-call | tf_op jit(solution)/shard_map/pack/pallas_call | solution.py:414
  2.3 0.5 %collective-permute-start = (bf16[80,4096]{1,0:T(8,128)(2,1)S(1)}, bf16[80,4096]{1,0:T(8,128)(2,1)S(1)}, u32[]{:S(2)}, u32[]{:S(2)}) collective-permute-start(bf16[80,4096]{1,0:T(8,128)(2,1)S(1)} %get-tuple-element.23.refs_1_.refs_0_), channel_id=1, source_target_pairs={{0,16},{16,0},{1,17},{17,1},{2,18},{18,2},{3,19},{19,3},{4,20},{20... | collective-permute-start | bytes 1966088 | tf_op jit(solution)/shard_map/ppermute | solution.py:29
  2.9 2.9 %collective-permute-start.6 = (bf16[2,128,512]{2,1,0:T(8,128)(2,1)S(1)}, bf16[2,128,512]{2,1,0:T(8,128)(2,1)S(1)}, u32[]{:S(2)}, u32[]{:S(2)}) collective-permute-start(bf16[2,128,512]{2,1,0:T(8,128)(2,1)S(1)} %get-tuple-element.25), channel_id=1, source_target_pairs={{0,1},{1,0},{2,3},{3,2},{4,5},{5,4},{6,7},{7,6},{8,9},{9,8},{10,11... | collective-permute-start | bytes 786440 | tf_op jit(solution)/shard_map/ppermute | solution.py:29
  5.8 1.5 %collective-permute-start.7 = (bf16[2,128,512]{2,1,0:T(8,128)(2,1)S(1)}, bf16[2,128,512]{2,1,0:T(8,128)(2,1)S(1)}, u32[]{:S(2)}, u32[]{:S(2)}) collective-permute-start(bf16[2,128,512]{2,1,0:T(8,128)(2,1)S(1)} %get-tuple-element.26), channel_id=1, source_target_pairs={{0,2},{1,3},{2,0},{3,1},{4,6},{5,7},{6,4},{7,5},{8,10},{9,11},{10,... | collective-permute-start | bytes 786440 | tf_op jit(solution)/shard_map/ppermute | solution.py:29
  7.3 1.6 %collective-permute-start.8 = (bf16[2,128,512]{2,1,0:T(8,128)(2,1)S(1)}, bf16[2,128,512]{2,1,0:T(8,128)(2,1)S(1)}, u32[]{:S(2)}, u32[]{:S(2)}) collective-permute-start(bf16[2,128,512]{2,1,0:T(8,128)(2,1)S(1)} %get-tuple-element.27), channel_id=1, source_target_pairs={{0,4},{1,5},{2,6},{3,7},{4,0},{5,1},{6,2},{7,3},{8,12},{9,13},{10,... | collective-permute-start | bytes 786440 | tf_op jit(solution)/shard_map/ppermute | solution.py:29
  8.9 1.5 %products.1.refs_0_ = f32[392,128]{1,0:T(8,128)S(1)} custom-call(bf16[2,128,2048]{2,1,0:T(8,128)(2,1)S(1)} %get-tuple-element.22.refs_0_, bf16[80,4096]{1,0:T(8,128)(2,1)S(1)} %get-tuple-element.23.refs_1_.refs_0_, bf16[1,64,4096]{2,1,0:T(8,128)(2,1)S(1)} %copy-done, bf16[80,4096]{1,0:T(8,128)(2,1)S(1)} %collective-permute-done.refs_3_.refs_2_, ...), custom_call_target="tpu_custom_call" | custom-call | flops 13200000000 | tf_op jit(solution)/shard_map/products/pallas_call | solution.py:460
  10.4 1.4 %collective-permute-done.2.refs_1_ = f32[392,128]{1,0:T(8,128)S(1)} collective-permute-done((f32[392,128]{1,0:T(8,128)S(1)}, f32[392,128]{1,0:T(8,128)S(1)}, u32[]{:S(2)}, u32[]{:S(2)}) %collective-permute-start.2) | collective-permute-done | bytes 200736 | tf_op jit(solution)/shard_map/ppermute | solution.py:29
  11.8 0.4 %relay.1.refs_0_ = bf16[208,128]{1,0:T(8,128)(2,1)S(1)} custom-call(f32[392,128]{1,0:T(8,128)S(1)} %products.1.refs_0_, f32[392,128]{1,0:T(8,128)S(1)} %collective-permute-done.2.refs_1_), custom_call_target="tpu_custom_call" | custom-call | flops 110000000 | tf_op jit(solution)/shard_map/relay/pallas_call | solution.py:476
  12.2 0.5 %collective-permute-start.5 = (bf16[208,128]{1,0:T(8,128)(2,1)S(1)}, bf16[208,128]{1,0:T(8,128)(2,1)S(1)}, u32[]{:S(2)}, u32[]{:S(2)}) collective-permute-start(bf16[208,128]{1,0:T(8,128)(2,1)S(1)} %relay.1.refs_0_), channel_id=1, source_target_pairs={{0,4},{1,5},{2,6},{3,7},{4,0},{5,1},{6,2},{7,3},{8,12},{9,13},{10,... | collective-permute-start | bytes 159752 | tf_op jit(solution)/shard_map/ppermute | solution.py:29
  12.8 0.5 %collective-permute-start.4 = (bf16[208,128]{1,0:T(8,128)(2,1)S(1)}, bf16[208,128]{1,0:T(8,128)(2,1)S(1)}, u32[]{:S(2)}, u32[]{:S(2)}) collective-permute-start(bf16[208,128]{1,0:T(8,128)(2,1)S(1)} %relay.1.refs_0_), channel_id=1, source_target_pairs={{0,2},{1,3},{2,0},{3,1},{4,6},{5,7},{6,4},{7,5},{8,10},{9,11},{10,... | collective-permute-start | bytes 159752 | tf_op jit(solution)/shard_map/ppermute | solution.py:29
  13.3 1.4 %collective-permute-start.3 = (bf16[208,128]{1,0:T(8,128)(2,1)S(1)}, bf16[208,128]{1,0:T(8,128)(2,1)S(1)}, u32[]{:S(2)}, u32[]{:S(2)}) collective-permute-start(bf16[208,128]{1,0:T(8,128)(2,1)S(1)} %relay.1.refs_0_), channel_id=1, source_target_pairs={{0,1},{1,0},{2,3},{3,2},{4,5},{5,4},{6,7},{7,6},{8,9},{9,8},{10,11... | collective-permute-start | bytes 159752 | tf_op jit(solution)/shard_map/ppermute | solution.py:29
  14.6 0.4 %collective-permute-done.8.refs_3_ = bf16[2,128,512]{2,1,0:T(8,128)(2,1)S(1)} collective-permute-done((bf16[2,128,512]{2,1,0:T(8,128)(2,1)S(1)}, bf16[2,128,512]{2,1,0:T(8,128)(2,1)S(1)}, u32[]{:S(2)}, u32[]{:S(2)}) %collective-permute-start.8) | collective-permute-done | bytes 262176 | tf_op jit(solution)/shard_map/ppermute | solution.py:29
  15.2 0.1 cut.1
  15.3 1.1 %collective-permute-done.5.refs_3_ = bf16[208,128]{1,0:T(8,128)(2,1)S(1)} collective-permute-done((bf16[208,128]{1,0:T(8,128)(2,1)S(1)}, bf16[208,128]{1,0:T(8,128)(2,1)S(1)}, u32[]{:S(2)}, u32[]{:S(2)}) %collective-permute-start.5) | collective-permute-done | bytes 53280 | tf_op jit(solution)/shard_map/ppermute | solution.py:29
  16.4 0.5 %collective-permute-done.4.refs_2_ = bf16[208,128]{1,0:T(8,128)(2,1)S(1)} collective-permute-done((bf16[208,128]{1,0:T(8,128)(2,1)S(1)}, bf16[208,128]{1,0:T(8,128)(2,1)S(1)}, u32[]{:S(2)}, u32[]{:S(2)}) %collective-permute-start.4) | collective-permute-done | bytes 53280 | tf_op jit(solution)/shard_map/ppermute | solution.py:29
  16.9 0.5 %collective-permute-done.3.refs_1_ = bf16[208,128]{1,0:T(8,128)(2,1)S(1)} collective-permute-done((bf16[208,128]{1,0:T(8,128)(2,1)S(1)}, bf16[208,128]{1,0:T(8,128)(2,1)S(1)}, u32[]{:S(2)}, u32[]{:S(2)}) %collective-permute-start.3) | collective-permute-done | bytes 53280 | tf_op jit(solution)/shard_map/ppermute | solution.py:29
  17.4 0.5 %grads.2 = (f32[2,2,64,256]{3,2,1,0:T(8,128)S(1)}, bf16[256,512]{1,0:T(8,128)(2,1)S(1)}, bf16[2,64,64]{2,1,0:T(8,128)(2,1)S(1)}) custom-call(bf16[208,128]{1,0:T(8,128)(2,1)S(1)} %relay.1.refs_0_, bf16[208,128]{1,0:T(8,128)(2,1)S(1)} %collective-permute-done.3.refs_1_, bf16[208,128]{1,0:T(8,128)(2,1)S(1)} %collective-permute-done.4.refs_2_, ...), custom_call_target="tpu_custom_call" | custom-call | flops 11000000512 | tf_op jit(solution)/shard_map/grads/pallas_call | solution.py:557
  17.9 0.4 %grads.3 = (f32[2,64,256]{2,1,0:T(8,128)S(1)}, bf16[2,64,256]{2,1,0:T(8,128)(2,1)S(1)}, bf16[2,64,256]{2,1,0:T(8,128)(2,1)S(1)}, bf16[2,64,256]{2,1,0:T(8,128)(2,1)S(1)}) custom-call(bf16[256,512]{1,0:T(8,128)(2,1)S(1)} %get-tuple-element.35.refs_0_, bf16[2,64,64]{2,1,0:T(8,128)(2,1)S(1)} %get-tuple-element.36.refs_1_, ...), custom_call_target="tpu_custom_call" | custom-call | flops 11000000512 | tf_op jit(solution)/shard_map/grads/pallas_call | solution.py:557
  18.3 2.7 %collective-permute-start.10 = (bf16[2,64,256]{2,1,0:T(8,128)(2,1)S(1)}, bf16[2,64,256]{2,1,0:T(8,128)(2,1)S(1)}, u32[]{:S(2)}, u32[]{:S(2)}) collective-permute-start(bf16[2,64,256]{2,1,0:T(8,128)(2,1)S(1)} %get-tuple-element.39), channel_id=1, source_target_pairs={{0,8},{1,9},{2,10},{3,11},{4,12},{5,13},{6,14},{7,15},{8,0},{9,1},... | collective-permute-start | bytes 196616 | tf_op jit(solution)/shard_map/ppermute | solution.py:29
  21.0 2.5 %collective-permute-start.11 = (bf16[2,64,256]{2,1,0:T(8,128)(2,1)S(1)}, bf16[2,64,256]{2,1,0:T(8,128)(2,1)S(1)}, u32[]{:S(2)}, u32[]{:S(2)}) collective-permute-start(bf16[2,64,256]{2,1,0:T(8,128)(2,1)S(1)} %get-tuple-element.40), channel_id=1, source_target_pairs={{0,15},{1,14},{2,13},{3,12},{4,11},{5,10},{6,9},{7,8},{8,7},{9,6},... | collective-permute-start | bytes 196616 | tf_op jit(solution)/shard_map/ppermute | solution.py:29
  23.5 0.2 collective-permute-start.12
  23.7 5.7 %collective-permute-done.11 = bf16[2,64,256]{2,1,0:T(8,128)(2,1)S(1)} collective-permute-done((bf16[2,64,256]{2,1,0:T(8,128)(2,1)S(1)}, bf16[2,64,256]{2,1,0:T(8,128)(2,1)S(1)}, u32[]{:S(2)}, u32[]{:S(2)}) %collective-permute-start.11) | collective-permute-done | bytes 65568 | tf_op jit(solution)/shard_map/ppermute | solution.py:29
  29.4 0.5 %collective-permute-done.12 = bf16[2,64,256]{2,1,0:T(8,128)(2,1)S(1)} collective-permute-done((bf16[2,64,256]{2,1,0:T(8,128)(2,1)S(1)}, bf16[2,64,256]{2,1,0:T(8,128)(2,1)S(1)}, u32[]{:S(2)}, u32[]{:S(2)}) %collective-permute-start.12) | collective-permute-done | bytes 65568 | tf_op jit(solution)/shard_map/ppermute | solution.py:29
  29.9 0.7 %fusion = (f32[1,64,256]{2,1,0:T(8,128)}, f32[1,64,256]{2,1,0:T(8,128)}) fusion(f32[2,64,256]{2,1,0:T(8,128)S(1)} %convert_add_fusion), kind=kLoop, calls=%fused_computation.1 | loop fusion | bytes 262144 | tf_op jit(solution)/shard_map/slice | solution.py:582
  (13 shorter events, 0.3 us)
Async XLA Ops:
  0.6 2.1 %copy-start = (bf16[1,64,4096]{2,1,0:T(8,128)(2,1)S(1)}, bf16[1,64,4096]{2,1,0:T(8,128)(2,1)}, u32[]{:S(2)}) copy-start(bf16[1,64,4096]{2,1,0:T(8,128)(2,1)} %refs_1_.2) | copy-start | bytes 1572868
  2.3 6.6 %collective-permute-start = (bf16[80,4096]{1,0:T(8,128)(2,1)S(1)}, bf16[80,4096]{1,0:T(8,128)(2,1)S(1)}, u32[]{:S(2)}, u32[]{:S(2)}) collective-permute-start(bf16[80,4096]{1,0:T(8,128)(2,1)S(1)} %get-tuple-element.23.refs_1_.refs_0_), channel_id=1, source_target_pairs={{0,16},{16,0},{1,17},{17,1},{2,18},{18,2},{3,19},{19,3},{4,20},{20... | collective-permute-start | bytes 1966088 | tf_op jit(solution)/shard_map/ppermute | solution.py:29
  2.8 6.1 %collective-permute-start.1 = (bf16[1,64,4096]{2,1,0:T(8,128)(2,1)S(1)}, bf16[1,64,4096]{2,1,0:T(8,128)(2,1)S(1)}, u32[]{:S(2)}, u32[]{:S(2)}) collective-permute-start(bf16[1,64,4096]{2,1,0:T(8,128)(2,1)S(1)} %copy-done), channel_id=1, source_target_pairs={{0,16},{16,0},{1,17},{17,1},{2,18},{18,2},{3,19},{19,3},{4,20},{20... | collective-permute-start | bytes 1572872 | tf_op jit(solution)/shard_map/ppermute | solution.py:29
  2.9 10.4 %collective-permute-start.6 = (bf16[2,128,512]{2,1,0:T(8,128)(2,1)S(1)}, bf16[2,128,512]{2,1,0:T(8,128)(2,1)S(1)}, u32[]{:S(2)}, u32[]{:S(2)}) collective-permute-start(bf16[2,128,512]{2,1,0:T(8,128)(2,1)S(1)} %get-tuple-element.25), channel_id=1, source_target_pairs={{0,1},{1,0},{2,3},{3,2},{4,5},{5,4},{6,7},{7,6},{8,9},{9,8},{10,11... | collective-permute-start | bytes 786440 | tf_op jit(solution)/shard_map/ppermute | solution.py:29
  5.8 8.9 %collective-permute-start.7 = (bf16[2,128,512]{2,1,0:T(8,128)(2,1)S(1)}, bf16[2,128,512]{2,1,0:T(8,128)(2,1)S(1)}, u32[]{:S(2)}, u32[]{:S(2)}) collective-permute-start(bf16[2,128,512]{2,1,0:T(8,128)(2,1)S(1)} %get-tuple-element.26), channel_id=1, source_target_pairs={{0,2},{1,3},{2,0},{3,1},{4,6},{5,7},{6,4},{7,5},{8,10},{9,11},{10,... | collective-permute-start | bytes 786440 | tf_op jit(solution)/shard_map/ppermute | solution.py:29
  7.3 7.7 %collective-permute-start.8 = (bf16[2,128,512]{2,1,0:T(8,128)(2,1)S(1)}, bf16[2,128,512]{2,1,0:T(8,128)(2,1)S(1)}, u32[]{:S(2)}, u32[]{:S(2)}) collective-permute-start(bf16[2,128,512]{2,1,0:T(8,128)(2,1)S(1)} %get-tuple-element.27), channel_id=1, source_target_pairs={{0,4},{1,5},{2,6},{3,7},{4,0},{5,1},{6,2},{7,3},{8,12},{9,13},{10,... | collective-permute-start | bytes 786440 | tf_op jit(solution)/shard_map/ppermute | solution.py:29
  10.3 1.5 %collective-permute-start.2 = (f32[392,128]{1,0:T(8,128)S(1)}, f32[392,128]{1,0:T(8,128)S(1)}, u32[]{:S(2)}, u32[]{:S(2)}) collective-permute-start(f32[392,128]{1,0:T(8,128)S(1)} %products.1.refs_0_), channel_id=1, source_target_pairs={{0,16},{16,0},{1,17},{17,1},{2,18},{18,2},{3,19},{19,3},{4,20},{20... | collective-permute-start | bytes 602120 | tf_op jit(solution)/shard_map/ppermute | solution.py:29
  12.2 4.2 %collective-permute-start.5 = (bf16[208,128]{1,0:T(8,128)(2,1)S(1)}, bf16[208,128]{1,0:T(8,128)(2,1)S(1)}, u32[]{:S(2)}, u32[]{:S(2)}) collective-permute-start(bf16[208,128]{1,0:T(8,128)(2,1)S(1)} %relay.1.refs_0_), channel_id=1, source_target_pairs={{0,4},{1,5},{2,6},{3,7},{4,0},{5,1},{6,2},{7,3},{8,12},{9,13},{10,... | collective-permute-start | bytes 159752 | tf_op jit(solution)/shard_map/ppermute | solution.py:29
  12.8 4.1 %collective-permute-start.4 = (bf16[208,128]{1,0:T(8,128)(2,1)S(1)}, bf16[208,128]{1,0:T(8,128)(2,1)S(1)}, u32[]{:S(2)}, u32[]{:S(2)}) collective-permute-start(bf16[208,128]{1,0:T(8,128)(2,1)S(1)} %relay.1.refs_0_), channel_id=1, source_target_pairs={{0,2},{1,3},{2,0},{3,1},{4,6},{5,7},{6,4},{7,5},{8,10},{9,11},{10,... | collective-permute-start | bytes 159752 | tf_op jit(solution)/shard_map/ppermute | solution.py:29
  13.3 4.1 %collective-permute-start.3 = (bf16[208,128]{1,0:T(8,128)(2,1)S(1)}, bf16[208,128]{1,0:T(8,128)(2,1)S(1)}, u32[]{:S(2)}, u32[]{:S(2)}) collective-permute-start(bf16[208,128]{1,0:T(8,128)(2,1)S(1)} %relay.1.refs_0_), channel_id=1, source_target_pairs={{0,1},{1,0},{2,3},{3,2},{4,5},{5,4},{6,7},{7,6},{8,9},{9,8},{10,11... | collective-permute-start | bytes 159752 | tf_op jit(solution)/shard_map/ppermute | solution.py:29
  15.1 2.8 %collective-permute-start.9 = (bf16[2,512,512]{2,1,0:T(8,128)(2,1)S(1)}, bf16[2,512,512]{2,1,0:T(8,128)(2,1)S(1)}, u32[]{:S(2)}, u32[]{:S(2)}) collective-permute-start(bf16[2,512,512]{2,1,0:T(8,128)(2,1)S(1)} %stack.1.refs_4_), channel_id=1, source_target_pairs={{0,16},{16,0},{1,17},{17,1},{2,18},{18,2},{3,19},{19,3},{4,20},{20... | collective-permute-start | bytes 3145736 | tf_op jit(solution)/shard_map/ppermute | solution.py:29
  18.3 5.4 %collective-permute-start.10 = (bf16[2,64,256]{2,1,0:T(8,128)(2,1)S(1)}, bf16[2,64,256]{2,1,0:T(8,128)(2,1)S(1)}, u32[]{:S(2)}, u32[]{:S(2)}) collective-permute-start(bf16[2,64,256]{2,1,0:T(8,128)(2,1)S(1)} %get-tuple-element.39), channel_id=1, source_target_pairs={{0,8},{1,9},{2,10},{3,11},{4,12},{5,13},{6,14},{7,15},{8,0},{9,1},... | collective-permute-start | bytes 196616 | tf_op jit(solution)/shard_map/ppermute | solution.py:29
  21.0 8.5 %collective-permute-start.11 = (bf16[2,64,256]{2,1,0:T(8,128)(2,1)S(1)}, bf16[2,64,256]{2,1,0:T(8,128)(2,1)S(1)}, u32[]{:S(2)}, u32[]{:S(2)}) collective-permute-start(bf16[2,64,256]{2,1,0:T(8,128)(2,1)S(1)} %get-tuple-element.40), channel_id=1, source_target_pairs={{0,15},{1,14},{2,13},{3,12},{4,11},{5,10},{6,9},{7,8},{8,7},{9,6},... | collective-permute-start | bytes 196616 | tf_op jit(solution)/shard_map/ppermute | solution.py:29
  23.5 6.4 %collective-permute-start.12 = (bf16[2,64,256]{2,1,0:T(8,128)(2,1)S(1)}, bf16[2,64,256]{2,1,0:T(8,128)(2,1)S(1)}, u32[]{:S(2)}, u32[]{:S(2)}) collective-permute-start(bf16[2,64,256]{2,1,0:T(8,128)(2,1)S(1)} %get-tuple-element.41), channel_id=1, source_target_pairs={{0,7},{1,6},{2,5},{3,4},{4,3},{5,2},{6,1},{7,0},{8,15},{9,14},{10,... | collective-permute-start | bytes 196616 | tf_op jit(solution)/shard_map/ppermute | solution.py:29

commit v8 on v7

--- a/solution.py
+++ b/solution.py
@@ -339,8 +339,8 @@
                 values.append(value)
     for i in range(inner):
         mate, other, pulled, held = (jnp.concatenate(v, axis=1) for v in mates_of[i])
-        mates[2 * i] = dot_nt(mate, other).astype(bf16)
-        mates[2 * i + 1] = dot_nt(pulled, held).astype(bf16)
+        mates[4 * i], mates[4 * i + 1] = split(dot_nt(mate, other))
+        mates[4 * i + 2], mates[4 * i + 3] = split(dot_nt(pulled, held))
 
 
 def grads_kernel(layers, bottle, width, group, chunks, turn, *refs):
@@ -364,10 +364,12 @@
     for i in range(inner):
         above = section <= i
         other = i + jnp.where(above, 1, 0)
-        term = dot_nn(mates[2 * i], both[turn, jnp.where(above, other, layers + other)])
+        basis = both[turn, jnp.where(above, other, layers + other)]
+        term = dot_nn(mates[4 * i], basis) + dot_nn(mates[4 * i + 1], basis)
         up = up + jnp.where(above, term, 0.0)
         down = down + jnp.where(above, 0.0, term)
-        up = up + dot_nn(mates[2 * i + 1], both[turn, layers + i])
+        basis = both[turn, layers + i]
+        up = up + dot_nn(mates[4 * i + 2], basis) + dot_nn(mates[4 * i + 3], basis)
     down = down * gain[turn]
     start = (section ^ turn) * group if final else 0
     for part in range(group):
@@ -538,7 +540,7 @@
 
     message = (2, bottle, width)
     left_shape = jax.ShapeDtypeStruct((4 * bottle, MEMBERS * rows), bf16)
-    mate_shape = jax.ShapeDtypeStruct((max(2 * inner, 1), bottle, bottle), bf16)
+    mate_shape = jax.ShapeDtypeStruct((max(4 * inner, 1), bottle, bottle), bf16)
     held = jax.ShapeDtypeStruct((group,) + message, f32)
     before = []
     for k in range(sections):

time: 30.8 us -> 30.8 us (level)
  no operation moved by 1% of the time
where the time goes in v8:
time: 30.8 us; the launch traced here: 30.7 us
  starting transfers between devices  14.5 us (47%)
  waiting for transfers between devices  10.1 us (33%)
  Pallas kernels  4.61 us (15%)
  between operations  0.72 us (2%)
  local copies, waits for them, and re-layouts  0.66 us (2%)
    ppermute x13, starting transfers between devices, from_partner(): lax.ppermute(value, axis, [(i, i ^ flip) for i in range(lax.axis_size(axi...  14.5 us
    ppermute x13, waiting for transfers between devices, from_partner(): lax.ppermute(value, axis, [(i, i ^ flip) for i in range(lax.axis_size(axi...  10.1 us
    pallas_call x1, Pallas kernels, per_device(): pl.pallas_call(functools.partial(pack_kernel, width, group, chunks), out_...  1.6 us
    pallas_call x1, Pallas kernels, per_device(): pl.pallas_call(functools.partial(products_kernel, layers), out_shape=[jax...  1.46 us
    pallas_call x2, Pallas kernels, per_device(): pl.pallas_call(functools.partial(grads_kernel, layers, bottle, width, gro...  0.96 us
    slice x1, local copies, waits for them, and re-layouts, per_device(): return (total[0][None], total[1][None])  0.66 us
  transfers between devices with their start and end apart: 13, of which 7 were waited for; matrix products, arithmetic and copies ran while one was open for 0% of the time, Pallas kernels for 8%

profile of v8, /device:TPU:0, one launch (start us, length us, event | category | flops | bytes accessed | tf_op | source)
XLA Modules:
  0.0 30.7 jit_solution(14419558883163660138)
XLA Ops:
  0.6 1.6 %pack.1 = (bf16[2,128,2048]{2,1,0:T(8,128)(2,1)S(1)}, bf16[80,4096]{1,0:T(8,128)(2,1)S(1)}, bf16[2,128,512]{2,1,0:T(8,128)(2,1)S(1)}, bf16[2,128,512]{2,1,0:T(8,...) custom-call(bf16[2,32,2048]{2,1,0:T(8,128)(2,1)} %refs_0_.1, ...), custom_call_target="tpu_custom_call" | custom-call | tf_op jit(solution)/shard_map/pack/pallas_call | solution.py:416
  2.3 0.5 %collective-permute-start = (bf16[80,4096]{1,0:T(8,128)(2,1)S(1)}, bf16[80,4096]{1,0:T(8,128)(2,1)S(1)}, u32[]{:S(2)}, u32[]{:S(2)}) collective-permute-start(bf16[80,4096]{1,0:T(8,128)(2,1)S(1)} %get-tuple-element.23.refs_1_.refs_0_), channel_id=1, source_target_pairs={{0,16},{16,0},{1,17},{17,1},{2,18},{18,2},{3,19},{19,3},{4,20},{20... | collective-permute-start | bytes 1966088 | tf_op jit(solution)/shard_map/ppermute | solution.py:29
  2.9 2.9 %collective-permute-start.6 = (bf16[2,128,512]{2,1,0:T(8,128)(2,1)S(1)}, bf16[2,128,512]{2,1,0:T(8,128)(2,1)S(1)}, u32[]{:S(2)}, u32[]{:S(2)}) collective-permute-start(bf16[2,128,512]{2,1,0:T(8,128)(2,1)S(1)} %get-tuple-element.25), channel_id=1, source_target_pairs={{0,1},{1,0},{2,3},{3,2},{4,5},{5,4},{6,7},{7,6},{8,9},{9,8},{10,11... | collective-permute-start | bytes 786440 | tf_op jit(solution)/shard_map/ppermute | solution.py:29
  5.8 1.5 %collective-permute-start.7 = (bf16[2,128,512]{2,1,0:T(8,128)(2,1)S(1)}, bf16[2,128,512]{2,1,0:T(8,128)(2,1)S(1)}, u32[]{:S(2)}, u32[]{:S(2)}) collective-permute-start(bf16[2,128,512]{2,1,0:T(8,128)(2,1)S(1)} %get-tuple-element.26), channel_id=1, source_target_pairs={{0,2},{1,3},{2,0},{3,1},{4,6},{5,7},{6,4},{7,5},{8,10},{9,11},{10,... | collective-permute-start | bytes 786440 | tf_op jit(solution)/shard_map/ppermute | solution.py:29
  7.3 1.6 %collective-permute-start.8 = (bf16[2,128,512]{2,1,0:T(8,128)(2,1)S(1)}, bf16[2,128,512]{2,1,0:T(8,128)(2,1)S(1)}, u32[]{:S(2)}, u32[]{:S(2)}) collective-permute-start(bf16[2,128,512]{2,1,0:T(8,128)(2,1)S(1)} %get-tuple-element.27), channel_id=1, source_target_pairs={{0,4},{1,5},{2,6},{3,7},{4,0},{5,1},{6,2},{7,3},{8,12},{9,13},{10,... | collective-permute-start | bytes 786440 | tf_op jit(solution)/shard_map/ppermute | solution.py:29
  8.9 1.5 %products.1.refs_0_ = f32[392,128]{1,0:T(8,128)S(1)} custom-call(bf16[2,128,2048]{2,1,0:T(8,128)(2,1)S(1)} %get-tuple-element.22.refs_0_, bf16[80,4096]{1,0:T(8,128)(2,1)S(1)} %get-tuple-element.23.refs_1_.refs_0_, bf16[1,64,4096]{2,1,0:T(8,128)(2,1)S(1)} %copy-done, bf16[80,4096]{1,0:T(8,128)(2,1)S(1)} %collective-permute-done.refs_3_.refs_2_, ...), custom_call_target="tpu_custom_call" | custom-call | flops 13200000000 | tf_op jit(solution)/shard_map/products/pallas_call | solution.py:462
  10.4 1.4 %collective-permute-done.2.refs_1_ = f32[392,128]{1,0:T(8,128)S(1)} collective-permute-done((f32[392,128]{1,0:T(8,128)S(1)}, f32[392,128]{1,0:T(8,128)S(1)}, u32[]{:S(2)}, u32[]{:S(2)}) %collective-permute-start.2) | collective-permute-done | bytes 200736 | tf_op jit(solution)/shard_map/ppermute | solution.py:29
  11.8 0.4 %relay.1.refs_0_ = bf16[208,128]{1,0:T(8,128)(2,1)S(1)} custom-call(f32[392,128]{1,0:T(8,128)S(1)} %products.1.refs_0_, f32[392,128]{1,0:T(8,128)S(1)} %collective-permute-done.2.refs_1_), custom_call_target="tpu_custom_call" | custom-call | flops 110000000 | tf_op jit(solution)/shard_map/relay/pallas_call | solution.py:478
  12.2 0.5 %collective-permute-start.5 = (bf16[208,128]{1,0:T(8,128)(2,1)S(1)}, bf16[208,128]{1,0:T(8,128)(2,1)S(1)}, u32[]{:S(2)}, u32[]{:S(2)}) collective-permute-start(bf16[208,128]{1,0:T(8,128)(2,1)S(1)} %relay.1.refs_0_), channel_id=1, source_target_pairs={{0,4},{1,5},{2,6},{3,7},{4,0},{5,1},{6,2},{7,3},{8,12},{9,13},{10,... | collective-permute-start | bytes 159752 | tf_op jit(solution)/shard_map/ppermute | solution.py:29
  12.8 0.5 %collective-permute-start.4 = (bf16[208,128]{1,0:T(8,128)(2,1)S(1)}, bf16[208,128]{1,0:T(8,128)(2,1)S(1)}, u32[]{:S(2)}, u32[]{:S(2)}) collective-permute-start(bf16[208,128]{1,0:T(8,128)(2,1)S(1)} %relay.1.refs_0_), channel_id=1, source_target_pairs={{0,2},{1,3},{2,0},{3,1},{4,6},{5,7},{6,4},{7,5},{8,10},{9,11},{10,... | collective-permute-start | bytes 159752 | tf_op jit(solution)/shard_map/ppermute | solution.py:29
  13.3 1.4 %collective-permute-start.3 = (bf16[208,128]{1,0:T(8,128)(2,1)S(1)}, bf16[208,128]{1,0:T(8,128)(2,1)S(1)}, u32[]{:S(2)}, u32[]{:S(2)}) collective-permute-start(bf16[208,128]{1,0:T(8,128)(2,1)S(1)} %relay.1.refs_0_), channel_id=1, source_target_pairs={{0,1},{1,0},{2,3},{3,2},{4,5},{5,4},{6,7},{7,6},{8,9},{9,8},{10,11... | collective-permute-start | bytes 159752 | tf_op jit(solution)/shard_map/ppermute | solution.py:29
  14.6 0.4 %collective-permute-done.8.refs_3_ = bf16[2,128,512]{2,1,0:T(8,128)(2,1)S(1)} collective-permute-done((bf16[2,128,512]{2,1,0:T(8,128)(2,1)S(1)}, bf16[2,128,512]{2,1,0:T(8,128)(2,1)S(1)}, u32[]{:S(2)}, u32[]{:S(2)}) %collective-permute-start.8) | collective-permute-done | bytes 262176 | tf_op jit(solution)/shard_map/ppermute | solution.py:29
  15.2 0.1 cut.1
  15.3 1.1 %collective-permute-done.5.refs_3_ = bf16[208,128]{1,0:T(8,128)(2,1)S(1)} collective-permute-done((bf16[208,128]{1,0:T(8,128)(2,1)S(1)}, bf16[208,128]{1,0:T(8,128)(2,1)S(1)}, u32[]{:S(2)}, u32[]{:S(2)}) %collective-permute-start.5) | collective-permute-done | bytes 53280 | tf_op jit(solution)/shard_map/ppermute | solution.py:29
  16.4 0.5 %collective-permute-done.4.refs_2_ = bf16[208,128]{1,0:T(8,128)(2,1)S(1)} collective-permute-done((bf16[208,128]{1,0:T(8,128)(2,1)S(1)}, bf16[208,128]{1,0:T(8,128)(2,1)S(1)}, u32[]{:S(2)}, u32[]{:S(2)}) %collective-permute-start.4) | collective-permute-done | bytes 53280 | tf_op jit(solution)/shard_map/ppermute | solution.py:29
  16.9 0.5 %collective-permute-done.3.refs_1_ = bf16[208,128]{1,0:T(8,128)(2,1)S(1)} collective-permute-done((bf16[208,128]{1,0:T(8,128)(2,1)S(1)}, bf16[208,128]{1,0:T(8,128)(2,1)S(1)}, u32[]{:S(2)}, u32[]{:S(2)}) %collective-permute-start.3) | collective-permute-done | bytes 53280 | tf_op jit(solution)/shard_map/ppermute | solution.py:29
  17.4 0.5 %grads.2 = (f32[2,2,64,256]{3,2,1,0:T(8,128)S(1)}, bf16[256,512]{1,0:T(8,128)(2,1)S(1)}, bf16[4,64,64]{2,1,0:T(8,128)(2,1)S(1)}) custom-call(bf16[208,128]{1,0:T(8,128)(2,1)S(1)} %relay.1.refs_0_, bf16[208,128]{1,0:T(8,128)(2,1)S(1)} %collective-permute-done.3.refs_1_, bf16[208,128]{1,0:T(8,128)(2,1)S(1)} %collective-permute-done.4.refs_2_, ...), custom_call_target="tpu_custom_call" | custom-call | flops 11000000512 | tf_op jit(solution)/shard_map/grads/pallas_call | solution.py:559
  17.9 0.5 %grads.3 = (f32[2,64,256]{2,1,0:T(8,128)S(1)}, bf16[2,64,256]{2,1,0:T(8,128)(2,1)S(1)}, bf16[2,64,256]{2,1,0:T(8,128)(2,1)S(1)}, bf16[2,64,256]{2,1,0:T(8,128)(2,1)S(1)}) custom-call(bf16[256,512]{1,0:T(8,128)(2,1)S(1)} %get-tuple-element.35.refs_0_, bf16[4,64,64]{2,1,0:T(8,128)(2,1)S(1)} %get-tuple-element.36.refs_1_, ...), custom_call_target="tpu_custom_call" | custom-call | flops 11000000512 | tf_op jit(solution)/shard_map/grads/pallas_call | solution.py:559
  18.4 2.7 %collective-permute-start.10 = (bf16[2,64,256]{2,1,0:T(8,128)(2,1)S(1)}, bf16[2,64,256]{2,1,0:T(8,128)(2,1)S(1)}, u32[]{:S(2)}, u32[]{:S(2)}) collective-permute-start(bf16[2,64,256]{2,1,0:T(8,128)(2,1)S(1)} %get-tuple-element.39), channel_id=1, source_target_pairs={{0,8},{1,9},{2,10},{3,11},{4,12},{5,13},{6,14},{7,15},{8,0},{9,1},... | collective-permute-start | bytes 196616 | tf_op jit(solution)/shard_map/ppermute | solution.py:29
  21.1 2.5 %collective-permute-start.11 = (bf16[2,64,256]{2,1,0:T(8,128)(2,1)S(1)}, bf16[2,64,256]{2,1,0:T(8,128)(2,1)S(1)}, u32[]{:S(2)}, u32[]{:S(2)}) collective-permute-start(bf16[2,64,256]{2,1,0:T(8,128)(2,1)S(1)} %get-tuple-element.40), channel_id=1, source_target_pairs={{0,15},{1,14},{2,13},{3,12},{4,11},{5,10},{6,9},{7,8},{8,7},{9,6},... | collective-permute-start | bytes 196616 | tf_op jit(solution)/shard_map/ppermute | solution.py:29
  23.6 0.2 collective-permute-start.12
  23.8 5.7 %collective-permute-done.11 = bf16[2,64,256]{2,1,0:T(8,128)(2,1)S(1)} collective-permute-done((bf16[2,64,256]{2,1,0:T(8,128)(2,1)S(1)}, bf16[2,64,256]{2,1,0:T(8,128)(2,1)S(1)}, u32[]{:S(2)}, u32[]{:S(2)}) %collective-permute-start.11) | collective-permute-done | bytes 65568 | tf_op jit(solution)/shard_map/ppermute | solution.py:29
  29.5 0.5 %collective-permute-done.12 = bf16[2,64,256]{2,1,0:T(8,128)(2,1)S(1)} collective-permute-done((bf16[2,64,256]{2,1,0:T(8,128)(2,1)S(1)}, bf16[2,64,256]{2,1,0:T(8,128)(2,1)S(1)}, u32[]{:S(2)}, u32[]{:S(2)}) %collective-permute-start.12) | collective-permute-done | bytes 65568 | tf_op jit(solution)/shard_map/ppermute | solution.py:29
  30.0 0.7 %fusion = (f32[1,64,256]{2,1,0:T(8,128)}, f32[1,64,256]{2,1,0:T(8,128)}) fusion(f32[2,64,256]{2,1,0:T(8,128)S(1)} %convert_add_fusion), kind=kLoop, calls=%fused_computation.1 | loop fusion | bytes 262144 | tf_op jit(solution)/shard_map/slice | solution.py:584
  (13 shorter events, 0.3 us)
Async XLA Ops:
  0.6 2.1 %copy-start = (bf16[1,64,4096]{2,1,0:T(8,128)(2,1)S(1)}, bf16[1,64,4096]{2,1,0:T(8,128)(2,1)}, u32[]{:S(2)}) copy-start(bf16[1,64,4096]{2,1,0:T(8,128)(2,1)} %refs_1_.2) | copy-start | bytes 1572868
  2.3 6.6 %collective-permute-start = (bf16[80,4096]{1,0:T(8,128)(2,1)S(1)}, bf16[80,4096]{1,0:T(8,128)(2,1)S(1)}, u32[]{:S(2)}, u32[]{:S(2)}) collective-permute-start(bf16[80,4096]{1,0:T(8,128)(2,1)S(1)} %get-tuple-element.23.refs_1_.refs_0_), channel_id=1, source_target_pairs={{0,16},{16,0},{1,17},{17,1},{2,18},{18,2},{3,19},{19,3},{4,20},{20... | collective-permute-start | bytes 1966088 | tf_op jit(solution)/shard_map/ppermute | solution.py:29
  2.8 6.1 %collective-permute-start.1 = (bf16[1,64,4096]{2,1,0:T(8,128)(2,1)S(1)}, bf16[1,64,4096]{2,1,0:T(8,128)(2,1)S(1)}, u32[]{:S(2)}, u32[]{:S(2)}) collective-permute-start(bf16[1,64,4096]{2,1,0:T(8,128)(2,1)S(1)} %copy-done), channel_id=1, source_target_pairs={{0,16},{16,0},{1,17},{17,1},{2,18},{18,2},{3,19},{19,3},{4,20},{20... | collective-permute-start | bytes 1572872 | tf_op jit(solution)/shard_map/ppermute | solution.py:29
  2.9 10.4 %collective-permute-start.6 = (bf16[2,128,512]{2,1,0:T(8,128)(2,1)S(1)}, bf16[2,128,512]{2,1,0:T(8,128)(2,1)S(1)}, u32[]{:S(2)}, u32[]{:S(2)}) collective-permute-start(bf16[2,128,512]{2,1,0:T(8,128)(2,1)S(1)} %get-tuple-element.25), channel_id=1, source_target_pairs={{0,1},{1,0},{2,3},{3,2},{4,5},{5,4},{6,7},{7,6},{8,9},{9,8},{10,11... | collective-permute-start | bytes 786440 | tf_op jit(solution)/shard_map/ppermute | solution.py:29
  5.8 8.9 %collective-permute-start.7 = (bf16[2,128,512]{2,1,0:T(8,128)(2,1)S(1)}, bf16[2,128,512]{2,1,0:T(8,128)(2,1)S(1)}, u32[]{:S(2)}, u32[]{:S(2)}) collective-permute-start(bf16[2,128,512]{2,1,0:T(8,128)(2,1)S(1)} %get-tuple-element.26), channel_id=1, source_target_pairs={{0,2},{1,3},{2,0},{3,1},{4,6},{5,7},{6,4},{7,5},{8,10},{9,11},{10,... | collective-permute-start | bytes 786440 | tf_op jit(solution)/shard_map/ppermute | solution.py:29
  7.3 7.7 %collective-permute-start.8 = (bf16[2,128,512]{2,1,0:T(8,128)(2,1)S(1)}, bf16[2,128,512]{2,1,0:T(8,128)(2,1)S(1)}, u32[]{:S(2)}, u32[]{:S(2)}) collective-permute-start(bf16[2,128,512]{2,1,0:T(8,128)(2,1)S(1)} %get-tuple-element.27), channel_id=1, source_target_pairs={{0,4},{1,5},{2,6},{3,7},{4,0},{5,1},{6,2},{7,3},{8,12},{9,13},{10,... | collective-permute-start | bytes 786440 | tf_op jit(solution)/shard_map/ppermute | solution.py:29
  10.3 1.5 %collective-permute-start.2 = (f32[392,128]{1,0:T(8,128)S(1)}, f32[392,128]{1,0:T(8,128)S(1)}, u32[]{:S(2)}, u32[]{:S(2)}) collective-permute-start(f32[392,128]{1,0:T(8,128)S(1)} %products.1.refs_0_), channel_id=1, source_target_pairs={{0,16},{16,0},{1,17},{17,1},{2,18},{18,2},{3,19},{19,3},{4,20},{20... | collective-permute-start | bytes 602120 | tf_op jit(solution)/shard_map/ppermute | solution.py:29
  12.2 4.2 %collective-permute-start.5 = (bf16[208,128]{1,0:T(8,128)(2,1)S(1)}, bf16[208,128]{1,0:T(8,128)(2,1)S(1)}, u32[]{:S(2)}, u32[]{:S(2)}) collective-permute-start(bf16[208,128]{1,0:T(8,128)(2,1)S(1)} %relay.1.refs_0_), channel_id=1, source_target_pairs={{0,4},{1,5},{2,6},{3,7},{4,0},{5,1},{6,2},{7,3},{8,12},{9,13},{10,... | collective-permute-start | bytes 159752 | tf_op jit(solution)/shard_map/ppermute | solution.py:29
  12.8 4.1 %collective-permute-start.4 = (bf16[208,128]{1,0:T(8,128)(2,1)S(1)}, bf16[208,128]{1,0:T(8,128)(2,1)S(1)}, u32[]{:S(2)}, u32[]{:S(2)}) collective-permute-start(bf16[208,128]{1,0:T(8,128)(2,1)S(1)} %relay.1.refs_0_), channel_id=1, source_target_pairs={{0,2},{1,3},{2,0},{3,1},{4,6},{5,7},{6,4},{7,5},{8,10},{9,11},{10,... | collective-permute-start | bytes 159752 | tf_op jit(solution)/shard_map/ppermute | solution.py:29
  13.3 4.1 %collective-permute-start.3 = (bf16[208,128]{1,0:T(8,128)(2,1)S(1)}, bf16[208,128]{1,0:T(8,128)(2,1)S(1)}, u32[]{:S(2)}, u32[]{:S(2)}) collective-permute-start(bf16[208,128]{1,0:T(8,128)(2,1)S(1)} %relay.1.refs_0_), channel_id=1, source_target_pairs={{0,1},{1,0},{2,3},{3,2},{4,5},{5,4},{6,7},{7,6},{8,9},{9,8},{10,11... | collective-permute-start | bytes 159752 | tf_op jit(solution)/shard_map/ppermute | solution.py:29
  15.1 2.8 %collective-permute-start.9 = (bf16[2,512,512]{2,1,0:T(8,128)(2,1)S(1)}, bf16[2,512,512]{2,1,0:T(8,128)(2,1)S(1)}, u32[]{:S(2)}, u32[]{:S(2)}) collective-permute-start(bf16[2,512,512]{2,1,0:T(8,128)(2,1)S(1)} %stack.1.refs_4_), channel_id=1, source_target_pairs={{0,16},{16,0},{1,17},{17,1},{2,18},{18,2},{3,19},{19,3},{4,20},{20... | collective-permute-start | bytes 3145736 | tf_op jit(solution)/shard_map/ppermute | solution.py:29
  18.4 5.4 %collective-permute-start.10 = (bf16[2,64,256]{2,1,0:T(8,128)(2,1)S(1)}, bf16[2,64,256]{2,1,0:T(8,128)(2,1)S(1)}, u32[]{:S(2)}, u32[]{:S(2)}) collective-permute-start(bf16[2,64,256]{2,1,0:T(8,128)(2,1)S(1)} %get-tuple-element.39), channel_id=1, source_target_pairs={{0,8},{1,9},{2,10},{3,11},{4,12},{5,13},{6,14},{7,15},{8,0},{9,1},... | collective-permute-start | bytes 196616 | tf_op jit(solution)/shard_map/ppermute | solution.py:29
  21.1 8.4 %collective-permute-start.11 = (bf16[2,64,256]{2,1,0:T(8,128)(2,1)S(1)}, bf16[2,64,256]{2,1,0:T(8,128)(2,1)S(1)}, u32[]{:S(2)}, u32[]{:S(2)}) collective-permute-start(bf16[2,64,256]{2,1,0:T(8,128)(2,1)S(1)} %get-tuple-element.40), channel_id=1, source_target_pairs={{0,15},{1,14},{2,13},{3,12},{4,11},{5,10},{6,9},{7,8},{8,7},{9,6},... | collective-permute-start | bytes 196616 | tf_op jit(solution)/shard_map/ppermute | solution.py:29
  23.6 6.4 %collective-permute-start.12 = (bf16[2,64,256]{2,1,0:T(8,128)(2,1)S(1)}, bf16[2,64,256]{2,1,0:T(8,128)(2,1)S(1)}, u32[]{:S(2)}, u32[]{:S(2)}) collective-permute-start(bf16[2,64,256]{2,1,0:T(8,128)(2,1)S(1)} %get-tuple-element.41), channel_id=1, source_target_pairs={{0,7},{1,6},{2,5},{3,4},{4,3},{5,2},{6,1},{7,0},{8,15},{9,14},{10,... | collective-permute-start | bytes 196616 | tf_op jit(solution)/shard_map/ppermute | solution.py:29

commit v9 on v7

--- a/solution.py
+++ b/solution.py
@@ -114,7 +114,7 @@
         copies[n].wait()
         a, m = divmod(n, micro)
         start = ((a % 2) * micro + m) * tokens
-        for k, out in enumerate(outs):
+        for k, out in enumerate(outs, 1):
             for part in range(group):
                 chunk = chunk_of(label ^ k, part, section)
                 span = pl.ds(pl.multiple_of(chunk * width, width), width)
@@ -290,10 +290,19 @@
                 both_out[k, layers + layer, :, here] = up[0, :, span]
 
 
-def stack_kernel(*refs):
+def stack_kernel(width, group, chunks, *refs):
     rows = refs[0].shape[1]
-    for k, ref in enumerate(refs[:-1]):
-        refs[-1][:, k * rows : (k + 1) * rows] = ref[...]
+    out = refs[-1]
+    if refs[0].shape[2] == out.shape[2]:
+        out[:, :rows] = refs[0][...]
+    else:
+        section, label, _ = whereabouts(group, chunks)
+        for part in range(group):
+            chunk = chunk_of(label, part, section)
+            span = pl.ds(pl.multiple_of(chunk * width, width), width)
+            out[:, :rows, part * width : (part + 1) * width] = refs[0][:, :, span]
+    for k, ref in enumerate(refs[1:-1], 1):
+        out[:, k * rows : (k + 1) * rows] = ref[...]
 
 
 def factors_kernel_part(layers, bottle, section, coefs, lefts, mates):
@@ -417,9 +426,9 @@
                 pltpu.VMEM((2, rows, share), bf16),
                 pltpu.VMEM((bottle + 16, features), bf16),
             ]
-            + [pltpu.VMEM((2, rows, columns), bf16)] * MEMBERS,
+            + [pltpu.VMEM((2, rows, columns), bf16)] * (MEMBERS - 1),
             in_specs=[IN_HBM] * 6,
-            out_specs=[IN_VMEM] * (2 + MEMBERS),
+            out_specs=[IN_VMEM] * (1 + MEMBERS),
             scratch_shapes=[
                 pltpu.VMEM((1, features), bf16),
                 pltpu.SemaphoreType.DMA((4 * micro + 2,)),
@@ -427,6 +436,7 @@
             compiler_params=params,
             name="pack",
         )(*[pltpu.with_memory_space_constraint(v, pltpu.HBM) for v in taken])
+        packed = [both, *packed]
     else:
         tall = jnp.concatenate(
             [adapt_down[0], jnp.broadcast_to(norm_gains, (16, features))], axis=0
@@ -526,7 +536,7 @@
 
     gated = list(lax.optimization_barrier((*pieces, coef))[:-1])
     stacked = pl.pallas_call(
-        stack_kernel,
+        functools.partial(stack_kernel, width, group, chunks),
         out_shape=jax.ShapeDtypeStruct((2, MEMBERS * rows, columns), bf16),
         in_specs=[IN_VMEM] * MEMBERS,
         out_specs=IN_VMEM,

time: 30.8 us -> 30.7 us (level)
  no operation moved by 1% of the time
where the time goes in v9:
time: 30.7 us; the launch traced here: 30.6 us
  starting transfers between devices  14.5 us (47%)
  waiting for transfers between devices  10.1 us (33%)
  Pallas kernels  4.55 us (15%)
  between operations  0.72 us (2%)
  local copies, waits for them, and re-layouts  0.66 us (2%)
    ppermute x13, starting transfers between devices, from_partner(): lax.ppermute(value, axis, [(i, i ^ flip) for i in range(lax.axis_size(axi...  14.5 us
    ppermute x13, waiting for transfers between devices, from_partner(): lax.ppermute(value, axis, [(i, i ^ flip) for i in range(lax.axis_size(axi...  10.1 us
    pallas_call x1, Pallas kernels, per_device(): pl.pallas_call(functools.partial(pack_kernel, width, group, chunks), out_...  1.6 us
    pallas_call x1, Pallas kernels, per_device(): pl.pallas_call(functools.partial(products_kernel, layers), out_shape=[jax...  1.46 us
    pallas_call x2, Pallas kernels, per_device(): pl.pallas_call(functools.partial(grads_kernel, layers, bottle, width, gro...  0.88 us
    slice x1, local copies, waits for them, and re-layouts, per_device(): return (total[0][None], total[1][None])  0.66 us
  transfers between devices with their start and end apart: 13, of which 7 were waited for; matrix products, arithmetic and copies ran while one was open for 0% of the time, Pallas kernels for 8%

profile of v9, /device:TPU:0, one launch (start us, length us, event | category | flops | bytes accessed | tf_op | source)
XLA Modules:
  0.0 30.6 jit_solution(1133771096159856840)
XLA Ops:
  0.6 1.6 %pack.1 = (bf16[2,128,2048]{2,1,0:T(8,128)(2,1)S(1)}, bf16[80,4096]{1,0:T(8,128)(2,1)S(1)}, bf16[2,128,512]{2,1,0:T(8,128)(2,1)S(1)}, bf16[2,128,512]{2,1,0:T(8,128)(2,1)S(1)}, bf16[2,128,512]{2,1,0:T(8,128)(2,1)S(1)}) custom-call(bf16[2,32,2048]{2,1,0:T(8,128)(2,1)} %refs_0_.1, bf16[2,32,2048]{2,1,0:T(8,128)(2,1)} %refs_1_.1, bf16[2,32,2048]{2,1,0:T(8,128)(2,1)} %refs_2_.1, ...), custom_call_target="tpu_custom_call" | custom-call | tf_op jit(solution)/shard_map/pack/pallas_call | solution.py:423
  2.3 0.5 %collective-permute-start = (bf16[80,4096]{1,0:T(8,128)(2,1)S(1)}, bf16[80,4096]{1,0:T(8,128)(2,1)S(1)}, u32[]{:S(2)}, u32[]{:S(2)}) collective-permute-start(bf16[80,4096]{1,0:T(8,128)(2,1)S(1)} %get-tuple-element.22.refs_1_.refs_0_), channel_id=1, source_target_pairs={{0,16},{16,0},{1,17},{17,1},{2,18},{18,2},{3,19},{19,3},{4,20},{20... | collective-permute-start | bytes 1966088 | tf_op jit(solution)/shard_map/ppermute | solution.py:29
  2.9 2.9 %collective-permute-start.6 = (bf16[2,128,512]{2,1,0:T(8,128)(2,1)S(1)}, bf16[2,128,512]{2,1,0:T(8,128)(2,1)S(1)}, u32[]{:S(2)}, u32[]{:S(2)}) collective-permute-start(bf16[2,128,512]{2,1,0:T(8,128)(2,1)S(1)} %get-tuple-element.23), channel_id=1, source_target_pairs={{0,1},{1,0},{2,3},{3,2},{4,5},{5,4},{6,7},{7,6},{8,9},{9,8},{10,11... | collective-permute-start | bytes 786440 | tf_op jit(solution)/shard_map/ppermute | solution.py:29
  5.8 1.5 %collective-permute-start.7 = (bf16[2,128,512]{2,1,0:T(8,128)(2,1)S(1)}, bf16[2,128,512]{2,1,0:T(8,128)(2,1)S(1)}, u32[]{:S(2)}, u32[]{:S(2)}) collective-permute-start(bf16[2,128,512]{2,1,0:T(8,128)(2,1)S(1)} %get-tuple-element.24), channel_id=1, source_target_pairs={{0,2},{1,3},{2,0},{3,1},{4,6},{5,7},{6,4},{7,5},{8,10},{9,11},{10,... | collective-permute-start | bytes 786440 | tf_op jit(solution)/shard_map/ppermute | solution.py:29
  7.3 1.6 %collective-permute-start.8 = (bf16[2,128,512]{2,1,0:T(8,128)(2,1)S(1)}, bf16[2,128,512]{2,1,0:T(8,128)(2,1)S(1)}, u32[]{:S(2)}, u32[]{:S(2)}) collective-permute-start(bf16[2,128,512]{2,1,0:T(8,128)(2,1)S(1)} %get-tuple-element.25), channel_id=1, source_target_pairs={{0,4},{1,5},{2,6},{3,7},{4,0},{5,1},{6,2},{7,3},{8,12},{9,13},{10,... | collective-permute-start | bytes 786440 | tf_op jit(solution)/shard_map/ppermute | solution.py:29
  8.9 1.5 %products.1.refs_0_ = f32[392,128]{1,0:T(8,128)S(1)} custom-call(bf16[2,128,2048]{2,1,0:T(8,128)(2,1)S(1)} %get-tuple-element.27.refs_0_, bf16[80,4096]{1,0:T(8,128)(2,1)S(1)} %get-tuple-element.22.refs_1_.refs_0_, bf16[1,64,4096]{2,1,0:T(8,128)(2,1)S(1)} %copy-done, bf16[80,4096]{1,0:T(8,128)(2,1)S(1)} %collective-permute-done.refs_3_.refs_2_, ...), custom_call_target="tpu_custom_call" | custom-call | flops 13200000000 | tf_op jit(solution)/shard_map/products/pallas_call | solution.py:470
  10.4 1.4 %collective-permute-done.2.refs_1_ = f32[392,128]{1,0:T(8,128)S(1)} collective-permute-done((f32[392,128]{1,0:T(8,128)S(1)}, f32[392,128]{1,0:T(8,128)S(1)}, u32[]{:S(2)}, u32[]{:S(2)}) %collective-permute-start.2) | collective-permute-done | bytes 200736 | tf_op jit(solution)/shard_map/ppermute | solution.py:29
  11.8 0.4 %relay.1.refs_0_ = bf16[208,128]{1,0:T(8,128)(2,1)S(1)} custom-call(f32[392,128]{1,0:T(8,128)S(1)} %products.1.refs_0_, f32[392,128]{1,0:T(8,128)S(1)} %collective-permute-done.2.refs_1_), custom_call_target="tpu_custom_call" | custom-call | flops 110000000 | tf_op jit(solution)/shard_map/relay/pallas_call | solution.py:486
  12.2 0.5 %collective-permute-start.5 = (bf16[208,128]{1,0:T(8,128)(2,1)S(1)}, bf16[208,128]{1,0:T(8,128)(2,1)S(1)}, u32[]{:S(2)}, u32[]{:S(2)}) collective-permute-start(bf16[208,128]{1,0:T(8,128)(2,1)S(1)} %relay.1.refs_0_), channel_id=1, source_target_pairs={{0,4},{1,5},{2,6},{3,7},{4,0},{5,1},{6,2},{7,3},{8,12},{9,13},{10,... | collective-permute-start | bytes 159752 | tf_op jit(solution)/shard_map/ppermute | solution.py:29
  12.7 0.5 %collective-permute-start.4 = (bf16[208,128]{1,0:T(8,128)(2,1)S(1)}, bf16[208,128]{1,0:T(8,128)(2,1)S(1)}, u32[]{:S(2)}, u32[]{:S(2)}) collective-permute-start(bf16[208,128]{1,0:T(8,128)(2,1)S(1)} %relay.1.refs_0_), channel_id=1, source_target_pairs={{0,2},{1,3},{2,0},{3,1},{4,6},{5,7},{6,4},{7,5},{8,10},{9,11},{10,... | collective-permute-start | bytes 159752 | tf_op jit(solution)/shard_map/ppermute | solution.py:29
  13.3 1.4 %collective-permute-start.3 = (bf16[208,128]{1,0:T(8,128)(2,1)S(1)}, bf16[208,128]{1,0:T(8,128)(2,1)S(1)}, u32[]{:S(2)}, u32[]{:S(2)}) collective-permute-start(bf16[208,128]{1,0:T(8,128)(2,1)S(1)} %relay.1.refs_0_), channel_id=1, source_target_pairs={{0,1},{1,0},{2,3},{3,2},{4,5},{5,4},{6,7},{7,6},{8,9},{9,8},{10,11... | collective-permute-start | bytes 159752 | tf_op jit(solution)/shard_map/ppermute | solution.py:29
  14.6 0.4 %collective-permute-done.8.refs_3_ = bf16[2,128,512]{2,1,0:T(8,128)(2,1)S(1)} collective-permute-done((bf16[2,128,512]{2,1,0:T(8,128)(2,1)S(1)}, bf16[2,128,512]{2,1,0:T(8,128)(2,1)S(1)}, u32[]{:S(2)}, u32[]{:S(2)}) %collective-permute-start.8) | collective-permute-done | bytes 262176 | tf_op jit(solution)/shard_map/ppermute | solution.py:29
  15.2 0.1 cut.1
  15.3 1.1 %collective-permute-done.5.refs_3_ = bf16[208,128]{1,0:T(8,128)(2,1)S(1)} collective-permute-done((bf16[208,128]{1,0:T(8,128)(2,1)S(1)}, bf16[208,128]{1,0:T(8,128)(2,1)S(1)}, u32[]{:S(2)}, u32[]{:S(2)}) %collective-permute-start.5) | collective-permute-done | bytes 53280 | tf_op jit(solution)/shard_map/ppermute | solution.py:29
  16.4 0.4 %collective-permute-done.4.refs_2_ = bf16[208,128]{1,0:T(8,128)(2,1)S(1)} collective-permute-done((bf16[208,128]{1,0:T(8,128)(2,1)S(1)}, bf16[208,128]{1,0:T(8,128)(2,1)S(1)}, u32[]{:S(2)}, u32[]{:S(2)}) %collective-permute-start.4) | collective-permute-done | bytes 53280 | tf_op jit(solution)/shard_map/ppermute | solution.py:29
  16.9 0.5 %collective-permute-done.3.refs_1_ = bf16[208,128]{1,0:T(8,128)(2,1)S(1)} collective-permute-done((bf16[208,128]{1,0:T(8,128)(2,1)S(1)}, bf16[208,128]{1,0:T(8,128)(2,1)S(1)}, u32[]{:S(2)}, u32[]{:S(2)}) %collective-permute-start.3) | collective-permute-done | bytes 53280 | tf_op jit(solution)/shard_map/ppermute | solution.py:29
  17.4 0.5 %grads.2 = (f32[2,2,64,256]{3,2,1,0:T(8,128)S(1)}, bf16[256,512]{1,0:T(8,128)(2,1)S(1)}, bf16[2,64,64]{2,1,0:T(8,128)(2,1)S(1)}) custom-call(bf16[208,128]{1,0:T(8,128)(2,1)S(1)} %relay.1.refs_0_, bf16[208,128]{1,0:T(8,128)(2,1)S(1)} %collective-permute-done.3.refs_1_, bf16[208,128]{1,0:T(8,128)(2,1)S(1)} %collective-permute-done.4.refs_2_, ...), custom_call_target="tpu_custom_call" | custom-call | flops 11000000512 | tf_op jit(solution)/shard_map/grads/pallas_call | solution.py:567
  17.9 0.4 %grads.3 = (f32[2,64,256]{2,1,0:T(8,128)S(1)}, bf16[2,64,256]{2,1,0:T(8,128)(2,1)S(1)}, bf16[2,64,256]{2,1,0:T(8,128)(2,1)S(1)}, bf16[2,64,256]{2,1,0:T(8,128)(2,1)S(1)}) custom-call(bf16[256,512]{1,0:T(8,128)(2,1)S(1)} %get-tuple-element.33.refs_0_, bf16[2,64,64]{2,1,0:T(8,128)(2,1)S(1)} %get-tuple-element.34.refs_1_, ...), custom_call_target="tpu_custom_call" | custom-call | flops 11000000512 | tf_op jit(solution)/shard_map/grads/pallas_call | solution.py:567
  18.3 2.7 %collective-permute-start.10 = (bf16[2,64,256]{2,1,0:T(8,128)(2,1)S(1)}, bf16[2,64,256]{2,1,0:T(8,128)(2,1)S(1)}, u32[]{:S(2)}, u32[]{:S(2)}) collective-permute-start(bf16[2,64,256]{2,1,0:T(8,128)(2,1)S(1)} %get-tuple-element.37), channel_id=1, source_target_pairs={{0,8},{1,9},{2,10},{3,11},{4,12},{5,13},{6,14},{7,15},{8,0},{9,1},... | collective-permute-start | bytes 196616 | tf_op jit(solution)/shard_map/ppermute | solution.py:29
  21.0 2.5 %collective-permute-start.11 = (bf16[2,64,256]{2,1,0:T(8,128)(2,1)S(1)}, bf16[2,64,256]{2,1,0:T(8,128)(2,1)S(1)}, u32[]{:S(2)}, u32[]{:S(2)}) collective-permute-start(bf16[2,64,256]{2,1,0:T(8,128)(2,1)S(1)} %get-tuple-element.38), channel_id=1, source_target_pairs={{0,15},{1,14},{2,13},{3,12},{4,11},{5,10},{6,9},{7,8},{8,7},{9,6},... | collective-permute-start | bytes 196616 | tf_op jit(solution)/shard_map/ppermute | solution.py:29
  23.5 0.2 collective-permute-start.12
  23.7 5.7 %collective-permute-done.11 = bf16[2,64,256]{2,1,0:T(8,128)(2,1)S(1)} collective-permute-done((bf16[2,64,256]{2,1,0:T(8,128)(2,1)S(1)}, bf16[2,64,256]{2,1,0:T(8,128)(2,1)S(1)}, u32[]{:S(2)}, u32[]{:S(2)}) %collective-permute-start.11) | collective-permute-done | bytes 65568 | tf_op jit(solution)/shard_map/ppermute | solution.py:29
  29.4 0.5 %collective-permute-done.12 = bf16[2,64,256]{2,1,0:T(8,128)(2,1)S(1)} collective-permute-done((bf16[2,64,256]{2,1,0:T(8,128)(2,1)S(1)}, bf16[2,64,256]{2,1,0:T(8,128)(2,1)S(1)}, u32[]{:S(2)}, u32[]{:S(2)}) %collective-permute-start.12) | collective-permute-done | bytes 65568 | tf_op jit(solution)/shard_map/ppermute | solution.py:29
  29.9 0.7 %fusion = (f32[1,64,256]{2,1,0:T(8,128)}, f32[1,64,256]{2,1,0:T(8,128)}) fusion(f32[2,64,256]{2,1,0:T(8,128)S(1)} %convert_add_fusion), kind=kLoop, calls=%fused_computation.1 | loop fusion | bytes 262144 | tf_op jit(solution)/shard_map/slice | solution.py:592
  (13 shorter events, 0.3 us)
Async XLA Ops:
  0.6 2.1 %copy-start = (bf16[1,64,4096]{2,1,0:T(8,128)(2,1)S(1)}, bf16[1,64,4096]{2,1,0:T(8,128)(2,1)}, u32[]{:S(2)}) copy-start(bf16[1,64,4096]{2,1,0:T(8,128)(2,1)} %refs_1_.2) | copy-start | bytes 1572868
  2.3 6.6 %collective-permute-start = (bf16[80,4096]{1,0:T(8,128)(2,1)S(1)}, bf16[80,4096]{1,0:T(8,128)(2,1)S(1)}, u32[]{:S(2)}, u32[]{:S(2)}) collective-permute-start(bf16[80,4096]{1,0:T(8,128)(2,1)S(1)} %get-tuple-element.22.refs_1_.refs_0_), channel_id=1, source_target_pairs={{0,16},{16,0},{1,17},{17,1},{2,18},{18,2},{3,19},{19,3},{4,20},{20... | collective-permute-start | bytes 1966088 | tf_op jit(solution)/shard_map/ppermute | solution.py:29
  2.8 6.1 %collective-permute-start.1 = (bf16[1,64,4096]{2,1,0:T(8,128)(2,1)S(1)}, bf16[1,64,4096]{2,1,0:T(8,128)(2,1)S(1)}, u32[]{:S(2)}, u32[]{:S(2)}) collective-permute-start(bf16[1,64,4096]{2,1,0:T(8,128)(2,1)S(1)} %copy-done), channel_id=1, source_target_pairs={{0,16},{16,0},{1,17},{17,1},{2,18},{18,2},{3,19},{19,3},{4,20},{20... | collective-permute-start | bytes 1572872 | tf_op jit(solution)/shard_map/ppermute | solution.py:29
  2.9 10.4 %collective-permute-start.6 = (bf16[2,128,512]{2,1,0:T(8,128)(2,1)S(1)}, bf16[2,128,512]{2,1,0:T(8,128)(2,1)S(1)}, u32[]{:S(2)}, u32[]{:S(2)}) collective-permute-start(bf16[2,128,512]{2,1,0:T(8,128)(2,1)S(1)} %get-tuple-element.23), channel_id=1, source_target_pairs={{0,1},{1,0},{2,3},{3,2},{4,5},{5,4},{6,7},{7,6},{8,9},{9,8},{10,11... | collective-permute-start | bytes 786440 | tf_op jit(solution)/shard_map/ppermute | solution.py:29
  5.8 8.9 %collective-permute-start.7 = (bf16[2,128,512]{2,1,0:T(8,128)(2,1)S(1)}, bf16[2,128,512]{2,1,0:T(8,128)(2,1)S(1)}, u32[]{:S(2)}, u32[]{:S(2)}) collective-permute-start(bf16[2,128,512]{2,1,0:T(8,128)(2,1)S(1)} %get-tuple-element.24), channel_id=1, source_target_pairs={{0,2},{1,3},{2,0},{3,1},{4,6},{5,7},{6,4},{7,5},{8,10},{9,11},{10,... | collective-permute-start | bytes 786440 | tf_op jit(solution)/shard_map/ppermute | solution.py:29
  7.3 7.7 %collective-permute-start.8 = (bf16[2,128,512]{2,1,0:T(8,128)(2,1)S(1)}, bf16[2,128,512]{2,1,0:T(8,128)(2,1)S(1)}, u32[]{:S(2)}, u32[]{:S(2)}) collective-permute-start(bf16[2,128,512]{2,1,0:T(8,128)(2,1)S(1)} %get-tuple-element.25), channel_id=1, source_target_pairs={{0,4},{1,5},{2,6},{3,7},{4,0},{5,1},{6,2},{7,3},{8,12},{9,13},{10,... | collective-permute-start | bytes 786440 | tf_op jit(solution)/shard_map/ppermute | solution.py:29
  10.3 1.5 %collective-permute-start.2 = (f32[392,128]{1,0:T(8,128)S(1)}, f32[392,128]{1,0:T(8,128)S(1)}, u32[]{:S(2)}, u32[]{:S(2)}) collective-permute-start(f32[392,128]{1,0:T(8,128)S(1)} %products.1.refs_0_), channel_id=1, source_target_pairs={{0,16},{16,0},{1,17},{17,1},{2,18},{18,2},{3,19},{19,3},{4,20},{20... | collective-permute-start | bytes 602120 | tf_op jit(solution)/shard_map/ppermute | solution.py:29
  12.2 4.2 %collective-permute-start.5 = (bf16[208,128]{1,0:T(8,128)(2,1)S(1)}, bf16[208,128]{1,0:T(8,128)(2,1)S(1)}, u32[]{:S(2)}, u32[]{:S(2)}) collective-permute-start(bf16[208,128]{1,0:T(8,128)(2,1)S(1)} %relay.1.refs_0_), channel_id=1, source_target_pairs={{0,4},{1,5},{2,6},{3,7},{4,0},{5,1},{6,2},{7,3},{8,12},{9,13},{10,... | collective-permute-start | bytes 159752 | tf_op jit(solution)/shard_map/ppermute | solution.py:29
  12.7 4.1 %collective-permute-start.4 = (bf16[208,128]{1,0:T(8,128)(2,1)S(1)}, bf16[208,128]{1,0:T(8,128)(2,1)S(1)}, u32[]{:S(2)}, u32[]{:S(2)}) collective-permute-start(bf16[208,128]{1,0:T(8,128)(2,1)S(1)} %relay.1.refs_0_), channel_id=1, source_target_pairs={{0,2},{1,3},{2,0},{3,1},{4,6},{5,7},{6,4},{7,5},{8,10},{9,11},{10,... | collective-permute-start | bytes 159752 | tf_op jit(solution)/shard_map/ppermute | solution.py:29
  13.3 4.1 %collective-permute-start.3 = (bf16[208,128]{1,0:T(8,128)(2,1)S(1)}, bf16[208,128]{1,0:T(8,128)(2,1)S(1)}, u32[]{:S(2)}, u32[]{:S(2)}) collective-permute-start(bf16[208,128]{1,0:T(8,128)(2,1)S(1)} %relay.1.refs_0_), channel_id=1, source_target_pairs={{0,1},{1,0},{2,3},{3,2},{4,5},{5,4},{6,7},{7,6},{8,9},{9,8},{10,11... | collective-permute-start | bytes 159752 | tf_op jit(solution)/shard_map/ppermute | solution.py:29
  15.1 2.7 %collective-permute-start.9 = (bf16[2,512,512]{2,1,0:T(8,128)(2,1)S(1)}, bf16[2,512,512]{2,1,0:T(8,128)(2,1)S(1)}, u32[]{:S(2)}, u32[]{:S(2)}) collective-permute-start(bf16[2,512,512]{2,1,0:T(8,128)(2,1)S(1)} %stack.1.refs_4_), channel_id=1, source_target_pairs={{0,16},{16,0},{1,17},{17,1},{2,18},{18,2},{3,19},{19,3},{4,20},{20... | collective-permute-start | bytes 3145736 | tf_op jit(solution)/shard_map/ppermute | solution.py:29
  18.3 5.4 %collective-permute-start.10 = (bf16[2,64,256]{2,1,0:T(8,128)(2,1)S(1)}, bf16[2,64,256]{2,1,0:T(8,128)(2,1)S(1)}, u32[]{:S(2)}, u32[]{:S(2)}) collective-permute-start(bf16[2,64,256]{2,1,0:T(8,128)(2,1)S(1)} %get-tuple-element.37), channel_id=1, source_target_pairs={{0,8},{1,9},{2,10},{3,11},{4,12},{5,13},{6,14},{7,15},{8,0},{9,1},... | collective-permute-start | bytes 196616 | tf_op jit(solution)/shard_map/ppermute | solution.py:29
  21.0 8.5 %collective-permute-start.11 = (bf16[2,64,256]{2,1,0:T(8,128)(2,1)S(1)}, bf16[2,64,256]{2,1,0:T(8,128)(2,1)S(1)}, u32[]{:S(2)}, u32[]{:S(2)}) collective-permute-start(bf16[2,64,256]{2,1,0:T(8,128)(2,1)S(1)} %get-tuple-element.38), channel_id=1, source_target_pairs={{0,15},{1,14},{2,13},{3,12},{4,11},{5,10},{6,9},{7,8},{8,7},{9,6},... | collective-permute-start | bytes 196616 | tf_op jit(solution)/shard_map/ppermute | solution.py:29
  23.5 6.4 %collective-permute-start.12 = (bf16[2,64,256]{2,1,0:T(8,128)(2,1)S(1)}, bf16[2,64,256]{2,1,0:T(8,128)(2,1)S(1)}, u32[]{:S(2)}, u32[]{:S(2)}) collective-permute-start(bf16[2,64,256]{2,1,0:T(8,128)(2,1)S(1)} %get-tuple-element.39), channel_id=1, source_target_pairs={{0,7},{1,6},{2,5},{3,4},{4,3},{5,2},{6,1},{7,0},{8,15},{9,14},{10,... | collective-permute-start | bytes 196616 | tf_op jit(solution)/shard_map/ppermute | solution.py:29

commit v10 on v9

--- a/solution.py
+++ b/solution.py
@@ -11,7 +11,7 @@
 VMEM_BYTES = 32 * 1024 * 1024
 MEMBERS = 4
 STAR = True
-TWIST = 0
+TWIST = 4
 COST_PRODUCTS = 12
 COST_SMALL = 0.1
 COST_GRADS = 10
@@ -586,7 +586,7 @@
         parcels[1:] = [v.astype(bf16) for v in parcels[1:]]
 
     total = parcels[0]
-    for r in (*range(slots // 2, slots), *range(1, slots // 2)):
+    for r in range(slots - 1, 0, -1):
         received = from_partner(parcels[r], "dp", mask(r, group, chunks))
         total = total + received.astype(f32)
     return (total[0][None], total[1][None])

time: 30.7 us -> 30.7 us (level)
  starting transfers between devices: 14.5 us -> 15.7 us
  waiting for transfers between devices: 10.1 us -> 8.92 us
    ppermute x13, waiting for transfers between devices: 10.1 us -> 8.92 us  [from_partner(): lax.ppermute(value, axis, [(i, i ^ flip) for i in range(lax.axis_size(axi...]
    ppermute x13, starting transfers between devices: 14.5 us -> 15.7 us  [from_partner(): lax.ppermute(value, axis, [(i, i ^ flip) for i in range(lax.axis_size(axi...]
  transfers between devices with their start and end apart: 13 -> 13, of which waited for: 7 -> 8; matrix products, arithmetic and copies ran while one was open for 0% -> 0% of each run, Pallas kernels for 8% -> 8%
where the time goes in v10:
time: 30.7 us; the launch traced here: 30.6 us
  starting transfers between devices  15.7 us (51%)
  waiting for transfers between devices  8.92 us (29%)
  Pallas kernels  4.55 us (15%)
  between operations  0.72 us (2%)
  local copies, waits for them, and re-layouts  0.66 us (2%)
    ppermute x13, starting transfers between devices, from_partner(): lax.ppermute(value, axis, [(i, i ^ flip) for i in range(lax.axis_size(axi...  15.7 us
    ppermute x13, waiting for transfers between devices, from_partner(): lax.ppermute(value, axis, [(i, i ^ flip) for i in range(lax.axis_size(axi...  8.92 us
    pallas_call x1, Pallas kernels, per_device(): pl.pallas_call(functools.partial(pack_kernel, width, group, chunks), out_...  1.6 us
    pallas_call x1, Pallas kernels, per_device(): pl.pallas_call(functools.partial(products_kernel, layers), out_shape=[jax...  1.46 us
    pallas_call x2, Pallas kernels, per_device(): pl.pallas_call(functools.partial(grads_kernel, layers, bottle, width, gro...  0.88 us
    slice x1, local copies, waits for them, and re-layouts, per_device(): return (total[0][None], total[1][None])  0.66 us
  transfers between devices with their start and end apart: 13, of which 8 were waited for; matrix products, arithmetic and copies ran while one was open for 0% of the time, Pallas kernels for 8%

profile of v10, /device:TPU:0, one launch (start us, length us, event | category | flops | bytes accessed | tf_op | source)
XLA Modules:
  0.0 30.6 jit_solution(1518013729993796140)
XLA Ops:
  0.6 1.6 %pack.1 = (bf16[2,128,2048]{2,1,0:T(8,128)(2,1)S(1)}, bf16[80,4096]{1,0:T(8,128)(2,1)S(1)}, bf16[2,128,512]{2,1,0:T(8,128)(2,1)S(1)}, bf16[2,128,512]{2,1,0:T(8,128)(2,1)S(1)}, bf16[2,128,512]{2,1,0:T(8,128)(2,1)S(1)}) custom-call(bf16[2,32,2048]{2,1,0:T(8,128)(2,1)} %refs_0_.1, bf16[2,32,2048]{2,1,0:T(8,128)(2,1)} %refs_1_.1, bf16[2,32,2048]{2,1,0:T(8,128)(2,1)} %refs_2_.1, ...), custom_call_target="tpu_custom_call" | custom-call | tf_op jit(solution)/shard_map/pack/pallas_call | solution.py:423
  2.3 0.5 %collective-permute-start = (bf16[80,4096]{1,0:T(8,128)(2,1)S(1)}, bf16[80,4096]{1,0:T(8,128)(2,1)S(1)}, u32[]{:S(2)}, u32[]{:S(2)}) collective-permute-start(bf16[80,4096]{1,0:T(8,128)(2,1)S(1)} %get-tuple-element.22.refs_1_.refs_0_), channel_id=1, source_target_pairs={{0,16},{16,0},{1,17},{17,1},{2,18},{18,2},{3,19},{19,3},{4,20},{20... | collective-permute-start | bytes 1966088 | tf_op jit(solution)/shard_map/ppermute | solution.py:29
  2.9 2.9 %collective-permute-start.6 = (bf16[2,128,512]{2,1,0:T(8,128)(2,1)S(1)}, bf16[2,128,512]{2,1,0:T(8,128)(2,1)S(1)}, u32[]{:S(2)}, u32[]{:S(2)}) collective-permute-start(bf16[2,128,512]{2,1,0:T(8,128)(2,1)S(1)} %get-tuple-element.23), channel_id=1, source_target_pairs={{0,1},{1,0},{2,3},{3,2},{4,5},{5,4},{6,7},{7,6},{8,9},{9,8},{10,11... | collective-permute-start | bytes 786440 | tf_op jit(solution)/shard_map/ppermute | solution.py:29
  5.8 1.5 %collective-permute-start.7 = (bf16[2,128,512]{2,1,0:T(8,128)(2,1)S(1)}, bf16[2,128,512]{2,1,0:T(8,128)(2,1)S(1)}, u32[]{:S(2)}, u32[]{:S(2)}) collective-permute-start(bf16[2,128,512]{2,1,0:T(8,128)(2,1)S(1)} %get-tuple-element.24), channel_id=1, source_target_pairs={{0,2},{1,3},{2,0},{3,1},{4,6},{5,7},{6,4},{7,5},{8,10},{9,11},{10,... | collective-permute-start | bytes 786440 | tf_op jit(solution)/shard_map/ppermute | solution.py:29
  7.3 1.6 %collective-permute-start.8 = (bf16[2,128,512]{2,1,0:T(8,128)(2,1)S(1)}, bf16[2,128,512]{2,1,0:T(8,128)(2,1)S(1)}, u32[]{:S(2)}, u32[]{:S(2)}) collective-permute-start(bf16[2,128,512]{2,1,0:T(8,128)(2,1)S(1)} %get-tuple-element.25), channel_id=1, source_target_pairs={{0,4},{1,5},{2,6},{3,7},{4,0},{5,1},{6,2},{7,3},{8,12},{9,13},{10,... | collective-permute-start | bytes 786440 | tf_op jit(solution)/shard_map/ppermute | solution.py:29
  8.9 1.5 %products.1.refs_0_ = f32[392,128]{1,0:T(8,128)S(1)} custom-call(bf16[2,128,2048]{2,1,0:T(8,128)(2,1)S(1)} %get-tuple-element.27.refs_0_, bf16[80,4096]{1,0:T(8,128)(2,1)S(1)} %get-tuple-element.22.refs_1_.refs_0_, bf16[1,64,4096]{2,1,0:T(8,128)(2,1)S(1)} %copy-done, bf16[80,4096]{1,0:T(8,128)(2,1)S(1)} %collective-permute-done.refs_3_.refs_2_, ...), custom_call_target="tpu_custom_call" | custom-call | flops 13200000000 | tf_op jit(solution)/shard_map/products/pallas_call | solution.py:470
  10.4 1.4 %collective-permute-done.2.refs_1_ = f32[392,128]{1,0:T(8,128)S(1)} collective-permute-done((f32[392,128]{1,0:T(8,128)S(1)}, f32[392,128]{1,0:T(8,128)S(1)}, u32[]{:S(2)}, u32[]{:S(2)}) %collective-permute-start.2) | collective-permute-done | bytes 200736 | tf_op jit(solution)/shard_map/ppermute | solution.py:29
  11.8 0.4 %relay.1.refs_0_ = bf16[208,128]{1,0:T(8,128)(2,1)S(1)} custom-call(f32[392,128]{1,0:T(8,128)S(1)} %products.1.refs_0_, f32[392,128]{1,0:T(8,128)S(1)} %collective-permute-done.2.refs_1_), custom_call_target="tpu_custom_call" | custom-call | flops 110000000 | tf_op jit(solution)/shard_map/relay/pallas_call | solution.py:486
  12.2 0.5 %collective-permute-start.5 = (bf16[208,128]{1,0:T(8,128)(2,1)S(1)}, bf16[208,128]{1,0:T(8,128)(2,1)S(1)}, u32[]{:S(2)}, u32[]{:S(2)}) collective-permute-start(bf16[208,128]{1,0:T(8,128)(2,1)S(1)} %relay.1.refs_0_), channel_id=1, source_target_pairs={{0,4},{1,5},{2,6},{3,7},{4,0},{5,1},{6,2},{7,3},{8,12},{9,13},{10,... | collective-permute-start | bytes 159752 | tf_op jit(solution)/shard_map/ppermute | solution.py:29
  12.8 0.5 %collective-permute-start.4 = (bf16[208,128]{1,0:T(8,128)(2,1)S(1)}, bf16[208,128]{1,0:T(8,128)(2,1)S(1)}, u32[]{:S(2)}, u32[]{:S(2)}) collective-permute-start(bf16[208,128]{1,0:T(8,128)(2,1)S(1)} %relay.1.refs_0_), channel_id=1, source_target_pairs={{0,2},{1,3},{2,0},{3,1},{4,6},{5,7},{6,4},{7,5},{8,10},{9,11},{10,... | collective-permute-start | bytes 159752 | tf_op jit(solution)/shard_map/ppermute | solution.py:29
  13.3 1.4 %collective-permute-start.3 = (bf16[208,128]{1,0:T(8,128)(2,1)S(1)}, bf16[208,128]{1,0:T(8,128)(2,1)S(1)}, u32[]{:S(2)}, u32[]{:S(2)}) collective-permute-start(bf16[208,128]{1,0:T(8,128)(2,1)S(1)} %relay.1.refs_0_), channel_id=1, source_target_pairs={{0,1},{1,0},{2,3},{3,2},{4,5},{5,4},{6,7},{7,6},{8,9},{9,8},{10,11... | collective-permute-start | bytes 159752 | tf_op jit(solution)/shard_map/ppermute | solution.py:29
  14.6 0.4 %collective-permute-done.8.refs_3_ = bf16[2,128,512]{2,1,0:T(8,128)(2,1)S(1)} collective-permute-done((bf16[2,128,512]{2,1,0:T(8,128)(2,1)S(1)}, bf16[2,128,512]{2,1,0:T(8,128)(2,1)S(1)}, u32[]{:S(2)}, u32[]{:S(2)}) %collective-permute-start.8) | collective-permute-done | bytes 262176 | tf_op jit(solution)/shard_map/ppermute | solution.py:29
  15.3 1.1 %collective-permute-done.5.refs_3_ = bf16[208,128]{1,0:T(8,128)(2,1)S(1)} collective-permute-done((bf16[208,128]{1,0:T(8,128)(2,1)S(1)}, bf16[208,128]{1,0:T(8,128)(2,1)S(1)}, u32[]{:S(2)}, u32[]{:S(2)}) %collective-permute-start.5) | collective-permute-done | bytes 53280 | tf_op jit(solution)/shard_map/ppermute | solution.py:29
  16.4 0.5 %collective-permute-done.4.refs_2_ = bf16[208,128]{1,0:T(8,128)(2,1)S(1)} collective-permute-done((bf16[208,128]{1,0:T(8,128)(2,1)S(1)}, bf16[208,128]{1,0:T(8,128)(2,1)S(1)}, u32[]{:S(2)}, u32[]{:S(2)}) %collective-permute-start.4) | collective-permute-done | bytes 53280 | tf_op jit(solution)/shard_map/ppermute | solution.py:29
  16.9 0.5 %collective-permute-done.3.refs_1_ = bf16[208,128]{1,0:T(8,128)(2,1)S(1)} collective-permute-done((bf16[208,128]{1,0:T(8,128)(2,1)S(1)}, bf16[208,128]{1,0:T(8,128)(2,1)S(1)}, u32[]{:S(2)}, u32[]{:S(2)}) %collective-permute-start.3) | collective-permute-done | bytes 53280 | tf_op jit(solution)/shard_map/ppermute | solution.py:29
  17.4 0.5 %grads.2 = (f32[2,2,64,256]{3,2,1,0:T(8,128)S(1)}, bf16[256,512]{1,0:T(8,128)(2,1)S(1)}, bf16[2,64,64]{2,1,0:T(8,128)(2,1)S(1)}) custom-call(bf16[208,128]{1,0:T(8,128)(2,1)S(1)} %relay.1.refs_0_, bf16[208,128]{1,0:T(8,128)(2,1)S(1)} %collective-permute-done.3.refs_1_, bf16[208,128]{1,0:T(8,128)(2,1)S(1)} %collective-permute-done.4.refs_2_, ...), custom_call_target="tpu_custom_call" | custom-call | flops 11000000512 | tf_op jit(solution)/shard_map/grads/pallas_call | solution.py:567
  17.9 0.4 %grads.3 = (f32[2,64,256]{2,1,0:T(8,128)S(1)}, bf16[2,64,256]{2,1,0:T(8,128)(2,1)S(1)}, bf16[2,64,256]{2,1,0:T(8,128)(2,1)S(1)}, bf16[2,64,256]{2,1,0:T(8,128)(2,1)S(1)}) custom-call(bf16[256,512]{1,0:T(8,128)(2,1)S(1)} %get-tuple-element.33.refs_0_, bf16[2,64,64]{2,1,0:T(8,128)(2,1)S(1)} %get-tuple-element.34.refs_1_, ...), custom_call_target="tpu_custom_call" | custom-call | flops 11000000512 | tf_op jit(solution)/shard_map/grads/pallas_call | solution.py:567
  18.3 3.8 %collective-permute-start.10 = (bf16[2,64,256]{2,1,0:T(8,128)(2,1)S(1)}, bf16[2,64,256]{2,1,0:T(8,128)(2,1)S(1)}, u32[]{:S(2)}, u32[]{:S(2)}) collective-permute-start(bf16[2,64,256]{2,1,0:T(8,128)(2,1)S(1)} %get-tuple-element.37), channel_id=1, source_target_pairs={{0,11},{1,10},{2,9},{3,8},{4,15},{5,14},{6,13},{7,12},{8,3},{9,2},... | collective-permute-start | bytes 196616 | tf_op jit(solution)/shard_map/ppermute | solution.py:29
  22.1 1.4 %collective-permute-start.11 = (bf16[2,64,256]{2,1,0:T(8,128)(2,1)S(1)}, bf16[2,64,256]{2,1,0:T(8,128)(2,1)S(1)}, u32[]{:S(2)}, u32[]{:S(2)}) collective-permute-start(bf16[2,64,256]{2,1,0:T(8,128)(2,1)S(1)} %get-tuple-element.38), channel_id=1, source_target_pairs={{0,12},{1,13},{2,14},{3,15},{4,8},{5,9},{6,10},{7,11},{8,4},{9,5},... | collective-permute-start | bytes 196616 | tf_op jit(solution)/shard_map/ppermute | solution.py:29
  23.5 1.4 %collective-permute-start.12 = (bf16[2,64,256]{2,1,0:T(8,128)(2,1)S(1)}, bf16[2,64,256]{2,1,0:T(8,128)(2,1)S(1)}, u32[]{:S(2)}, u32[]{:S(2)}) collective-permute-start(bf16[2,64,256]{2,1,0:T(8,128)(2,1)S(1)} %get-tuple-element.39), channel_id=1, source_target_pairs={{0,7},{1,6},{2,5},{3,4},{4,3},{5,2},{6,1},{7,0},{8,15},{9,14},{10,... | collective-permute-start | bytes 196616 | tf_op jit(solution)/shard_map/ppermute | solution.py:29
  24.9 0.5 %collective-permute-done.10 = bf16[2,64,256]{2,1,0:T(8,128)(2,1)S(1)} collective-permute-done((bf16[2,64,256]{2,1,0:T(8,128)(2,1)S(1)}, bf16[2,64,256]{2,1,0:T(8,128)(2,1)S(1)}, u32[]{:S(2)}, u32[]{:S(2)}) %collective-permute-start.10) | collective-permute-done | bytes 65568 | tf_op jit(solution)/shard_map/ppermute | solution.py:29
  25.3 3.2 %collective-permute-done.11 = bf16[2,64,256]{2,1,0:T(8,128)(2,1)S(1)} collective-permute-done((bf16[2,64,256]{2,1,0:T(8,128)(2,1)S(1)}, bf16[2,64,256]{2,1,0:T(8,128)(2,1)S(1)}, u32[]{:S(2)}, u32[]{:S(2)}) %collective-permute-start.11) | collective-permute-done | bytes 65568 | tf_op jit(solution)/shard_map/ppermute | solution.py:29
  28.6 1.3 %collective-permute-done.12 = bf16[2,64,256]{2,1,0:T(8,128)(2,1)S(1)} collective-permute-done((bf16[2,64,256]{2,1,0:T(8,128)(2,1)S(1)}, bf16[2,64,256]{2,1,0:T(8,128)(2,1)S(1)}, u32[]{:S(2)}, u32[]{:S(2)}) %collective-permute-start.12) | collective-permute-done | bytes 65568 | tf_op jit(solution)/shard_map/ppermute | solution.py:29
  29.9 0.7 %fusion = (f32[1,64,256]{2,1,0:T(8,128)}, f32[1,64,256]{2,1,0:T(8,128)}) fusion(f32[2,64,256]{2,1,0:T(8,128)S(1)} %convert_add_fusion), kind=kLoop, calls=%fused_computation.1 | loop fusion | bytes 262144 | tf_op jit(solution)/shard_map/slice | solution.py:592
  (13 shorter events, 0.4 us)
Async XLA Ops:
  0.6 2.1 %copy-start = (bf16[1,64,4096]{2,1,0:T(8,128)(2,1)S(1)}, bf16[1,64,4096]{2,1,0:T(8,128)(2,1)}, u32[]{:S(2)}) copy-start(bf16[1,64,4096]{2,1,0:T(8,128)(2,1)} %refs_1_.2) | copy-start | bytes 1572868
  2.3 6.6 %collective-permute-start = (bf16[80,4096]{1,0:T(8,128)(2,1)S(1)}, bf16[80,4096]{1,0:T(8,128)(2,1)S(1)}, u32[]{:S(2)}, u32[]{:S(2)}) collective-permute-start(bf16[80,4096]{1,0:T(8,128)(2,1)S(1)} %get-tuple-element.22.refs_1_.refs_0_), channel_id=1, source_target_pairs={{0,16},{16,0},{1,17},{17,1},{2,18},{18,2},{3,19},{19,3},{4,20},{20... | collective-permute-start | bytes 1966088 | tf_op jit(solution)/shard_map/ppermute | solution.py:29
  2.8 6.1 %collective-permute-start.1 = (bf16[1,64,4096]{2,1,0:T(8,128)(2,1)S(1)}, bf16[1,64,4096]{2,1,0:T(8,128)(2,1)S(1)}, u32[]{:S(2)}, u32[]{:S(2)}) collective-permute-start(bf16[1,64,4096]{2,1,0:T(8,128)(2,1)S(1)} %copy-done), channel_id=1, source_target_pairs={{0,16},{16,0},{1,17},{17,1},{2,18},{18,2},{3,19},{19,3},{4,20},{20... | collective-permute-start | bytes 1572872 | tf_op jit(solution)/shard_map/ppermute | solution.py:29
  2.9 10.4 %collective-permute-start.6 = (bf16[2,128,512]{2,1,0:T(8,128)(2,1)S(1)}, bf16[2,128,512]{2,1,0:T(8,128)(2,1)S(1)}, u32[]{:S(2)}, u32[]{:S(2)}) collective-permute-start(bf16[2,128,512]{2,1,0:T(8,128)(2,1)S(1)} %get-tuple-element.23), channel_id=1, source_target_pairs={{0,1},{1,0},{2,3},{3,2},{4,5},{5,4},{6,7},{7,6},{8,9},{9,8},{10,11... | collective-permute-start | bytes 786440 | tf_op jit(solution)/shard_map/ppermute | solution.py:29
  5.8 8.9 %collective-permute-start.7 = (bf16[2,128,512]{2,1,0:T(8,128)(2,1)S(1)}, bf16[2,128,512]{2,1,0:T(8,128)(2,1)S(1)}, u32[]{:S(2)}, u32[]{:S(2)}) collective-permute-start(bf16[2,128,512]{2,1,0:T(8,128)(2,1)S(1)} %get-tuple-element.24), channel_id=1, source_target_pairs={{0,2},{1,3},{2,0},{3,1},{4,6},{5,7},{6,4},{7,5},{8,10},{9,11},{10,... | collective-permute-start | bytes 786440 | tf_op jit(solution)/shard_map/ppermute | solution.py:29
  7.3 7.7 %collective-permute-start.8 = (bf16[2,128,512]{2,1,0:T(8,128)(2,1)S(1)}, bf16[2,128,512]{2,1,0:T(8,128)(2,1)S(1)}, u32[]{:S(2)}, u32[]{:S(2)}) collective-permute-start(bf16[2,128,512]{2,1,0:T(8,128)(2,1)S(1)} %get-tuple-element.25), channel_id=1, source_target_pairs={{0,4},{1,5},{2,6},{3,7},{4,0},{5,1},{6,2},{7,3},{8,12},{9,13},{10,... | collective-permute-start | bytes 786440 | tf_op jit(solution)/shard_map/ppermute | solution.py:29
  10.3 1.5 %collective-permute-start.2 = (f32[392,128]{1,0:T(8,128)S(1)}, f32[392,128]{1,0:T(8,128)S(1)}, u32[]{:S(2)}, u32[]{:S(2)}) collective-permute-start(f32[392,128]{1,0:T(8,128)S(1)} %products.1.refs_0_), channel_id=1, source_target_pairs={{0,16},{16,0},{1,17},{17,1},{2,18},{18,2},{3,19},{19,3},{4,20},{20... | collective-permute-start | bytes 602120 | tf_op jit(solution)/shard_map/ppermute | solution.py:29
  12.2 4.2 %collective-permute-start.5 = (bf16[208,128]{1,0:T(8,128)(2,1)S(1)}, bf16[208,128]{1,0:T(8,128)(2,1)S(1)}, u32[]{:S(2)}, u32[]{:S(2)}) collective-permute-start(bf16[208,128]{1,0:T(8,128)(2,1)S(1)} %relay.1.refs_0_), channel_id=1, source_target_pairs={{0,4},{1,5},{2,6},{3,7},{4,0},{5,1},{6,2},{7,3},{8,12},{9,13},{10,... | collective-permute-start | bytes 159752 | tf_op jit(solution)/shard_map/ppermute | solution.py:29
  12.8 4.1 %collective-permute-start.4 = (bf16[208,128]{1,0:T(8,128)(2,1)S(1)}, bf16[208,128]{1,0:T(8,128)(2,1)S(1)}, u32[]{:S(2)}, u32[]{:S(2)}) collective-permute-start(bf16[208,128]{1,0:T(8,128)(2,1)S(1)} %relay.1.refs_0_), channel_id=1, source_target_pairs={{0,2},{1,3},{2,0},{3,1},{4,6},{5,7},{6,4},{7,5},{8,10},{9,11},{10,... | collective-permute-start | bytes 159752 | tf_op jit(solution)/shard_map/ppermute | solution.py:29
  13.3 4.1 %collective-permute-start.3 = (bf16[208,128]{1,0:T(8,128)(2,1)S(1)}, bf16[208,128]{1,0:T(8,128)(2,1)S(1)}, u32[]{:S(2)}, u32[]{:S(2)}) collective-permute-start(bf16[208,128]{1,0:T(8,128)(2,1)S(1)} %relay.1.refs_0_), channel_id=1, source_target_pairs={{0,1},{1,0},{2,3},{3,2},{4,5},{5,4},{6,7},{7,6},{8,9},{9,8},{10,11... | collective-permute-start | bytes 159752 | tf_op jit(solution)/shard_map/ppermute | solution.py:29
  15.1 2.7 %collective-permute-start.9 = (bf16[2,512,512]{2,1,0:T(8,128)(2,1)S(1)}, bf16[2,512,512]{2,1,0:T(8,128)(2,1)S(1)}, u32[]{:S(2)}, u32[]{:S(2)}) collective-permute-start(bf16[2,512,512]{2,1,0:T(8,128)(2,1)S(1)} %stack.1.refs_4_), channel_id=1, source_target_pairs={{0,16},{16,0},{1,17},{17,1},{2,18},{18,2},{3,19},{19,3},{4,20},{20... | collective-permute-start | bytes 3145736 | tf_op jit(solution)/shard_map/ppermute | solution.py:29
  18.3 7.0 %collective-permute-start.10 = (bf16[2,64,256]{2,1,0:T(8,128)(2,1)S(1)}, bf16[2,64,256]{2,1,0:T(8,128)(2,1)S(1)}, u32[]{:S(2)}, u32[]{:S(2)}) collective-permute-start(bf16[2,64,256]{2,1,0:T(8,128)(2,1)S(1)} %get-tuple-element.37), channel_id=1, source_target_pairs={{0,11},{1,10},{2,9},{3,8},{4,15},{5,14},{6,13},{7,12},{8,3},{9,2},... | collective-permute-start | bytes 196616 | tf_op jit(solution)/shard_map/ppermute | solution.py:29
  22.1 6.4 %collective-permute-start.11 = (bf16[2,64,256]{2,1,0:T(8,128)(2,1)S(1)}, bf16[2,64,256]{2,1,0:T(8,128)(2,1)S(1)}, u32[]{:S(2)}, u32[]{:S(2)}) collective-permute-start(bf16[2,64,256]{2,1,0:T(8,128)(2,1)S(1)} %get-tuple-element.38), channel_id=1, source_target_pairs={{0,12},{1,13},{2,14},{3,15},{4,8},{5,9},{6,10},{7,11},{8,4},{9,5},... | collective-permute-start | bytes 196616 | tf_op jit(solution)/shard_map/ppermute | solution.py:29
  23.5 6.4 %collective-permute-start.12 = (bf16[2,64,256]{2,1,0:T(8,128)(2,1)S(1)}, bf16[2,64,256]{2,1,0:T(8,128)(2,1)S(1)}, u32[]{:S(2)}, u32[]{:S(2)}) collective-permute-start(bf16[2,64,256]{2,1,0:T(8,128)(2,1)S(1)} %get-tuple-element.39), channel_id=1, source_target_pairs={{0,7},{1,6},{2,5},{3,4},{4,3},{5,2},{6,1},{7,0},{8,15},{9,14},{10,... | collective-permute-start | bytes 196616 | tf_op jit(solution)/shard_map/ppermute | solution.py:29

commit v11 on v9

--- a/solution.py
+++ b/solution.py
@@ -11,7 +11,7 @@
 VMEM_BYTES = 32 * 1024 * 1024
 MEMBERS = 4
 STAR = True
-TWIST = 0
+TWIST = 2
 COST_PRODUCTS = 12
 COST_SMALL = 0.1
 COST_GRADS = 10

time: 30.7 us -> 30.7 us (level)
  transfers between devices with their start and end apart: 13 -> 13, of which waited for: 7 -> 8; matrix products, arithmetic and copies ran while one was open for 0% -> 0% of each run, Pallas kernels for 8% -> 8%
where the time goes in v11:
time: 30.7 us; the launch traced here: 30.6 us
  starting transfers between devices  14.8 us (48%)
  waiting for transfers between devices  9.85 us (32%)
  Pallas kernels  4.55 us (15%)
  between operations  0.72 us (2%)
  local copies, waits for them, and re-layouts  0.66 us (2%)
    ppermute x13, starting transfers between devices, from_partner(): lax.ppermute(value, axis, [(i, i ^ flip) for i in range(lax.axis_size(axi...  14.8 us
    ppermute x13, waiting for transfers between devices, from_partner(): lax.ppermute(value, axis, [(i, i ^ flip) for i in range(lax.axis_size(axi...  9.85 us
    pallas_call x1, Pallas kernels, per_device(): pl.pallas_call(functools.partial(pack_kernel, width, group, chunks), out_...  1.6 us
    pallas_call x1, Pallas kernels, per_device(): pl.pallas_call(functools.partial(products_kernel, layers), out_shape=[jax...  1.46 us
    pallas_call x2, Pallas kernels, per_device(): pl.pallas_call(functools.partial(grads_kernel, layers, bottle, width, gro...  0.88 us
    slice x1, local copies, waits for them, and re-layouts, per_device(): return (total[0][None], total[1][None])  0.66 us
  transfers between devices with their start and end apart: 13, of which 8 were waited for; matrix products, arithmetic and copies ran while one was open for 0% of the time, Pallas kernels for 8%

profile of v11, /device:TPU:0, one launch (start us, length us, event | category | flops | bytes accessed | tf_op | source)
XLA Modules:
  0.0 30.6 jit_solution(1048998262945779870)
XLA Ops:
  0.6 1.6 %pack.1 = (bf16[2,128,2048]{2,1,0:T(8,128)(2,1)S(1)}, bf16[80,4096]{1,0:T(8,128)(2,1)S(1)}, bf16[2,128,512]{2,1,0:T(8,128)(2,1)S(1)}, bf16[2,128,512]{2,1,0:T(8,128)(2,1)S(1)}, bf16[2,128,512]{2,1,0:T(8,128)(2,1)S(1)}) custom-call(bf16[2,32,2048]{2,1,0:T(8,128)(2,1)} %refs_0_.1, bf16[2,32,2048]{2,1,0:T(8,128)(2,1)} %refs_1_.1, bf16[2,32,2048]{2,1,0:T(8,128)(2,1)} %refs_2_.1, ...), custom_call_target="tpu_custom_call" | custom-call | tf_op jit(solution)/shard_map/pack/pallas_call | solution.py:423
  2.3 0.5 %collective-permute-start = (bf16[80,4096]{1,0:T(8,128)(2,1)S(1)}, bf16[80,4096]{1,0:T(8,128)(2,1)S(1)}, u32[]{:S(2)}, u32[]{:S(2)}) collective-permute-start(bf16[80,4096]{1,0:T(8,128)(2,1)S(1)} %get-tuple-element.22.refs_1_.refs_0_), channel_id=1, source_target_pairs={{0,16},{16,0},{1,17},{17,1},{2,18},{18,2},{3,19},{19,3},{4,20},{20... | collective-permute-start | bytes 1966088 | tf_op jit(solution)/shard_map/ppermute | solution.py:29
  2.9 2.9 %collective-permute-start.6 = (bf16[2,128,512]{2,1,0:T(8,128)(2,1)S(1)}, bf16[2,128,512]{2,1,0:T(8,128)(2,1)S(1)}, u32[]{:S(2)}, u32[]{:S(2)}) collective-permute-start(bf16[2,128,512]{2,1,0:T(8,128)(2,1)S(1)} %get-tuple-element.23), channel_id=1, source_target_pairs={{0,1},{1,0},{2,3},{3,2},{4,5},{5,4},{6,7},{7,6},{8,9},{9,8},{10,11... | collective-permute-start | bytes 786440 | tf_op jit(solution)/shard_map/ppermute | solution.py:29
  5.8 1.5 %collective-permute-start.7 = (bf16[2,128,512]{2,1,0:T(8,128)(2,1)S(1)}, bf16[2,128,512]{2,1,0:T(8,128)(2,1)S(1)}, u32[]{:S(2)}, u32[]{:S(2)}) collective-permute-start(bf16[2,128,512]{2,1,0:T(8,128)(2,1)S(1)} %get-tuple-element.24), channel_id=1, source_target_pairs={{0,2},{1,3},{2,0},{3,1},{4,6},{5,7},{6,4},{7,5},{8,10},{9,11},{10,... | collective-permute-start | bytes 786440 | tf_op jit(solution)/shard_map/ppermute | solution.py:29
  7.3 1.6 %collective-permute-start.8 = (bf16[2,128,512]{2,1,0:T(8,128)(2,1)S(1)}, bf16[2,128,512]{2,1,0:T(8,128)(2,1)S(1)}, u32[]{:S(2)}, u32[]{:S(2)}) collective-permute-start(bf16[2,128,512]{2,1,0:T(8,128)(2,1)S(1)} %get-tuple-element.25), channel_id=1, source_target_pairs={{0,4},{1,5},{2,6},{3,7},{4,0},{5,1},{6,2},{7,3},{8,12},{9,13},{10,... | collective-permute-start | bytes 786440 | tf_op jit(solution)/shard_map/ppermute | solution.py:29
  8.9 1.5 %products.1.refs_0_ = f32[392,128]{1,0:T(8,128)S(1)} custom-call(bf16[2,128,2048]{2,1,0:T(8,128)(2,1)S(1)} %get-tuple-element.27.refs_0_, bf16[80,4096]{1,0:T(8,128)(2,1)S(1)} %get-tuple-element.22.refs_1_.refs_0_, bf16[1,64,4096]{2,1,0:T(8,128)(2,1)S(1)} %copy-done, bf16[80,4096]{1,0:T(8,128)(2,1)S(1)} %collective-permute-done.refs_3_.refs_2_, ...), custom_call_target="tpu_custom_call" | custom-call | flops 13200000000 | tf_op jit(solution)/shard_map/products/pallas_call | solution.py:470
  10.4 1.4 %collective-permute-done.2.refs_1_ = f32[392,128]{1,0:T(8,128)S(1)} collective-permute-done((f32[392,128]{1,0:T(8,128)S(1)}, f32[392,128]{1,0:T(8,128)S(1)}, u32[]{:S(2)}, u32[]{:S(2)}) %collective-permute-start.2) | collective-permute-done | bytes 200736 | tf_op jit(solution)/shard_map/ppermute | solution.py:29
  11.8 0.4 %relay.1.refs_0_ = bf16[208,128]{1,0:T(8,128)(2,1)S(1)} custom-call(f32[392,128]{1,0:T(8,128)S(1)} %products.1.refs_0_, f32[392,128]{1,0:T(8,128)S(1)} %collective-permute-done.2.refs_1_), custom_call_target="tpu_custom_call" | custom-call | flops 110000000 | tf_op jit(solution)/shard_map/relay/pallas_call | solution.py:486
  12.2 0.5 %collective-permute-start.5 = (bf16[208,128]{1,0:T(8,128)(2,1)S(1)}, bf16[208,128]{1,0:T(8,128)(2,1)S(1)}, u32[]{:S(2)}, u32[]{:S(2)}) collective-permute-start(bf16[208,128]{1,0:T(8,128)(2,1)S(1)} %relay.1.refs_0_), channel_id=1, source_target_pairs={{0,4},{1,5},{2,6},{3,7},{4,0},{5,1},{6,2},{7,3},{8,12},{9,13},{10,... | collective-permute-start | bytes 159752 | tf_op jit(solution)/shard_map/ppermute | solution.py:29
  12.8 0.5 %collective-permute-start.4 = (bf16[208,128]{1,0:T(8,128)(2,1)S(1)}, bf16[208,128]{1,0:T(8,128)(2,1)S(1)}, u32[]{:S(2)}, u32[]{:S(2)}) collective-permute-start(bf16[208,128]{1,0:T(8,128)(2,1)S(1)} %relay.1.refs_0_), channel_id=1, source_target_pairs={{0,2},{1,3},{2,0},{3,1},{4,6},{5,7},{6,4},{7,5},{8,10},{9,11},{10,... | collective-permute-start | bytes 159752 | tf_op jit(solution)/shard_map/ppermute | solution.py:29
  13.3 1.4 %collective-permute-start.3 = (bf16[208,128]{1,0:T(8,128)(2,1)S(1)}, bf16[208,128]{1,0:T(8,128)(2,1)S(1)}, u32[]{:S(2)}, u32[]{:S(2)}) collective-permute-start(bf16[208,128]{1,0:T(8,128)(2,1)S(1)} %relay.1.refs_0_), channel_id=1, source_target_pairs={{0,1},{1,0},{2,3},{3,2},{4,5},{5,4},{6,7},{7,6},{8,9},{9,8},{10,11... | collective-permute-start | bytes 159752 | tf_op jit(solution)/shard_map/ppermute | solution.py:29
  14.6 0.4 %collective-permute-done.8.refs_3_ = bf16[2,128,512]{2,1,0:T(8,128)(2,1)S(1)} collective-permute-done((bf16[2,128,512]{2,1,0:T(8,128)(2,1)S(1)}, bf16[2,128,512]{2,1,0:T(8,128)(2,1)S(1)}, u32[]{:S(2)}, u32[]{:S(2)}) %collective-permute-start.8) | collective-permute-done | bytes 262176 | tf_op jit(solution)/shard_map/ppermute | solution.py:29
  15.3 1.1 %collective-permute-done.5.refs_3_ = bf16[208,128]{1,0:T(8,128)(2,1)S(1)} collective-permute-done((bf16[208,128]{1,0:T(8,128)(2,1)S(1)}, bf16[208,128]{1,0:T(8,128)(2,1)S(1)}, u32[]{:S(2)}, u32[]{:S(2)}) %collective-permute-start.5) | collective-permute-done | bytes 53280 | tf_op jit(solution)/shard_map/ppermute | solution.py:29
  16.4 0.5 %collective-permute-done.4.refs_2_ = bf16[208,128]{1,0:T(8,128)(2,1)S(1)} collective-permute-done((bf16[208,128]{1,0:T(8,128)(2,1)S(1)}, bf16[208,128]{1,0:T(8,128)(2,1)S(1)}, u32[]{:S(2)}, u32[]{:S(2)}) %collective-permute-start.4) | collective-permute-done | bytes 53280 | tf_op jit(solution)/shard_map/ppermute | solution.py:29
  16.9 0.5 %collective-permute-done.3.refs_1_ = bf16[208,128]{1,0:T(8,128)(2,1)S(1)} collective-permute-done((bf16[208,128]{1,0:T(8,128)(2,1)S(1)}, bf16[208,128]{1,0:T(8,128)(2,1)S(1)}, u32[]{:S(2)}, u32[]{:S(2)}) %collective-permute-start.3) | collective-permute-done | bytes 53280 | tf_op jit(solution)/shard_map/ppermute | solution.py:29
  17.4 0.5 %grads.2 = (f32[2,2,64,256]{3,2,1,0:T(8,128)S(1)}, bf16[256,512]{1,0:T(8,128)(2,1)S(1)}, bf16[2,64,64]{2,1,0:T(8,128)(2,1)S(1)}) custom-call(bf16[208,128]{1,0:T(8,128)(2,1)S(1)} %relay.1.refs_0_, bf16[208,128]{1,0:T(8,128)(2,1)S(1)} %collective-permute-done.3.refs_1_, bf16[208,128]{1,0:T(8,128)(2,1)S(1)} %collective-permute-done.4.refs_2_, ...), custom_call_target="tpu_custom_call" | custom-call | flops 11000000512 | tf_op jit(solution)/shard_map/grads/pallas_call | solution.py:567
  17.9 0.4 %grads.3 = (f32[2,64,256]{2,1,0:T(8,128)S(1)}, bf16[2,64,256]{2,1,0:T(8,128)(2,1)S(1)}, bf16[2,64,256]{2,1,0:T(8,128)(2,1)S(1)}, bf16[2,64,256]{2,1,0:T(8,128)(2,1)S(1)}) custom-call(bf16[256,512]{1,0:T(8,128)(2,1)S(1)} %get-tuple-element.33.refs_0_, bf16[2,64,64]{2,1,0:T(8,128)(2,1)S(1)} %get-tuple-element.34.refs_1_, ...), custom_call_target="tpu_custom_call" | custom-call | flops 11000000512 | tf_op jit(solution)/shard_map/grads/pallas_call | solution.py:567
  18.3 3.6 %collective-permute-start.10 = (bf16[2,64,256]{2,1,0:T(8,128)(2,1)S(1)}, bf16[2,64,256]{2,1,0:T(8,128)(2,1)S(1)}, u32[]{:S(2)}, u32[]{:S(2)}) collective-permute-start(bf16[2,64,256]{2,1,0:T(8,128)(2,1)S(1)} %get-tuple-element.37), channel_id=1, source_target_pairs={{0,10},{1,11},{2,8},{3,9},{4,14},{5,15},{6,12},{7,13},{8,2},{9,3},... | collective-permute-start | bytes 196616 | tf_op jit(solution)/shard_map/ppermute | solution.py:29
  21.9 1.6 %collective-permute-start.11 = (bf16[2,64,256]{2,1,0:T(8,128)(2,1)S(1)}, bf16[2,64,256]{2,1,0:T(8,128)(2,1)S(1)}, u32[]{:S(2)}, u32[]{:S(2)}) collective-permute-start(bf16[2,64,256]{2,1,0:T(8,128)(2,1)S(1)} %get-tuple-element.38), channel_id=1, source_target_pairs={{0,13},{1,12},{2,15},{3,14},{4,9},{5,8},{6,11},{7,10},{8,5},{9,4},... | collective-permute-start | bytes 196616 | tf_op jit(solution)/shard_map/ppermute | solution.py:29
  23.5 0.5 %collective-permute-start.12 = (bf16[2,64,256]{2,1,0:T(8,128)(2,1)S(1)}, bf16[2,64,256]{2,1,0:T(8,128)(2,1)S(1)}, u32[]{:S(2)}, u32[]{:S(2)}) collective-permute-start(bf16[2,64,256]{2,1,0:T(8,128)(2,1)S(1)} %get-tuple-element.39), channel_id=1, source_target_pairs={{0,7},{1,6},{2,5},{3,4},{4,3},{5,2},{6,1},{7,0},{8,15},{9,14},{10,... | collective-permute-start | bytes 196616 | tf_op jit(solution)/shard_map/ppermute | solution.py:29
  24.0 0.5 %collective-permute-done.10 = bf16[2,64,256]{2,1,0:T(8,128)(2,1)S(1)} collective-permute-done((bf16[2,64,256]{2,1,0:T(8,128)(2,1)S(1)}, bf16[2,64,256]{2,1,0:T(8,128)(2,1)S(1)}, u32[]{:S(2)}, u32[]{:S(2)}) %collective-permute-start.10) | collective-permute-done | bytes 65568 | tf_op jit(solution)/shard_map/ppermute | solution.py:29
  24.4 5.0 %collective-permute-done.11 = bf16[2,64,256]{2,1,0:T(8,128)(2,1)S(1)} collective-permute-done((bf16[2,64,256]{2,1,0:T(8,128)(2,1)S(1)}, bf16[2,64,256]{2,1,0:T(8,128)(2,1)S(1)}, u32[]{:S(2)}, u32[]{:S(2)}) %collective-permute-start.11) | collective-permute-done | bytes 65568 | tf_op jit(solution)/shard_map/ppermute | solution.py:29
  29.4 0.5 %collective-permute-done.12 = bf16[2,64,256]{2,1,0:T(8,128)(2,1)S(1)} collective-permute-done((bf16[2,64,256]{2,1,0:T(8,128)(2,1)S(1)}, bf16[2,64,256]{2,1,0:T(8,128)(2,1)S(1)}, u32[]{:S(2)}, u32[]{:S(2)}) %collective-permute-start.12) | collective-permute-done | bytes 65568 | tf_op jit(solution)/shard_map/ppermute | solution.py:29
  29.9 0.7 %fusion = (f32[1,64,256]{2,1,0:T(8,128)}, f32[1,64,256]{2,1,0:T(8,128)}) fusion(f32[2,64,256]{2,1,0:T(8,128)S(1)} %convert_add_fusion), kind=kLoop, calls=%fused_computation.1 | loop fusion | bytes 262144 | tf_op jit(solution)/shard_map/slice | solution.py:592
  (13 shorter events, 0.4 us)
Async XLA Ops:
  0.6 2.1 %copy-start = (bf16[1,64,4096]{2,1,0:T(8,128)(2,1)S(1)}, bf16[1,64,4096]{2,1,0:T(8,128)(2,1)}, u32[]{:S(2)}) copy-start(bf16[1,64,4096]{2,1,0:T(8,128)(2,1)} %refs_1_.2) | copy-start | bytes 1572868
  2.3 6.6 %collective-permute-start = (bf16[80,4096]{1,0:T(8,128)(2,1)S(1)}, bf16[80,4096]{1,0:T(8,128)(2,1)S(1)}, u32[]{:S(2)}, u32[]{:S(2)}) collective-permute-start(bf16[80,4096]{1,0:T(8,128)(2,1)S(1)} %get-tuple-element.22.refs_1_.refs_0_), channel_id=1, source_target_pairs={{0,16},{16,0},{1,17},{17,1},{2,18},{18,2},{3,19},{19,3},{4,20},{20... | collective-permute-start | bytes 1966088 | tf_op jit(solution)/shard_map/ppermute | solution.py:29
  2.8 6.1 %collective-permute-start.1 = (bf16[1,64,4096]{2,1,0:T(8,128)(2,1)S(1)}, bf16[1,64,4096]{2,1,0:T(8,128)(2,1)S(1)}, u32[]{:S(2)}, u32[]{:S(2)}) collective-permute-start(bf16[1,64,4096]{2,1,0:T(8,128)(2,1)S(1)} %copy-done), channel_id=1, source_target_pairs={{0,16},{16,0},{1,17},{17,1},{2,18},{18,2},{3,19},{19,3},{4,20},{20... | collective-permute-start | bytes 1572872 | tf_op jit(solution)/shard_map/ppermute | solution.py:29
  2.9 10.4 %collective-permute-start.6 = (bf16[2,128,512]{2,1,0:T(8,128)(2,1)S(1)}, bf16[2,128,512]{2,1,0:T(8,128)(2,1)S(1)}, u32[]{:S(2)}, u32[]{:S(2)}) collective-permute-start(bf16[2,128,512]{2,1,0:T(8,128)(2,1)S(1)} %get-tuple-element.23), channel_id=1, source_target_pairs={{0,1},{1,0},{2,3},{3,2},{4,5},{5,4},{6,7},{7,6},{8,9},{9,8},{10,11... | collective-permute-start | bytes 786440 | tf_op jit(solution)/shard_map/ppermute | solution.py:29
  5.8 8.9 %collective-permute-start.7 = (bf16[2,128,512]{2,1,0:T(8,128)(2,1)S(1)}, bf16[2,128,512]{2,1,0:T(8,128)(2,1)S(1)}, u32[]{:S(2)}, u32[]{:S(2)}) collective-permute-start(bf16[2,128,512]{2,1,0:T(8,128)(2,1)S(1)} %get-tuple-element.24), channel_id=1, source_target_pairs={{0,2},{1,3},{2,0},{3,1},{4,6},{5,7},{6,4},{7,5},{8,10},{9,11},{10,... | collective-permute-start | bytes 786440 | tf_op jit(solution)/shard_map/ppermute | solution.py:29
  7.3 7.7 %collective-permute-start.8 = (bf16[2,128,512]{2,1,0:T(8,128)(2,1)S(1)}, bf16[2,128,512]{2,1,0:T(8,128)(2,1)S(1)}, u32[]{:S(2)}, u32[]{:S(2)}) collective-permute-start(bf16[2,128,512]{2,1,0:T(8,128)(2,1)S(1)} %get-tuple-element.25), channel_id=1, source_target_pairs={{0,4},{1,5},{2,6},{3,7},{4,0},{5,1},{6,2},{7,3},{8,12},{9,13},{10,... | collective-permute-start | bytes 786440 | tf_op jit(solution)/shard_map/ppermute | solution.py:29
  10.3 1.5 %collective-permute-start.2 = (f32[392,128]{1,0:T(8,128)S(1)}, f32[392,128]{1,0:T(8,128)S(1)}, u32[]{:S(2)}, u32[]{:S(2)}) collective-permute-start(f32[392,128]{1,0:T(8,128)S(1)} %products.1.refs_0_), channel_id=1, source_target_pairs={{0,16},{16,0},{1,17},{17,1},{2,18},{18,2},{3,19},{19,3},{4,20},{20... | collective-permute-start | bytes 602120 | tf_op jit(solution)/shard_map/ppermute | solution.py:29
  12.2 4.2 %collective-permute-start.5 = (bf16[208,128]{1,0:T(8,128)(2,1)S(1)}, bf16[208,128]{1,0:T(8,128)(2,1)S(1)}, u32[]{:S(2)}, u32[]{:S(2)}) collective-permute-start(bf16[208,128]{1,0:T(8,128)(2,1)S(1)} %relay.1.refs_0_), channel_id=1, source_target_pairs={{0,4},{1,5},{2,6},{3,7},{4,0},{5,1},{6,2},{7,3},{8,12},{9,13},{10,... | collective-permute-start | bytes 159752 | tf_op jit(solution)/shard_map/ppermute | solution.py:29
  12.8 4.1 %collective-permute-start.4 = (bf16[208,128]{1,0:T(8,128)(2,1)S(1)}, bf16[208,128]{1,0:T(8,128)(2,1)S(1)}, u32[]{:S(2)}, u32[]{:S(2)}) collective-permute-start(bf16[208,128]{1,0:T(8,128)(2,1)S(1)} %relay.1.refs_0_), channel_id=1, source_target_pairs={{0,2},{1,3},{2,0},{3,1},{4,6},{5,7},{6,4},{7,5},{8,10},{9,11},{10,... | collective-permute-start | bytes 159752 | tf_op jit(solution)/shard_map/ppermute | solution.py:29
  13.3 4.1 %collective-permute-start.3 = (bf16[208,128]{1,0:T(8,128)(2,1)S(1)}, bf16[208,128]{1,0:T(8,128)(2,1)S(1)}, u32[]{:S(2)}, u32[]{:S(2)}) collective-permute-start(bf16[208,128]{1,0:T(8,128)(2,1)S(1)} %relay.1.refs_0_), channel_id=1, source_target_pairs={{0,1},{1,0},{2,3},{3,2},{4,5},{5,4},{6,7},{7,6},{8,9},{9,8},{10,11... | collective-permute-start | bytes 159752 | tf_op jit(solution)/shard_map/ppermute | solution.py:29
  15.1 2.7 %collective-permute-start.9 = (bf16[2,512,512]{2,1,0:T(8,128)(2,1)S(1)}, bf16[2,512,512]{2,1,0:T(8,128)(2,1)S(1)}, u32[]{:S(2)}, u32[]{:S(2)}) collective-permute-start(bf16[2,512,512]{2,1,0:T(8,128)(2,1)S(1)} %stack.1.refs_4_), channel_id=1, source_target_pairs={{0,16},{16,0},{1,17},{17,1},{2,18},{18,2},{3,19},{19,3},{4,20},{20... | collective-permute-start | bytes 3145736 | tf_op jit(solution)/shard_map/ppermute | solution.py:29
  18.3 6.1 %collective-permute-start.10 = (bf16[2,64,256]{2,1,0:T(8,128)(2,1)S(1)}, bf16[2,64,256]{2,1,0:T(8,128)(2,1)S(1)}, u32[]{:S(2)}, u32[]{:S(2)}) collective-permute-start(bf16[2,64,256]{2,1,0:T(8,128)(2,1)S(1)} %get-tuple-element.37), channel_id=1, source_target_pairs={{0,10},{1,11},{2,8},{3,9},{4,14},{5,15},{6,12},{7,13},{8,2},{9,3},... | collective-permute-start | bytes 196616 | tf_op jit(solution)/shard_map/ppermute | solution.py:29
  21.9 7.5 %collective-permute-start.11 = (bf16[2,64,256]{2,1,0:T(8,128)(2,1)S(1)}, bf16[2,64,256]{2,1,0:T(8,128)(2,1)S(1)}, u32[]{:S(2)}, u32[]{:S(2)}) collective-permute-start(bf16[2,64,256]{2,1,0:T(8,128)(2,1)S(1)} %get-tuple-element.38), channel_id=1, source_target_pairs={{0,13},{1,12},{2,15},{3,14},{4,9},{5,8},{6,11},{7,10},{8,5},{9,4},... | collective-permute-start | bytes 196616 | tf_op jit(solution)/shard_map/ppermute | solution.py:29
  23.5 6.4 %collective-permute-start.12 = (bf16[2,64,256]{2,1,0:T(8,128)(2,1)S(1)}, bf16[2,64,256]{2,1,0:T(8,128)(2,1)S(1)}, u32[]{:S(2)}, u32[]{:S(2)}) collective-permute-start(bf16[2,64,256]{2,1,0:T(8,128)(2,1)S(1)} %get-tuple-element.39), channel_id=1, source_target_pairs={{0,7},{1,6},{2,5},{3,4},{4,3},{5,2},{6,1},{7,0},{8,15},{9,14},{10,... | collective-permute-start | bytes 196616 | tf_op jit(solution)/shard_map/ppermute | solution.py:29
